TPU v7x, 128 devices: a whole 4x4x4 slice. The times are simulated.
128 devices in a mesh: gx: 16 (over y, x), gy: 8 (over z, core).
Axes of the slice: x: 4, y: 4, z: 4, core: 2. Of those that a mesh axis runs over, the one named last changes fastest.
Arguments:
- right_side: float32 [256, 128, 512], P('gx', 'gy'), may hold values from -6 to 6
- point_counts: int32 [32, 16, 64], P('gx', 'gy'), may hold values from 0 to 64
Outputs:
- solution_field: float32 [256, 128, 512], P('gx', 'gy')
- residual: float32 [256, 128, 512], P('gx', 'gy')
All inputs are finite; a program needn't handle non-finite values.
Results may differ from a plain program's by a relative error of at most 0.0003.
Values sent between devices are 32-bit elements; how exact they have to be, the bound alone decides.
No kernel may reach another device: no remote copies, remote signals or barrier semaphores. Data moves between devices by JAX's collectives and lax.ppermute only.
A program may use at most 512 MiB of HBM per device.

v0:
```python
import jax
import jax.numpy as jnp
from jax import lax
from jax.experimental import pallas as pl
from jax.experimental.pallas import tpu as pltpu
from jax.sharding import PartitionSpec as P

CENTER = 8.0 / 3.0
OMEGA = 2.0 / 3.0
SCREEN = 0.05
THIRD = 1.0 - OMEGA
F32 = jnp.float32
HIGH = lax.Precision.HIGHEST
CHUNK = 4


def iota(shape, dim):
    return lax.broadcasted_iota(jnp.int32, shape, dim)


def pairing(rows, columns, factor, value):
    r, c = iota((rows, columns), 0), iota((rows, columns), 1)
    hit = (r // factor == c) if rows > columns else (c // factor == r)
    return jnp.where(hit, value, 0.0).astype(F32)


def stencil_rows(load, rows, blocks):
    v, t = {}, {}
    for x in range(rows[0] - 1, rows[-1] + 2):
        v[x] = load(x, 0)
        t[x] = [a + b for a, b in zip(load(x, -1), load(x, 1))]
    lane = iota(v[rows[0]][0].shape, 1)
    first, last = lane == 0, lane == 127
    zero = jnp.zeros(lane.shape, F32)
    out = {}
    for x in rows:
        m = [t[x - 1][b] + t[x + 1][b] for b in range(blocks)]
        w = [0.5 * m[b] + (t[x][b] + (v[x - 1][b] + v[x + 1][b])) for b in range(blocks)]
        up = [pltpu.roll(w[b], 1, 1) for b in range(blocks)]
        down = [pltpu.roll(w[b], 127, 1) for b in range(blocks)]
        total = []
        for b in range(blocks):
            below = jnp.where(first, up[b - 1] if b else zero, up[b])
            above = jnp.where(last, down[b + 1] if b < blocks - 1 else zero, down[b])
            total.append((below + above) + m[b])
        out[x] = total
    return v, out


def sweep(source, target, coupling, drive, base, chunks, tiles, blocks, log_brick, origin):
    def body(c, carry):
        x0 = base + c * CHUNK
        for tile in tiles:
            def load(x, shift):
                return [
                    source[x0 + x, b, pl.ds(8 * tile + shift, 8), :] for b in range(blocks)
                ]

            v, out = stencil_rows(load, range(CHUNK), blocks)
            for x in range(CHUNK):
                at = lax.shift_right_logical(x0 + x - origin, log_brick)
                for b in range(blocks):
                    new = (
                        THIRD * v[x][b]
                        + coupling[at, tile - 1, b] * out[x][b]
                        + drive[x0 + x, b, pl.ds(8 * tile, 8), :]
                    )
                    target[x0 + x, b, pl.ds(8 * tile, 8), :] = new
        return carry

    lax.fori_loop(0, chunks, body, 0)


def restrict_kernel(side_ref, counts_ref, out_ref, tmp):
    for x in range(8):
        tmp[16 * x : 16 * x + 16, :] = side_ref[2 * x] + side_ref[2 * x + 1]
    halves = pairing(512, 256, 2, 0.5)
    rows = jnp.dot(pairing(64, 128, 2, 1.0), tmp[...], precision=HIGH, preferred_element_type=F32)
    coarse = jnp.dot(rows, halves, precision=HIGH, preferred_element_type=F32)
    for x in range(8):
        out_ref[x] = coarse[8 * x : 8 * x + 8, :]
    out_ref[8] = jnp.zeros((8, 256), F32)
    out_ref[8, 0:4, 0:64] = counts_ref[...].reshape(4, 64).astype(F32)


def in_domain(index, low, count):
    place = low + index - 1
    return jnp.where((place >= 0) & (place < count), 1.0, 0.0).astype(F32)


def coarse_kernel(mid_ref, low_ref, high_ref, c_ref, top_ref, bottom_ref, inv_ref, center_ref,
                  even, odd, drive, coupling):
    gx, gy = lax.axis_index("gx"), lax.axis_index("gy")
    n_gx, n_gy = lax.axis_size("gx"), lax.axis_size("gy")
    strips = (low_ref, mid_ref, high_ref)
    counts = jnp.concatenate([strips[j][9 * i + 8][:, 0:64] for i in range(3) for j in range(3)], axis=0)
    spread = jnp.dot(counts, pairing(64, 256, 4, 1.0), precision=HIGH, preferred_element_type=F32)
    weight = OMEGA / (CENTER + (SCREEN * 4.0) * spread)
    sub = iota((8, 128), 0)
    zero = jnp.zeros((8, 128), F32)
    for x in range(26):
        for b in range(2):
            for field in (even, odd):
                field[x, b, 0:8, :] = zero
                field[x, b, 32:40, :] = zero
                if x in (0, 25):
                    for tile in (1, 2, 3):
                        field[x, b, 8 * tile : 8 * tile + 8, :] = zero
    for i in range(3):
        for j in range(3):
            inside = in_domain(i, gx, n_gx) * in_domain(j, gy, n_gy)
            group = weight[8 * (3 * i + j) : 8 * (3 * i + j) + 8, :] * inside
            for k in range(2):
                for b in range(2):
                    lanes = slice(128 * b, 128 * b + 128)
                    tile = jnp.where(
                        sub < 4,
                        jnp.broadcast_to(group[2 * k : 2 * k + 1, lanes], (8, 128)),
                        jnp.broadcast_to(group[2 * k + 1 : 2 * k + 2, lanes], (8, 128)),
                    )
                    coupling[2 * i + k, j, b] = tile * (1.0 / 6.0)
                    for x in range(4):
                        at = 8 * i + 4 * k + x
                        value = tile * strips[j][9 * i + 4 * k + x, :, lanes]
                        drive[at + 1, b, pl.ds(8 * j + 8, 8), :] = value
                        even[at + 1, b, pl.ds(8 * j + 8, 8), :] = value

    def step(k, carry):
        sweep(even, odd, coupling, drive, 3 + 2 * k, 5 - k, (1, 2, 3), 2, 2, 1)
        sweep(odd, even, coupling, drive, 3 + 2 * k, 5 - k, (1, 2, 3), 2, 2, 1)
        return carry

    lax.fori_loop(0, 3, step, 0)
    sweep(even, odd, coupling, drive, 9, 2, (2,), 2, 2, 1)
    for x in range(8):
        row = jnp.concatenate([odd[9 + x, b, 16:24, :] for b in range(2)], axis=1)
        c_ref[x] = row
        if x < 5:
            bottom_ref[x] = row
        if x >= 3:
            top_ref[x - 3] = row

    wide = jnp.dot(counts, pairing(64, 512, 8, 1.0), precision=HIGH, preferred_element_type=F32)
    center = CENTER + SCREEN * wide
    inverse = OMEGA / center
    for xb in range(4):
        i, k = ((xb + 1) // 2, (xb + 1) % 2)
        for yb in range(4):
            j, l = ((yb + 1) // 2, (yb + 1) % 2)
            at = 8 * (3 * i + j) + 2 * k + l
            inside = in_domain(i, gx, n_gx) * in_domain(j, gy, n_gy)
            inv_ref[xb, yb : yb + 1, :] = inverse[at : at + 1, :] * inside
            center_ref[xb, yb : yb + 1, :] = center[at : at + 1, :]


def fine_kernel(side_ref, side_low, side_high, c_ref, c_low, c_high, inv_ref, center_ref, solution_ref, residual_ref,
                even, odd, drive, coupling):
    gx, gy = lax.axis_index("gx"), lax.axis_index("gy")
    n_gx, n_gy = lax.axis_size("gx"), lax.axis_size("gy")
    zero = jnp.zeros((8, 128), F32)
    for x in range(36):
        for b in range(4):
            odd[x, b, 0:8, :] = zero
            odd[x, b, 40:48, :] = zero
            if x in (0, 1, 34, 35):
                for tile in (1, 2, 3, 4):
                    odd[x, b, 8 * tile : 8 * tile + 8, :] = zero
    doubling = pairing(256, 512, 2, 1.0)
    for j, ref in enumerate((c_low, c_ref, c_high)):
        here = in_domain(j, gy, n_gy)
        rows = []
        for x in range(18):
            i = 0 if x < 5 else (1 if x < 13 else 2)
            rows.append(ref[x] * (here * in_domain(i, gx, n_gx)))
        grown = jnp.dot(jnp.concatenate(rows, axis=0), doubling, precision=HIGH, preferred_element_type=F32)
        for x in range(18):
            for b in range(4):
                value = grown[8 * x : 8 * x + 8, 128 * b : 128 * b + 128]
                for dx in range(2):
                    for dy in range(2):
                        even[2 * x + dx, b, pl.ds(16 * j + dy, 8, stride=2), :] = value
    for xb in range(4):
        for yb in range(4):
            for b in range(4):
                tile = jnp.broadcast_to(inv_ref[xb, yb : yb + 1, 128 * b : 128 * b + 128], (8, 128))
                coupling[xb, yb, b] = tile * (1.0 / 6.0)
                source = (side_low, side_ref, side_ref, side_high)[yb]
                row = (0, 0, 8, 0)[yb]

                def fill(x, carry, tile=tile, source=source, row=row, b=b, xb=xb, yb=yb):
                    at = 8 * xb + x
                    drive[at + 2, b, pl.ds(8 * yb + 8, 8), :] = (
                        tile * source[at, row : row + 8, 128 * b : 128 * b + 128]
                    )
                    return carry

                lax.fori_loop(0, 8, fill, 0, unroll=True)

    def step(k, carry):
        sweep(even, odd, coupling, drive, 2 + 2 * k, 8 - k, (1, 2, 3, 4), 4, 3, 2)
        sweep(odd, even, coupling, drive, 2 + 2 * k, 8 - k, (1, 2, 3, 4), 4, 3, 2)
        return carry

    lax.fori_loop(0, 4, step, 0)

    def finish(c, carry):
        x0 = c * CHUNK
        for tile in (2, 3):
            def load(x, shift):
                return [even[x0 + 10 + x, b, pl.ds(8 * tile + shift, 8), :] for b in range(4)]

            v, out = stencil_rows(load, range(CHUNK), 4)
            for x in range(CHUNK):
                brick = 1 + lax.shift_right_logical(x0 + x, 3)
                for b in range(4):
                    lanes = slice(128 * b, 128 * b + 128)
                    rows = slice(8 * tile - 16, 8 * tile - 8)
                    center = center_ref[brick, tile - 1 : tile, lanes]
                    solution_ref[x0 + x, rows, lanes] = v[x][b]
                    residual_ref[x0 + x, rows, lanes] = (
                        side_ref[x0 + x + 8, rows, lanes] - center * v[x][b] + (1.0 / 6.0) * out[x][b]
                    )
        return carry

    lax.fori_loop(0, 16 // CHUNK, finish, 0)


def shape(*dims):
    return jax.ShapeDtypeStruct(dims, F32)


def shards(right_side, point_counts):
    params = pltpu.CompilerParams(vmem_limit_bytes=24 * 1024 * 1024)
    n_gx, n_gy = lax.axis_size("gx"), lax.axis_size("gy")

    def move(value, axis, step):
        count = n_gx if axis == "gx" else n_gy
        return lax.ppermute(value, axis, [(i, (i + step) % count) for i in range(count)])

    packed = pl.pallas_call(
        restrict_kernel,
        out_shape=shape(9, 8, 256),
        scratch_shapes=[pltpu.VMEM((128, 512), F32)],
        compiler_params=params,
        name="restrict",
    )(right_side, point_counts)
    packed = jnp.concatenate([move(packed, "gx", 1), packed, move(packed, "gx", -1)], axis=0)
    coarse, top, bottom, inverse, center = pl.pallas_call(
        coarse_kernel,
        out_shape=[shape(8, 8, 256), shape(5, 8, 256), shape(5, 8, 256), shape(4, 4, 512), shape(4, 4, 512)],
        scratch_shapes=[
            pltpu.VMEM((26, 2, 40, 128), F32),
            pltpu.VMEM((26, 2, 40, 128), F32),
            pltpu.VMEM((26, 2, 40, 128), F32),
            pltpu.VMEM((6, 3, 2, 8, 128), F32),
        ],
        compiler_params=params,
        name="coarse",
    )(packed, move(packed, "gy", 1), move(packed, "gy", -1))
    coarse = jnp.concatenate([move(top, "gx", 1), coarse, move(bottom, "gx", -1)], axis=0)
    side = jnp.concatenate(
        [move(right_side[8:16], "gx", 1), right_side, move(right_side[0:8], "gx", -1)], axis=0
    )
    solution_field, residual = pl.pallas_call(
        fine_kernel,
        out_shape=[shape(16, 16, 512), shape(16, 16, 512)],
        scratch_shapes=[
            pltpu.VMEM((36, 4, 48, 128), F32),
            pltpu.VMEM((36, 4, 48, 128), F32),
            pltpu.VMEM((36, 4, 48, 128), F32),
            pltpu.VMEM((4, 4, 4, 8, 128), F32),
        ],
        compiler_params=params,
        name="fine",
    )(
        side,
        move(side[:, 8:16], "gy", 1),
        move(side[:, 0:8], "gy", -1),
        coarse,
        move(coarse, "gy", 1),
        move(coarse, "gy", -1),
        inverse,
        center,
    )
    return solution_field, residual


def solution(mesh):
    specs = (P("gx", "gy", None), P("gx", "gy", None))
    return jax.shard_map(shards, mesh=mesh, in_specs=specs, out_specs=specs, check_vma=False)
```

profile of v0, /device:TPU:0, one launch (start us, length us, event | category | flops | bytes accessed | tf_op | source)
XLA Modules:
  0.0 57.6 jit_solution(856001642726360884)
XLA Ops:
  0.6 1.1 %fusion.1 = (f32[8,16,512]{2,1,0:T(8,128)S(1)}, f32[8,16,512]{2,1,0:T(8,128)S(1)}) fusion(f32[16,16,512]{2,1,0:T(8,128)} %side_ref.1), kind=kLoop, calls=%fused_computation.8 | loop fusion | bytes 1048576 | tf_op jit(solution)/shard_map/slice | solution.py:262
  1.8 1.6 %collective-permute-start = (f32[8,16,512]{2,1,0:T(8,128)S(1)}, f32[8,16,512]{2,1,0:T(8,128)S(1)}, u32[]{:S(2)}, u32[]{:S(2)}) collective-permute-start(f32[8,16,512]{2,1,0:T(8,128)S(1)} %get-tuple-element.15), channel_id=1, source_target_pairs={{0,8},{8,16},{16,24},{24,32},{32,40},{40,48},{48,56},{56,64},{64,7... | collective-permute-start | bytes 786440 | tf_op jit(solution)/shard_map/ppermute | solution.py:238
  3.4 0.6 %restrict.1 = f32[9,8,256]{2,1,0:T(8,128)S(1)} custom-call(f32[16,16,512]{2,1,0:T(8,128)S(1)} %copy-done, s32[2,2,64]{2,1,0:T(2,128)S(1)} %copy-done.1), custom_call_target="tpu_custom_call" | custom-call | tf_op jit(solution)/shard_map/restrict/pallas_call | solution.py:240
  4.1 3.8 %collective-permute-start.5 = (f32[9,8,256]{2,1,0:T(8,128)S(1)}, f32[9,8,256]{2,1,0:T(8,128)S(1)}, u32[]{:S(2)}, u32[]{:S(2)}) collective-permute-start(f32[9,8,256]{2,1,0:T(8,128)S(1)} %restrict.1), channel_id=1, source_target_pairs={{0,120},{8,0},{16,8},{24,16},{32,24},{40,32},{48,40},{56,48},{64,5... | collective-permute-start | bytes 221192 | tf_op jit(solution)/shard_map/ppermute | solution.py:238
  7.9 0.0 collective-permute-start.4
  7.9 5.3 %collective-permute-start.1 = (f32[8,16,512]{2,1,0:T(8,128)S(1)}, f32[8,16,512]{2,1,0:T(8,128)S(1)}, u32[]{:S(2)}, u32[]{:S(2)}) collective-permute-start(f32[8,16,512]{2,1,0:T(8,128)S(1)} %get-tuple-element.14), channel_id=1, source_target_pairs={{0,120},{8,0},{16,8},{24,16},{32,24},{40,32},{48,40},{56,48},{64,5... | collective-permute-start | bytes 786440 | tf_op jit(solution)/shard_map/ppermute | solution.py:238
  13.3 0.0 collective-permute-done.5
  13.3 2.3 %collective-permute-done.4 = f32[9,8,256]{2,1,0:T(8,128)S(1)} collective-permute-done((f32[9,8,256]{2,1,0:T(8,128)S(1)}, f32[9,8,256]{2,1,0:T(8,128)S(1)}, u32[]{:S(2)}, u32[]{:S(2)}) %collective-permute-start.4) | collective-permute-done | bytes 73760 | tf_op jit(solution)/shard_map/ppermute | solution.py:238
  15.6 2.1 %collective-permute-start.7 = (f32[27,8,256]{2,1,0:T(8,128)S(1)}, f32[27,8,256]{2,1,0:T(8,128)S(1)}, u32[]{:S(2)}, u32[]{:S(2)}) collective-permute-start(f32[27,8,256]{2,1,0:T(8,128)S(1)} %pad_maximum_fusion.mid_ref), channel_id=1, source_target_pairs={{0,7},{1,0},{2,1},{3,2},{4,3},{5,4},{6,5},{7,6},{8,15},{9,8},{10,9... | collective-permute-start | bytes 663560 | tf_op jit(solution)/shard_map/ppermute | solution.py:238
  17.8 0.4 collective-permute-done.1
  18.3 2.9 %collective-permute-done.7.high_ref = f32[27,8,256]{2,1,0:T(8,128)S(1)} collective-permute-done((f32[27,8,256]{2,1,0:T(8,128)S(1)}, f32[27,8,256]{2,1,0:T(8,128)S(1)}, u32[]{:S(2)}, u32[]{:S(2)}) %collective-permute-start.7) | collective-permute-done | bytes 221216 | tf_op jit(solution)/shard_map/ppermute | solution.py:238
  21.2 3.1 %collective-permute-done.6.low_ref = f32[27,8,256]{2,1,0:T(8,128)S(1)} collective-permute-done((f32[27,8,256]{2,1,0:T(8,128)S(1)}, f32[27,8,256]{2,1,0:T(8,128)S(1)}, u32[]{:S(2)}, u32[]{:S(2)}) %collective-permute-start.6) | collective-permute-done | bytes 221216 | tf_op jit(solution)/shard_map/ppermute | solution.py:238
  24.3 4.0 %coarse.1 = (f32[8,8,256]{2,1,0:T(8,128)S(1)}, f32[5,8,256]{2,1,0:T(8,128)S(1)}, f32[5,8,256]{2,1,0:T(8,128)S(1)}, f32[4,4,512]{2,1,0:T(4,128)S(1)}, f32[4,4,512]{2,1,0:T(4,128)S(1)}) custom-call(f32[27,8,256]{2,1,0:T(8,128)S(1)} %pad_maximum_fusion.mid_ref, f32[27,8,256]{2,1,0:T(8,128)S(1)} %collective-permute-done.6.low_ref, ...), custom_call_target="tpu_custom_call" | custom-call | tf_op jit(solution)/shard_map/coarse/pallas_call | solution.py:248
  28.3 0.1 collective-permute-start.8
  28.4 0.1 fusion
  28.4 0.0 collective-permute-start.3
  28.5 0.5 collective-permute-start.2
  29.0 5.3 %collective-permute-start.9 = (f32[5,8,256]{2,1,0:T(8,128)S(1)}, f32[5,8,256]{2,1,0:T(8,128)S(1)}, u32[]{:S(2)}, u32[]{:S(2)}) collective-permute-start(f32[5,8,256]{2,1,0:T(8,128)S(1)} %get-tuple-element.9), channel_id=1, source_target_pairs={{0,120},{8,0},{16,8},{24,16},{32,24},{40,32},{48,40},{56,48},{64,5... | collective-permute-start | bytes 122888 | tf_op jit(solution)/shard_map/ppermute | solution.py:238
  34.3 1.4 %collective-permute-done.8 = f32[5,8,256]{2,1,0:T(8,128)S(1)} collective-permute-done((f32[5,8,256]{2,1,0:T(8,128)S(1)}, f32[5,8,256]{2,1,0:T(8,128)S(1)}, u32[]{:S(2)}, u32[]{:S(2)}) %collective-permute-start.8) | collective-permute-done | bytes 40992 | tf_op jit(solution)/shard_map/ppermute | solution.py:238
  35.7 0.3 collective-permute-done.9
  36.0 1.6 %collective-permute-start.11 = (f32[18,8,256]{2,1,0:T(8,128)S(1)}, f32[18,8,256]{2,1,0:T(8,128)S(1)}, u32[]{:S(2)}, u32[]{:S(2)}) collective-permute-start(f32[18,8,256]{2,1,0:T(8,128)S(1)} %constant_dynamic-update-slice_fusion.3.c_ref), channel_id=1, source_target_pairs={{0,7},{1,0},{2,1},{3,2},{4,3},{5,4},{6,5},{7,6},{8,15},{9,8},{10,9... | collective-permute-start | bytes 442376 | tf_op jit(solution)/shard_map/ppermute | solution.py:238
  37.6 2.7 %collective-permute-done.11.c_high = f32[18,8,256]{2,1,0:T(8,128)S(1)} collective-permute-done((f32[18,8,256]{2,1,0:T(8,128)S(1)}, f32[18,8,256]{2,1,0:T(8,128)S(1)}, u32[]{:S(2)}, u32[]{:S(2)}) %collective-permute-start.11) | collective-permute-done | bytes 147488 | tf_op jit(solution)/shard_map/ppermute | solution.py:238
  40.3 3.1 %collective-permute-done.10.c_low = f32[18,8,256]{2,1,0:T(8,128)S(1)} collective-permute-done((f32[18,8,256]{2,1,0:T(8,128)S(1)}, f32[18,8,256]{2,1,0:T(8,128)S(1)}, u32[]{:S(2)}, u32[]{:S(2)}) %collective-permute-start.10) | collective-permute-done | bytes 147488 | tf_op jit(solution)/shard_map/ppermute | solution.py:238
  43.4 14.2 %fine.1 = (f32[16,16,512]{2,1,0:T(8,128)}, f32[16,16,512]{2,1,0:T(8,128)}) custom-call(f32[32,16,512]{2,1,0:T(8,128)S(1)} %constant_dynamic-update-slice_fusion.side_ref, f32[32,8,512]{2,1,0:T(8,128)S(1)} %collective-permute-done.2.side_low, f32[32,8,512]{2,1,0:T(8,128)S(1)} %collective-permute-done.3.side_high, ...), custom_call_target="tpu_custom_call" | custom-call | tf_op jit(solution)/shard_map/fine/pallas_call | solution.py:264
  (16 shorter events, 0.1 us)
Async XLA Ops:
  0.6 2.8 %copy-start = (f32[16,16,512]{2,1,0:T(8,128)S(1)}, f32[16,16,512]{2,1,0:T(8,128)}, u32[]{:S(2)}) copy-start(f32[16,16,512]{2,1,0:T(8,128)} %side_ref.1) | copy-start | bytes 1572868
  0.6 2.8 %copy-start.1 = (s32[2,2,64]{2,1,0:T(2,128)S(1)}, s32[2,2,64]{2,1,0:T(2,128)}, u32[]{:S(2)}) copy-start(s32[2,2,64]{2,1,0:T(2,128)} %counts_ref.1) | copy-start | bytes 3076
  1.8 16.0 %collective-permute-start = (f32[8,16,512]{2,1,0:T(8,128)S(1)}, f32[8,16,512]{2,1,0:T(8,128)S(1)}, u32[]{:S(2)}, u32[]{:S(2)}) collective-permute-start(f32[8,16,512]{2,1,0:T(8,128)S(1)} %get-tuple-element.15), channel_id=1, source_target_pairs={{0,8},{8,16},{16,24},{24,32},{32,40},{40,48},{48,56},{56,64},{64,7... | collective-permute-start | bytes 786440 | tf_op jit(solution)/shard_map/ppermute | solution.py:238
  4.1 9.2 %collective-permute-start.5 = (f32[9,8,256]{2,1,0:T(8,128)S(1)}, f32[9,8,256]{2,1,0:T(8,128)S(1)}, u32[]{:S(2)}, u32[]{:S(2)}) collective-permute-start(f32[9,8,256]{2,1,0:T(8,128)S(1)} %restrict.1), channel_id=1, source_target_pairs={{0,120},{8,0},{16,8},{24,16},{32,24},{40,32},{48,40},{56,48},{64,5... | collective-permute-start | bytes 221192 | tf_op jit(solution)/shard_map/ppermute | solution.py:238
  7.9 7.7 %collective-permute-start.4 = (f32[9,8,256]{2,1,0:T(8,128)S(1)}, f32[9,8,256]{2,1,0:T(8,128)S(1)}, u32[]{:S(2)}, u32[]{:S(2)}) collective-permute-start(f32[9,8,256]{2,1,0:T(8,128)S(1)} %restrict.1), channel_id=1, source_target_pairs={{0,8},{8,16},{16,24},{24,32},{32,40},{40,48},{48,56},{56,64},{64,7... | collective-permute-start | bytes 221192 | tf_op jit(solution)/shard_map/ppermute | solution.py:238
  7.9 10.3 %collective-permute-start.1 = (f32[8,16,512]{2,1,0:T(8,128)S(1)}, f32[8,16,512]{2,1,0:T(8,128)S(1)}, u32[]{:S(2)}, u32[]{:S(2)}) collective-permute-start(f32[8,16,512]{2,1,0:T(8,128)S(1)} %get-tuple-element.14), channel_id=1, source_target_pairs={{0,120},{8,0},{16,8},{24,16},{32,24},{40,32},{48,40},{56,48},{64,5... | collective-permute-start | bytes 786440 | tf_op jit(solution)/shard_map/ppermute | solution.py:238
  15.6 5.6 %collective-permute-start.7 = (f32[27,8,256]{2,1,0:T(8,128)S(1)}, f32[27,8,256]{2,1,0:T(8,128)S(1)}, u32[]{:S(2)}, u32[]{:S(2)}) collective-permute-start(f32[27,8,256]{2,1,0:T(8,128)S(1)} %pad_maximum_fusion.mid_ref), channel_id=1, source_target_pairs={{0,7},{1,0},{2,1},{3,2},{4,3},{5,4},{6,5},{7,6},{8,15},{9,8},{10,9... | collective-permute-start | bytes 663560 | tf_op jit(solution)/shard_map/ppermute | solution.py:238
  17.7 6.6 %collective-permute-start.6 = (f32[27,8,256]{2,1,0:T(8,128)S(1)}, f32[27,8,256]{2,1,0:T(8,128)S(1)}, u32[]{:S(2)}, u32[]{:S(2)}) collective-permute-start(f32[27,8,256]{2,1,0:T(8,128)S(1)} %pad_maximum_fusion.mid_ref), channel_id=1, source_target_pairs={{0,1},{1,2},{2,3},{3,4},{4,5},{5,6},{6,7},{7,0},{8,9},{9,10},{10,1... | collective-permute-start | bytes 663560 | tf_op jit(solution)/shard_map/ppermute | solution.py:238
  28.3 7.4 %collective-permute-start.8 = (f32[5,8,256]{2,1,0:T(8,128)S(1)}, f32[5,8,256]{2,1,0:T(8,128)S(1)}, u32[]{:S(2)}, u32[]{:S(2)}) collective-permute-start(f32[5,8,256]{2,1,0:T(8,128)S(1)} %get-tuple-element.7), channel_id=1, source_target_pairs={{0,8},{8,16},{16,24},{24,32},{32,40},{40,48},{48,56},{56,64},{64,7... | collective-permute-start | bytes 122888 | tf_op jit(solution)/shard_map/ppermute | solution.py:238
  28.4 14.9 %collective-permute-start.3 = (f32[32,8,512]{2,1,0:T(8,128)S(1)}, f32[32,8,512]{2,1,0:T(8,128)S(1)}, u32[]{:S(2)}, u32[]{:S(2)}) collective-permute-start(f32[32,8,512]{2,1,0:T(8,128)S(1)} %get-tuple-element.12), channel_id=1, source_target_pairs={{0,7},{1,0},{2,1},{3,2},{4,3},{5,4},{6,5},{7,6},{8,15},{9,8},{10,9... | collective-permute-start | bytes 1572872 | tf_op jit(solution)/shard_map/ppermute | solution.py:238
  28.5 14.9 %collective-permute-start.2 = (f32[32,8,512]{2,1,0:T(8,128)S(1)}, f32[32,8,512]{2,1,0:T(8,128)S(1)}, u32[]{:S(2)}, u32[]{:S(2)}) collective-permute-start(f32[32,8,512]{2,1,0:T(8,128)S(1)} %get-tuple-element.13), channel_id=1, source_target_pairs={{0,1},{1,2},{2,3},{3,4},{4,5},{5,6},{6,7},{7,0},{8,9},{9,10},{10,1... | collective-permute-start | bytes 1572872 | tf_op jit(solution)/shard_map/ppermute | solution.py:238
  29.0 7.0 %collective-permute-start.9 = (f32[5,8,256]{2,1,0:T(8,128)S(1)}, f32[5,8,256]{2,1,0:T(8,128)S(1)}, u32[]{:S(2)}, u32[]{:S(2)}) collective-permute-start(f32[5,8,256]{2,1,0:T(8,128)S(1)} %get-tuple-element.9), channel_id=1, source_target_pairs={{0,120},{8,0},{16,8},{24,16},{32,24},{40,32},{48,40},{56,48},{64,5... | collective-permute-start | bytes 122888 | tf_op jit(solution)/shard_map/ppermute | solution.py:238
  36.0 4.3 %collective-permute-start.11 = (f32[18,8,256]{2,1,0:T(8,128)S(1)}, f32[18,8,256]{2,1,0:T(8,128)S(1)}, u32[]{:S(2)}, u32[]{:S(2)}) collective-permute-start(f32[18,8,256]{2,1,0:T(8,128)S(1)} %constant_dynamic-update-slice_fusion.3.c_ref), channel_id=1, source_target_pairs={{0,7},{1,0},{2,1},{3,2},{4,3},{5,4},{6,5},{7,6},{8,15},{9,8},{10,9... | collective-permute-start | bytes 442376 | tf_op jit(solution)/shard_map/ppermute | solution.py:238
  37.6 5.8 %collective-permute-start.10 = (f32[18,8,256]{2,1,0:T(8,128)S(1)}, f32[18,8,256]{2,1,0:T(8,128)S(1)}, u32[]{:S(2)}, u32[]{:S(2)}) collective-permute-start(f32[18,8,256]{2,1,0:T(8,128)S(1)} %constant_dynamic-update-slice_fusion.3.c_ref), channel_id=1, source_target_pairs={{0,1},{1,2},{2,3},{3,4},{4,5},{5,6},{6,7},{7,0},{8,9},{9,10},{10,1... | collective-permute-start | bytes 442376 | tf_op jit(solution)/shard_map/ppermute | solution.py:238
where the time goes:
time: 57.7 us; the launch traced here: 57.6 us
  starting transfers between devices  20.5 us (36%)
  Pallas kernels  18.8 us (33%)
  waiting for transfers between devices  16.2 us (28%)
  local copies, waits for them, and re-layouts  1.3 us (2%)
  between operations  0.73 us (1%)
    ppermute x12, starting transfers between devices, move(): lax.ppermute(value, axis, [(i, (i + step) % count) for i in range(count)])  20.5 us
    ppermute x12, waiting for transfers between devices, move(): lax.ppermute(value, axis, [(i, (i + step) % count) for i in range(count)])  16.2 us
    pallas_call x1, Pallas kernels, shards(): pl.pallas_call(fine_kernel, out_shape=[shape(16, 16, 512), shape(16, 16,...  14.2 us
    pallas_call x1, Pallas kernels, shards(): pl.pallas_call(coarse_kernel, out_shape=[shape(8, 8, 256), shape(5, 8, 25...  3.97 us
  transfers between devices with their start and end apart: 12, of which 8 were waited for; matrix products, arithmetic and copies ran while one was open for 0% of the time, Pallas kernels for 1%

commit v1 on v0

--- a/solution.py
+++ b/solution.py
@@ -11,7 +11,9 @@
 THIRD = 1.0 - OMEGA
 F32 = jnp.float32
 HIGH = lax.Precision.HIGHEST
-CHUNK = 4
+CHUNK = 8
+FINE_PARTS = 1
+COARSE_PARTS = 1
 
 
 def iota(shape, dim):
@@ -47,28 +49,31 @@
     return v, out
 
 
-def sweep(source, target, coupling, drive, base, chunks, tiles, blocks, log_brick, origin):
+def sweep(source, target, coupling, drive, base, rows, parts, tiles, blocks, log_brick, origin):
+    step = rows // parts
+
     def body(c, carry):
-        x0 = base + c * CHUNK
+        x0 = base + c * step
         for tile in tiles:
             def load(x, shift):
-                return [
-                    source[x0 + x, b, pl.ds(8 * tile + shift, 8), :] for b in range(blocks)
-                ]
-
-            v, out = stencil_rows(load, range(CHUNK), blocks)
-            for x in range(CHUNK):
-                at = lax.shift_right_logical(x0 + x - origin, log_brick)
+                return [source[x0 + x, b, pl.ds(8 * tile + shift, 8), :] for b in range(blocks)]
+
+            v, out = stencil_rows(load, range(step), blocks)
+            for x in range(step):
+                at = x0 + x - origin
+                at = at >> log_brick if parts == 1 else lax.shift_right_logical(at, log_brick)
                 for b in range(blocks):
-                    new = (
+                    target[x0 + x, b, pl.ds(8 * tile, 8), :] = (
                         THIRD * v[x][b]
                         + coupling[at, tile - 1, b] * out[x][b]
                         + drive[x0 + x, b, pl.ds(8 * tile, 8), :]
                     )
-                    target[x0 + x, b, pl.ds(8 * tile, 8), :] = new
         return carry
 
-    lax.fori_loop(0, chunks, body, 0)
+    if parts == 1:
+        body(0, 0)
+    else:
+        lax.fori_loop(0, parts, body, 0)
 
 
 def restrict_kernel(side_ref, counts_ref, out_ref, tmp):
@@ -125,13 +130,11 @@
                         drive[at + 1, b, pl.ds(8 * j + 8, 8), :] = value
                         even[at + 1, b, pl.ds(8 * j + 8, 8), :] = value
 
-    def step(k, carry):
-        sweep(even, odd, coupling, drive, 3 + 2 * k, 5 - k, (1, 2, 3), 2, 2, 1)
-        sweep(odd, even, coupling, drive, 3 + 2 * k, 5 - k, (1, 2, 3), 2, 2, 1)
-        return carry
-
-    lax.fori_loop(0, 3, step, 0)
-    sweep(even, odd, coupling, drive, 9, 2, (2,), 2, 2, 1)
+    for k in range(7):
+        source, target = (even, odd) if k % 2 == 0 else (odd, even)
+        halo = 6 - k
+        tiles = (1, 2, 3) if halo else (2,)
+        sweep(source, target, coupling, drive, 9 - halo, 8 + 2 * halo, COARSE_PARTS, tiles, 2, 2, 1)
     for x in range(8):
         row = jnp.concatenate([odd[9 + x, b, 16:24, :] for b in range(2)], axis=1)
         c_ref[x] = row
@@ -196,12 +199,10 @@
 
                 lax.fori_loop(0, 8, fill, 0, unroll=True)
 
-    def step(k, carry):
-        sweep(even, odd, coupling, drive, 2 + 2 * k, 8 - k, (1, 2, 3, 4), 4, 3, 2)
-        sweep(odd, even, coupling, drive, 2 + 2 * k, 8 - k, (1, 2, 3, 4), 4, 3, 2)
-        return carry
-
-    lax.fori_loop(0, 4, step, 0)
+    for k in range(8):
+        source, target = (even, odd) if k % 2 == 0 else (odd, even)
+        halo = 8 - k
+        sweep(source, target, coupling, drive, 10 - halo, 16 + 2 * halo, FINE_PARTS, (1, 2, 3, 4), 4, 3, 2)
 
     def finish(c, carry):
         x0 = c * CHUNK

time: 57.7 us -> 50.6 us (0.88)
  Pallas kernels: 18.8 us -> 11.6 us
    pallas_call x1, Pallas kernels: 14.2 us -> 9.25 us  [shards(): pl.pallas_call(fine_kernel, out_shape=[shape(16, 16, 512), shape(16, 16,...]
    pallas_call x1, Pallas kernels: 3.97 us -> 1.7 us  [shards(): pl.pallas_call(coarse_kernel, out_shape=[shape(8, 8, 256), shape(5, 8, 25...]
where the time goes in v1:
time: 50.6 us; the launch traced here: 50.4 us
  starting transfers between devices  20.5 us (41%)
  waiting for transfers between devices  16.2 us (32%)
  Pallas kernels  11.6 us (23%)
  local copies, waits for them, and re-layouts  1.3 us (3%)
  between operations  0.73 us (1%)
    ppermute x12, starting transfers between devices, move(): lax.ppermute(value, axis, [(i, (i + step) % count) for i in range(count)])  20.5 us
    ppermute x12, waiting for transfers between devices, move(): lax.ppermute(value, axis, [(i, (i + step) % count) for i in range(count)])  16.2 us
    pallas_call x1, Pallas kernels, shards(): pl.pallas_call(fine_kernel, out_shape=[shape(16, 16, 512), shape(16, 16,...  9.25 us
    pallas_call x1, Pallas kernels, shards(): pl.pallas_call(coarse_kernel, out_shape=[shape(8, 8, 256), shape(5, 8, 25...  1.7 us
    slice x1, local copies, waits for them, and re-layouts, shards(): right_side[0:8]  1.12 us
  transfers between devices with their start and end apart: 12, of which 8 were waited for; matrix products, arithmetic and copies ran while one was open for 0% of the time, Pallas kernels for 1%

profile of v1, /device:TPU:0, one launch (start us, length us, event | category | flops | bytes accessed | tf_op | source)
XLA Modules:
  0.0 50.4 jit_solution(4840449567049469162)
XLA Ops:
  0.6 1.1 %fusion.1 = (f32[8,16,512]{2,1,0:T(8,128)S(1)}, f32[8,16,512]{2,1,0:T(8,128)S(1)}) fusion(f32[16,16,512]{2,1,0:T(8,128)} %side_ref.1), kind=kLoop, calls=%fused_computation.8 | loop fusion | bytes 1048576 | tf_op jit(solution)/shard_map/slice | solution.py:263
  1.8 1.6 %collective-permute-start = (f32[8,16,512]{2,1,0:T(8,128)S(1)}, f32[8,16,512]{2,1,0:T(8,128)S(1)}, u32[]{:S(2)}, u32[]{:S(2)}) collective-permute-start(f32[8,16,512]{2,1,0:T(8,128)S(1)} %get-tuple-element.15), channel_id=1, source_target_pairs={{0,8},{8,16},{16,24},{24,32},{32,40},{40,48},{48,56},{56,64},{64,7... | collective-permute-start | bytes 786440 | tf_op jit(solution)/shard_map/ppermute | solution.py:239
  3.4 0.6 %restrict.1 = f32[9,8,256]{2,1,0:T(8,128)S(1)} custom-call(f32[16,16,512]{2,1,0:T(8,128)S(1)} %copy-done, s32[2,2,64]{2,1,0:T(2,128)S(1)} %copy-done.1), custom_call_target="tpu_custom_call" | custom-call | tf_op jit(solution)/shard_map/restrict/pallas_call | solution.py:241
  4.1 3.8 %collective-permute-start.5 = (f32[9,8,256]{2,1,0:T(8,128)S(1)}, f32[9,8,256]{2,1,0:T(8,128)S(1)}, u32[]{:S(2)}, u32[]{:S(2)}) collective-permute-start(f32[9,8,256]{2,1,0:T(8,128)S(1)} %restrict.1), channel_id=1, source_target_pairs={{0,120},{8,0},{16,8},{24,16},{32,24},{40,32},{48,40},{56,48},{64,5... | collective-permute-start | bytes 221192 | tf_op jit(solution)/shard_map/ppermute | solution.py:239
  7.9 5.3 %collective-permute-start.1 = (f32[8,16,512]{2,1,0:T(8,128)S(1)}, f32[8,16,512]{2,1,0:T(8,128)S(1)}, u32[]{:S(2)}, u32[]{:S(2)}) collective-permute-start(f32[8,16,512]{2,1,0:T(8,128)S(1)} %get-tuple-element.14), channel_id=1, source_target_pairs={{0,120},{8,0},{16,8},{24,16},{32,24},{40,32},{48,40},{56,48},{64,5... | collective-permute-start | bytes 786440 | tf_op jit(solution)/shard_map/ppermute | solution.py:239
  13.3 2.3 %collective-permute-done.4 = f32[9,8,256]{2,1,0:T(8,128)S(1)} collective-permute-done((f32[9,8,256]{2,1,0:T(8,128)S(1)}, f32[9,8,256]{2,1,0:T(8,128)S(1)}, u32[]{:S(2)}, u32[]{:S(2)}) %collective-permute-start.4) | collective-permute-done | bytes 73760 | tf_op jit(solution)/shard_map/ppermute | solution.py:239
  15.6 2.1 %collective-permute-start.7 = (f32[27,8,256]{2,1,0:T(8,128)S(1)}, f32[27,8,256]{2,1,0:T(8,128)S(1)}, u32[]{:S(2)}, u32[]{:S(2)}) collective-permute-start(f32[27,8,256]{2,1,0:T(8,128)S(1)} %pad_maximum_fusion.mid_ref), channel_id=1, source_target_pairs={{0,7},{1,0},{2,1},{3,2},{4,3},{5,4},{6,5},{7,6},{8,15},{9,8},{10,9... | collective-permute-start | bytes 663560 | tf_op jit(solution)/shard_map/ppermute | solution.py:239
  17.8 0.4 collective-permute-done.1
  18.3 2.9 %collective-permute-done.7.high_ref = f32[27,8,256]{2,1,0:T(8,128)S(1)} collective-permute-done((f32[27,8,256]{2,1,0:T(8,128)S(1)}, f32[27,8,256]{2,1,0:T(8,128)S(1)}, u32[]{:S(2)}, u32[]{:S(2)}) %collective-permute-start.7) | collective-permute-done | bytes 221216 | tf_op jit(solution)/shard_map/ppermute | solution.py:239
  21.2 3.1 %collective-permute-done.6.low_ref = f32[27,8,256]{2,1,0:T(8,128)S(1)} collective-permute-done((f32[27,8,256]{2,1,0:T(8,128)S(1)}, f32[27,8,256]{2,1,0:T(8,128)S(1)}, u32[]{:S(2)}, u32[]{:S(2)}) %collective-permute-start.6) | collective-permute-done | bytes 221216 | tf_op jit(solution)/shard_map/ppermute | solution.py:239
  24.3 1.7 %coarse.1 = (f32[8,8,256]{2,1,0:T(8,128)S(1)}, f32[5,8,256]{2,1,0:T(8,128)S(1)}, f32[5,8,256]{2,1,0:T(8,128)S(1)}, f32[4,4,512]{2,1,0:T(4,128)S(1)}, f32[4,4,512]{2,1,0:T(4,128)S(1)}) custom-call(f32[27,8,256]{2,1,0:T(8,128)S(1)} %pad_maximum_fusion.mid_ref, f32[27,8,256]{2,1,0:T(8,128)S(1)} %collective-permute-done.6.low_ref, ...), custom_call_target="tpu_custom_call" | custom-call | tf_op jit(solution)/shard_map/coarse/pallas_call | solution.py:249
  26.0 0.1 collective-permute-start.8
  26.1 0.1 fusion
  26.2 0.0 collective-permute-start.3
  26.2 0.5 collective-permute-start.2
  26.7 5.3 %collective-permute-start.9 = (f32[5,8,256]{2,1,0:T(8,128)S(1)}, f32[5,8,256]{2,1,0:T(8,128)S(1)}, u32[]{:S(2)}, u32[]{:S(2)}) collective-permute-start(f32[5,8,256]{2,1,0:T(8,128)S(1)} %get-tuple-element.9), channel_id=1, source_target_pairs={{0,120},{8,0},{16,8},{24,16},{32,24},{40,32},{48,40},{56,48},{64,5... | collective-permute-start | bytes 122888 | tf_op jit(solution)/shard_map/ppermute | solution.py:239
  32.0 1.4 %collective-permute-done.8 = f32[5,8,256]{2,1,0:T(8,128)S(1)} collective-permute-done((f32[5,8,256]{2,1,0:T(8,128)S(1)}, f32[5,8,256]{2,1,0:T(8,128)S(1)}, u32[]{:S(2)}, u32[]{:S(2)}) %collective-permute-start.8) | collective-permute-done | bytes 40992 | tf_op jit(solution)/shard_map/ppermute | solution.py:239
  33.4 0.3 collective-permute-done.9
  33.7 1.6 %collective-permute-start.11 = (f32[18,8,256]{2,1,0:T(8,128)S(1)}, f32[18,8,256]{2,1,0:T(8,128)S(1)}, u32[]{:S(2)}, u32[]{:S(2)}) collective-permute-start(f32[18,8,256]{2,1,0:T(8,128)S(1)} %constant_dynamic-update-slice_fusion.3.c_ref), channel_id=1, source_target_pairs={{0,7},{1,0},{2,1},{3,2},{4,3},{5,4},{6,5},{7,6},{8,15},{9,8},{10,9... | collective-permute-start | bytes 442376 | tf_op jit(solution)/shard_map/ppermute | solution.py:239
  35.3 0.0 collective-permute-start.10
  35.3 2.7 %collective-permute-done.11.c_high = f32[18,8,256]{2,1,0:T(8,128)S(1)} collective-permute-done((f32[18,8,256]{2,1,0:T(8,128)S(1)}, f32[18,8,256]{2,1,0:T(8,128)S(1)}, u32[]{:S(2)}, u32[]{:S(2)}) %collective-permute-start.11) | collective-permute-done | bytes 147488 | tf_op jit(solution)/shard_map/ppermute | solution.py:239
  38.0 3.1 %collective-permute-done.10.c_low = f32[18,8,256]{2,1,0:T(8,128)S(1)} collective-permute-done((f32[18,8,256]{2,1,0:T(8,128)S(1)}, f32[18,8,256]{2,1,0:T(8,128)S(1)}, u32[]{:S(2)}, u32[]{:S(2)}) %collective-permute-start.10) | collective-permute-done | bytes 147488 | tf_op jit(solution)/shard_map/ppermute | solution.py:239
  41.1 0.0 collective-permute-done.3.side_high
  41.1 9.3 %fine.1 = (f32[16,16,512]{2,1,0:T(8,128)}, f32[16,16,512]{2,1,0:T(8,128)}) custom-call(f32[32,16,512]{2,1,0:T(8,128)S(1)} %constant_dynamic-update-slice_fusion.side_ref, f32[32,8,512]{2,1,0:T(8,128)S(1)} %collective-permute-done.2.side_low, f32[32,8,512]{2,1,0:T(8,128)S(1)} %collective-permute-done.3.side_high, ...), custom_call_target="tpu_custom_call" | custom-call | tf_op jit(solution)/shard_map/fine/pallas_call | solution.py:265
  (16 shorter events, 0.1 us)
Async XLA Ops:
  0.6 2.8 %copy-start = (f32[16,16,512]{2,1,0:T(8,128)S(1)}, f32[16,16,512]{2,1,0:T(8,128)}, u32[]{:S(2)}) copy-start(f32[16,16,512]{2,1,0:T(8,128)} %side_ref.1) | copy-start | bytes 1572868
  0.6 2.8 %copy-start.1 = (s32[2,2,64]{2,1,0:T(2,128)S(1)}, s32[2,2,64]{2,1,0:T(2,128)}, u32[]{:S(2)}) copy-start(s32[2,2,64]{2,1,0:T(2,128)} %counts_ref.1) | copy-start | bytes 3076
  1.8 16.0 %collective-permute-start = (f32[8,16,512]{2,1,0:T(8,128)S(1)}, f32[8,16,512]{2,1,0:T(8,128)S(1)}, u32[]{:S(2)}, u32[]{:S(2)}) collective-permute-start(f32[8,16,512]{2,1,0:T(8,128)S(1)} %get-tuple-element.15), channel_id=1, source_target_pairs={{0,8},{8,16},{16,24},{24,32},{32,40},{40,48},{48,56},{56,64},{64,7... | collective-permute-start | bytes 786440 | tf_op jit(solution)/shard_map/ppermute | solution.py:239
  4.1 9.2 %collective-permute-start.5 = (f32[9,8,256]{2,1,0:T(8,128)S(1)}, f32[9,8,256]{2,1,0:T(8,128)S(1)}, u32[]{:S(2)}, u32[]{:S(2)}) collective-permute-start(f32[9,8,256]{2,1,0:T(8,128)S(1)} %restrict.1), channel_id=1, source_target_pairs={{0,120},{8,0},{16,8},{24,16},{32,24},{40,32},{48,40},{56,48},{64,5... | collective-permute-start | bytes 221192 | tf_op jit(solution)/shard_map/ppermute | solution.py:239
  7.9 7.7 %collective-permute-start.4 = (f32[9,8,256]{2,1,0:T(8,128)S(1)}, f32[9,8,256]{2,1,0:T(8,128)S(1)}, u32[]{:S(2)}, u32[]{:S(2)}) collective-permute-start(f32[9,8,256]{2,1,0:T(8,128)S(1)} %restrict.1), channel_id=1, source_target_pairs={{0,8},{8,16},{16,24},{24,32},{32,40},{40,48},{48,56},{56,64},{64,7... | collective-permute-start | bytes 221192 | tf_op jit(solution)/shard_map/ppermute | solution.py:239
  7.9 10.3 %collective-permute-start.1 = (f32[8,16,512]{2,1,0:T(8,128)S(1)}, f32[8,16,512]{2,1,0:T(8,128)S(1)}, u32[]{:S(2)}, u32[]{:S(2)}) collective-permute-start(f32[8,16,512]{2,1,0:T(8,128)S(1)} %get-tuple-element.14), channel_id=1, source_target_pairs={{0,120},{8,0},{16,8},{24,16},{32,24},{40,32},{48,40},{56,48},{64,5... | collective-permute-start | bytes 786440 | tf_op jit(solution)/shard_map/ppermute | solution.py:239
  15.6 5.6 %collective-permute-start.7 = (f32[27,8,256]{2,1,0:T(8,128)S(1)}, f32[27,8,256]{2,1,0:T(8,128)S(1)}, u32[]{:S(2)}, u32[]{:S(2)}) collective-permute-start(f32[27,8,256]{2,1,0:T(8,128)S(1)} %pad_maximum_fusion.mid_ref), channel_id=1, source_target_pairs={{0,7},{1,0},{2,1},{3,2},{4,3},{5,4},{6,5},{7,6},{8,15},{9,8},{10,9... | collective-permute-start | bytes 663560 | tf_op jit(solution)/shard_map/ppermute | solution.py:239
  17.7 6.6 %collective-permute-start.6 = (f32[27,8,256]{2,1,0:T(8,128)S(1)}, f32[27,8,256]{2,1,0:T(8,128)S(1)}, u32[]{:S(2)}, u32[]{:S(2)}) collective-permute-start(f32[27,8,256]{2,1,0:T(8,128)S(1)} %pad_maximum_fusion.mid_ref), channel_id=1, source_target_pairs={{0,1},{1,2},{2,3},{3,4},{4,5},{5,6},{6,7},{7,0},{8,9},{9,10},{10,1... | collective-permute-start | bytes 663560 | tf_op jit(solution)/shard_map/ppermute | solution.py:239
  26.0 7.4 %collective-permute-start.8 = (f32[5,8,256]{2,1,0:T(8,128)S(1)}, f32[5,8,256]{2,1,0:T(8,128)S(1)}, u32[]{:S(2)}, u32[]{:S(2)}) collective-permute-start(f32[5,8,256]{2,1,0:T(8,128)S(1)} %get-tuple-element.7), channel_id=1, source_target_pairs={{0,8},{8,16},{16,24},{24,32},{32,40},{40,48},{48,56},{56,64},{64,7... | collective-permute-start | bytes 122888 | tf_op jit(solution)/shard_map/ppermute | solution.py:239
  26.2 14.9 %collective-permute-start.3 = (f32[32,8,512]{2,1,0:T(8,128)S(1)}, f32[32,8,512]{2,1,0:T(8,128)S(1)}, u32[]{:S(2)}, u32[]{:S(2)}) collective-permute-start(f32[32,8,512]{2,1,0:T(8,128)S(1)} %get-tuple-element.12), channel_id=1, source_target_pairs={{0,7},{1,0},{2,1},{3,2},{4,3},{5,4},{6,5},{7,6},{8,15},{9,8},{10,9... | collective-permute-start | bytes 1572872 | tf_op jit(solution)/shard_map/ppermute | solution.py:239
  26.2 14.9 %collective-permute-start.2 = (f32[32,8,512]{2,1,0:T(8,128)S(1)}, f32[32,8,512]{2,1,0:T(8,128)S(1)}, u32[]{:S(2)}, u32[]{:S(2)}) collective-permute-start(f32[32,8,512]{2,1,0:T(8,128)S(1)} %get-tuple-element.13), channel_id=1, source_target_pairs={{0,1},{1,2},{2,3},{3,4},{4,5},{5,6},{6,7},{7,0},{8,9},{9,10},{10,1... | collective-permute-start | bytes 1572872 | tf_op jit(solution)/shard_map/ppermute | solution.py:239
  26.7 7.0 %collective-permute-start.9 = (f32[5,8,256]{2,1,0:T(8,128)S(1)}, f32[5,8,256]{2,1,0:T(8,128)S(1)}, u32[]{:S(2)}, u32[]{:S(2)}) collective-permute-start(f32[5,8,256]{2,1,0:T(8,128)S(1)} %get-tuple-element.9), channel_id=1, source_target_pairs={{0,120},{8,0},{16,8},{24,16},{32,24},{40,32},{48,40},{56,48},{64,5... | collective-permute-start | bytes 122888 | tf_op jit(solution)/shard_map/ppermute | solution.py:239
  33.7 4.3 %collective-permute-start.11 = (f32[18,8,256]{2,1,0:T(8,128)S(1)}, f32[18,8,256]{2,1,0:T(8,128)S(1)}, u32[]{:S(2)}, u32[]{:S(2)}) collective-permute-start(f32[18,8,256]{2,1,0:T(8,128)S(1)} %constant_dynamic-update-slice_fusion.3.c_ref), channel_id=1, source_target_pairs={{0,7},{1,0},{2,1},{3,2},{4,3},{5,4},{6,5},{7,6},{8,15},{9,8},{10,9... | collective-permute-start | bytes 442376 | tf_op jit(solution)/shard_map/ppermute | solution.py:239
  35.3 5.8 %collective-permute-start.10 = (f32[18,8,256]{2,1,0:T(8,128)S(1)}, f32[18,8,256]{2,1,0:T(8,128)S(1)}, u32[]{:S(2)}, u32[]{:S(2)}) collective-permute-start(f32[18,8,256]{2,1,0:T(8,128)S(1)} %constant_dynamic-update-slice_fusion.3.c_ref), channel_id=1, source_target_pairs={{0,1},{1,2},{2,3},{3,4},{4,5},{5,6},{6,7},{7,0},{8,9},{9,10},{10,1... | collective-permute-start | bytes 442376 | tf_op jit(solution)/shard_map/ppermute | solution.py:239

commit v2 on v1

v2 whole, which is shorter than its diff:
```python
import jax
import jax.numpy as jnp
from jax import lax
from jax.experimental import pallas as pl
from jax.experimental.pallas import tpu as pltpu
from jax.sharding import PartitionSpec as P

CENTER = 8.0 / 3.0
OMEGA = 2.0 / 3.0
SCREEN = 0.05
THIRD = 1.0 - OMEGA
F32 = jnp.float32
HIGH = lax.Precision.HIGHEST


def iota(shape, dim):
    return lax.broadcasted_iota(jnp.int32, shape, dim)


def pairing(rows, columns, factor, value):
    r, c = iota((rows, columns), 0), iota((rows, columns), 1)
    hit = (r // factor == c) if rows > columns else (c // factor == r)
    return jnp.where(hit, value, 0.0).astype(F32)


def stencil_rows(load, rows, blocks):
    v, t = {}, {}
    for x in range(rows[0] - 1, rows[-1] + 2):
        v[x] = load(x, 0)
        t[x] = [a + b for a, b in zip(load(x, -1), load(x, 1))]
    lane = iota(v[rows[0]][0].shape, 1)
    first, last = lane == 0, lane == 127
    zero = jnp.zeros(lane.shape, F32)
    out = {}
    for x in rows:
        m = [t[x - 1][b] + t[x + 1][b] for b in range(blocks)]
        w = [0.5 * m[b] + (t[x][b] + (v[x - 1][b] + v[x + 1][b])) for b in range(blocks)]
        up = [pltpu.roll(w[b], 1, 1) for b in range(blocks)]
        down = [pltpu.roll(w[b], 127, 1) for b in range(blocks)]
        total = []
        for b in range(blocks):
            below = jnp.where(first, up[b - 1] if b else zero, up[b])
            above = jnp.where(last, down[b + 1] if b < blocks - 1 else zero, down[b])
            total.append((below + above) + m[b])
        out[x] = total
    return v, out


def sweep(rows, starts, blocks, source, target, drive, coupling):
    for start in starts:
        def load(x, shift):
            ref, at = source(x)
            return [ref[at, b, pl.ds(start + shift, 8), :] for b in range(blocks)]

        v, out = stencil_rows(load, rows, blocks)
        here = pl.ds(start, 8)
        for x in rows:
            (to, i), (forcing, j), (factor, k) = target(x), drive(x), coupling(x)
            for b in range(blocks):
                to[i, b, here, :] = (
                    THIRD * v[x][b] + factor[k, b, here, :] * out[x][b] + forcing[j, b, here, :]
                )


def in_domain(index, low, count):
    place = low + index - 1
    return jnp.where((place >= 0) & (place < count), 1.0, 0.0).astype(F32)


def place():
    return lax.axis_index("gx"), lax.axis_index("gy"), lax.axis_size("gx"), lax.axis_size("gy")


def restrict_kernel(side_ref, counts_ref, out_ref, first_ref, second_ref, tmp):
    for x in range(8):
        tmp[16 * x : 16 * x + 16, :] = side_ref[2 * x] + side_ref[2 * x + 1]
    halves = pairing(512, 256, 2, 0.5)
    rows = jnp.dot(pairing(64, 128, 2, 1.0), tmp[...], precision=HIGH, preferred_element_type=F32)
    coarse = jnp.dot(rows, halves, precision=HIGH, preferred_element_type=F32)
    for x in range(8):
        out_ref[x] = coarse[8 * x : 8 * x + 8, :]
    out_ref[8] = jnp.zeros((8, 256), F32)
    out_ref[8, 0:4, 0:64] = counts_ref[...].reshape(4, 64).astype(F32)
    first_ref[...] = side_ref[:, 0:8, :]
    second_ref[...] = side_ref[:, 8:16, :]


def coarse_kernel(mid_ref, low_ref, high_ref, c_ref, inv_ref, center_ref, even, odd, drive, coupling):
    gx, gy, n_gx, n_gy = place()
    strips = (low_ref, mid_ref, high_ref)
    counts = jnp.concatenate([strips[j][9 * i + 8][:, 0:64] for i in range(3) for j in range(3)], axis=0)
    spread = jnp.dot(counts, pairing(64, 256, 4, 1.0), precision=HIGH, preferred_element_type=F32)
    weight = OMEGA / (CENTER + (SCREEN * 4.0) * spread)
    sub = iota((8, 128), 0)
    zero = jnp.zeros((8, 128), F32)
    for x in range(26):
        for b in range(2):
            for field in (even, odd):
                for start in (0, 32):
                    field[x, b, start : start + 8, :] = zero
    for i in range(3):
        for j in range(3):
            inside = in_domain(i, gx, n_gx) * in_domain(j, gy, n_gy)
            group = weight[8 * (3 * i + j) : 8 * (3 * i + j) + 8, :] * inside
            here = pl.ds(8 * j + 8, 8)
            for k in range(2):
                for b in range(2):
                    lanes = slice(128 * b, 128 * b + 128)
                    tile = jnp.where(
                        sub < 4,
                        jnp.broadcast_to(group[2 * k : 2 * k + 1, lanes], (8, 128)),
                        jnp.broadcast_to(group[2 * k + 1 : 2 * k + 2, lanes], (8, 128)),
                    )
                    coupling[2 * i + k, b, here, :] = tile * (1.0 / 6.0)
                    for x in range(4):
                        at = 8 * i + 4 * k + x
                        value = tile * strips[j][9 * i + 4 * k + x, :, lanes]
                        drive[at + 1, b, here, :] = value
                        even[at + 1, b, here, :] = value
    for k in range(7):
        halo = 6 - k
        source, target = (even, odd) if k % 2 == 0 else (odd, even)
        starts = (8, 16, 24) if halo > 4 else ((12, 20) if halo else (16,))
        sweep(
            range(-halo, 8 + halo), starts, 2,
            lambda x: (source, x + 9),
            lambda x: (target, x + 9),
            lambda x: (drive, x + 9),
            lambda x: (coupling, (x + 8) // 4),
        )
    for x in range(8):
        c_ref[x] = jnp.concatenate([odd[9 + x, b, 16:24, :] for b in range(2)], axis=1)

    wide = jnp.dot(counts, pairing(64, 512, 8, 1.0), precision=HIGH, preferred_element_type=F32)
    center = CENTER + SCREEN * wide
    inverse = OMEGA / center
    for xb in range(4):
        i, k = ((xb + 1) // 2, (xb + 1) % 2)
        for yb in range(4):
            j, l = ((yb + 1) // 2, (yb + 1) % 2)
            at = 8 * (3 * i + j) + 2 * k + l
            inside = in_domain(i, gx, n_gx) * in_domain(j, gy, n_gy)
            inv_ref[xb, yb : yb + 1, :] = inverse[at : at + 1, :] * inside
            center_ref[xb, yb : yb + 1, :] = center[at : at + 1, :]


def fine_starts(k):
    return (8, 16, 24, 32) if k < 5 else (12, 20, 28)


def inject(rows, targets):
    doubling = pairing(256, 512, 2, 1.0)
    grown = jnp.dot(jnp.concatenate(rows, axis=0), doubling, precision=HIGH, preferred_element_type=F32)
    for n, (field, x, start) in enumerate(targets):
        for b in range(4):
            value = grown[8 * n : 8 * n + 8, 128 * b : 128 * b + 128]
            for dx in range(2):
                for dy in range(2):
                    field[x + dx, b, pl.ds(start + dy, 8, stride=2), :] = value


def weigh(inv_ref, bricks, coupling, first, drive_rows):
    for xb in bricks:
        for yb in range(4):
            here = pl.ds(8 * yb + 8, 8)
            for b in range(4):
                lanes = slice(128 * b, 128 * b + 128)
                tile = jnp.broadcast_to(inv_ref[xb, yb : yb + 1, lanes], (8, 128))
                coupling[xb - first, b, here, :] = tile * (1.0 / 6.0)
                for to, at, sources in drive_rows(xb):
                    ref, x, row = sources[yb]
                    to[at, b, here, :] = tile * ref[x, row : row + 8, lanes]


def inner_kernel(side_ref, side_low, side_high, c_ref, c_low, c_high, inv_ref, even, odd, drive, coupling):
    _, gy, _, n_gy = place()
    zero = jnp.zeros((8, 128), F32)
    for x in range(16):
        for b in range(4):
            odd[x, b, 0:8, :] = zero
            odd[x, b, 40:48, :] = zero
    rows, targets = [], []
    for j, ref in enumerate((c_low, c_ref, c_high)):
        for x in range(8):
            rows.append(ref[x] * in_domain(j, gy, n_gy))
            targets.append((even, 2 * x, 16 * j))
    inject(rows, targets)
    weigh(
        inv_ref, (1, 2), coupling, 1,
        lambda xb: [
            (drive, x, ((side_low, x, 0), (side_ref, x, 0), (side_ref, x, 8), (side_high, x, 0)))
            for x in range(8 * xb - 8, 8 * xb)
        ],
    )
    for k in range(1, 8):
        source, target = (odd, even) if k % 2 == 0 else (even, odd)
        sweep(
            range(k, 16 - k), fine_starts(k), 4,
            lambda x: (source, x),
            lambda x: (target, x),
            lambda x: (drive, x),
            lambda x: (coupling, x // 8),
        )


def outer_kernel(side_ref, side_low, side_high, c_low, c_high, inv_ref, center_ref, inner_even, inner_odd,
                 inner_drive, inner_coupling, solution_ref, residual_ref, even, odd, drive, coupling):
    gx, gy, n_gx, n_gy = place()
    zero = jnp.zeros((8, 128), F32)
    for x in range(36):
        for b in range(4):
            odd[x, b, 0:8, :] = zero
            odd[x, b, 40:48, :] = zero
    rows, targets = [], []
    for i, ref, first in ((0, c_low, 0), (2, c_high, 26)):
        for j in range(3):
            inside = in_domain(i, gx, n_gx) * in_domain(j, gy, n_gy)
            for x in range(5):
                rows.append(ref[x, 8 * j : 8 * j + 8, :] * inside)
                targets.append((even, first + 2 * x, 16 * j))
    inject(rows, targets)
    weigh(
        inv_ref, (0, 3), coupling, 0,
        lambda xb: [
            (drive, x + (2 if xb == 0 else 26), [(side_low if xb == 0 else side_high, x, 8 * yb) for yb in range(4)])
            for x in range(8)
        ],
    )

    def state(k, x):
        if k <= x < 16 - k:
            return (inner_odd if k % 2 else inner_even), x
        return (odd if k % 2 else even), x + 10

    def forcing(x):
        return (inner_drive, x) if 0 <= x < 16 else (drive, x + 10)

    def factor(x):
        return (inner_coupling, x // 8) if 0 <= x < 16 else (coupling, x // 8 + 1)

    for k in range(1, 9):
        for rows in (range(k - 9, k), range(16 - k, 25 - k)):
            sweep(
                rows, fine_starts(k), 4,
                lambda x: state(k - 1, x),
                lambda x: state(k, x),
                forcing,
                factor,
            )
    for start in (16, 24):
        def load(x, shift):
            return [even[x + 10, b, pl.ds(start + shift, 8), :] for b in range(4)]

        v, out = stencil_rows(load, range(16), 4)
        for x in range(16):
            for b in range(4):
                lanes, rows = slice(128 * b, 128 * b + 128), slice(start - 16, start - 8)
                center = center_ref[1 + x // 8, start // 8 - 1 : start // 8, lanes]
                solution_ref[x, rows, lanes] = v[x][b]
                residual_ref[x, rows, lanes] = side_ref[x, rows, lanes] - center * v[x][b] + (1.0 / 6.0) * out[x][b]


def shape(*dims):
    return jax.ShapeDtypeStruct(dims, F32)


def call(kernel, outputs, scratch, name):
    return pl.pallas_call(
        kernel,
        out_shape=[shape(*dims) for dims in outputs],
        scratch_shapes=[pltpu.VMEM(dims, F32) for dims in scratch],
        compiler_params=pltpu.CompilerParams(vmem_limit_bytes=20 * 1024 * 1024),
        name=name,
    )


def shards(right_side, point_counts):
    def move(value, axis, step):
        count = lax.axis_size(axis)
        return lax.ppermute(value, axis, [(i, (i + step) % count) for i in range(count)])

    packed, first, second = call(
        restrict_kernel, [(9, 8, 256), (16, 8, 512), (16, 8, 512)], [(128, 512)], "restrict"
    )(right_side, point_counts)
    packed = jnp.concatenate([move(packed, "gx", 1), packed, move(packed, "gx", -1)], axis=0)
    side_low, side_high = move(second, "gy", 1), move(first, "gy", -1)
    coarse, inverse, center = call(
        coarse_kernel,
        [(8, 8, 256), (4, 4, 512), (4, 4, 512)],
        [(26, 2, 40, 128)] * 3 + [(6, 2, 40, 128)],
        "coarse",
    )(packed, move(packed, "gy", 1), move(packed, "gy", -1))
    coarse_low, coarse_high = move(coarse, "gy", 1), move(coarse, "gy", -1)
    side = jnp.concatenate([side_low, right_side, side_high], axis=1)
    side_left, side_right = move(side[8:16], "gx", 1), move(side[0:8], "gx", -1)
    wide = jnp.concatenate([coarse_low, coarse, coarse_high], axis=1)
    coarse_left, coarse_right = move(wide[3:8], "gx", 1), move(wide[0:5], "gx", -1)
    field = (16, 4, 48, 128)
    inner = call(inner_kernel, [field, field, field, (2, 4, 48, 128)], [], "inner")(
        right_side, side_low, side_high, coarse, coarse_low, coarse_high, inverse
    )
    field = (36, 4, 48, 128)
    return call(
        outer_kernel, [(16, 16, 512)] * 2, [field, field, field, (4, 4, 48, 128)], "outer"
    )(right_side, side_left, side_right, coarse_left, coarse_right, inverse, center, *inner)


def solution(mesh):
    specs = (P("gx", "gy", None), P("gx", "gy", None))
    return jax.shard_map(shards, mesh=mesh, in_specs=specs, out_specs=specs, check_vma=False)
```

time: 50.6 us -> 51.2 us (1.012)
  starting transfers between devices: 20.5 us -> 23.3 us
  waiting for transfers between devices: 16.2 us -> 14.1 us
  Pallas kernels: 11.6 us -> 10.9 us
  local copies, waits for them, and re-layouts: 1.3 us -> 1.95 us
    ppermute x12, starting transfers between devices: 20.5 us -> 23.3 us  [move(): lax.ppermute(value, axis, [(i, (i + step) % count) for i in range(count)])]
    ppermute x12, waiting for transfers between devices: 16.2 us -> 14.1 us  [move(): lax.ppermute(value, axis, [(i, (i + step) % count) for i in range(count)])]
    unnamed x8 -> x12, local copies, waits for them, and re-layouts: 0.07 us -> 1.81 us
    slice x2, local copies, waits for them, and re-layouts: 1.2 us -> 0.11 us  [the longest x1 0.09 us: shards(): side[0:8]]
    pallas_call x3 -> x4, Pallas kernels: 11.6 us -> 10.9 us  [the longest x1 6.12 us: shards(): call(outer_kernel, [(16, 16, 512)] * 2, [field, field, field, (4, 4, 48,...]
  transfers between devices with their start and end apart: 12 -> 12, of which waited for: 8 -> 6; matrix products, arithmetic and copies ran while one was open for 0% -> 0% of each run, Pallas kernels for 1% -> 5%
where the time goes in v2:
time: 51.2 us; the launch traced here: 51 us
  starting transfers between devices  23.3 us (46%)
  waiting for transfers between devices  14.1 us (28%)
  Pallas kernels  10.9 us (21%)
  local copies, waits for them, and re-layouts  1.95 us (4%)
  between operations  0.76 us (1%)
    ppermute x12, starting transfers between devices, move(): lax.ppermute(value, axis, [(i, (i + step) % count) for i in range(count)])  23.3 us
    ppermute x12, waiting for transfers between devices, move(): lax.ppermute(value, axis, [(i, (i + step) % count) for i in range(count)])  14.1 us
    pallas_call x1, Pallas kernels, shards(): call(outer_kernel, [(16, 16, 512)] * 2, [field, field, field, (4, 4, 48,...  6.12 us
    pallas_call x1, Pallas kernels, shards(): call(inner_kernel, [field, field, field, (2, 4, 48, 128)], [], 'inner')  2.58 us
    unnamed x12, local copies, waits for them, and re-layouts  1.81 us
    pallas_call x1, Pallas kernels, shards(): call(coarse_kernel, [(8, 8, 256), (4, 4, 512), (4, 4, 512)], [(26, 2, 40,...  1.62 us
  transfers between devices with their start and end apart: 12, of which 6 were waited for; matrix products, arithmetic and copies ran while one was open for 0% of the time, Pallas kernels for 5%

profile of v2, /device:TPU:0, one launch (start us, length us, event | category | flops | bytes accessed | tf_op | source)
XLA Modules:
  0.0 51.0 jit_solution(5633466954273581618)
XLA Ops:
  0.6 0.0 copy-start
  0.6 1.0 %copy-done = f32[16,16,512]{2,1,0:T(8,128)S(1)} copy-done((f32[16,16,512]{2,1,0:T(8,128)S(1)}, f32[16,16,512]{2,1,0:T(8,128)}, u32[]{:S(2)}) %copy-start) | copy-done | bytes 524312
  1.7 0.7 %copy-done.2 = s32[2,2,64]{2,1,0:T(2,128)S(1)} copy-done((s32[2,2,64]{2,1,0:T(2,128)S(1)}, s32[2,2,64]{2,1,0:T(2,128)}, u32[]{:S(2)}) %copy-start.2) | copy-done | bytes 1048
  2.4 0.6 %restrict.1 = (f32[9,8,256]{2,1,0:T(8,128)S(1)}, f32[16,8,512]{2,1,0:T(8,128)S(1)}, f32[16,8,512]{2,1,0:T(8,128)S(1)}) custom-call(f32[16,16,512]{2,1,0:T(8,128)S(1)} %copy-done, s32[2,2,64]{2,1,0:T(2,128)S(1)} %copy-done.2), custom_call_target="tpu_custom_call" | custom-call | tf_op jit(solution)/shard_map/restrict/pallas_call | solution.py:282
  3.0 1.6 %collective-permute-start.4 = (f32[9,8,256]{2,1,0:T(8,128)S(1)}, f32[9,8,256]{2,1,0:T(8,128)S(1)}, u32[]{:S(2)}, u32[]{:S(2)}) collective-permute-start(f32[9,8,256]{2,1,0:T(8,128)S(1)} %get-tuple-element.14), channel_id=1, source_target_pairs={{0,8},{8,16},{16,24},{24,32},{32,40},{40,48},{48,56},{56,64},{64,7... | collective-permute-start | bytes 221192 | tf_op jit(solution)/shard_map/ppermute | solution.py:280
  4.6 3.8 %collective-permute-start.5 = (f32[9,8,256]{2,1,0:T(8,128)S(1)}, f32[9,8,256]{2,1,0:T(8,128)S(1)}, u32[]{:S(2)}, u32[]{:S(2)}) collective-permute-start(f32[9,8,256]{2,1,0:T(8,128)S(1)} %get-tuple-element.14), channel_id=1, source_target_pairs={{0,120},{8,0},{16,8},{24,16},{32,24},{40,32},{48,40},{56,48},{64,5... | collective-permute-start | bytes 221192 | tf_op jit(solution)/shard_map/ppermute | solution.py:280
  8.4 3.2 %collective-permute-start.1 = (f32[16,8,512]{2,1,0:T(8,128)S(1)}, f32[16,8,512]{2,1,0:T(8,128)S(1)}, u32[]{:S(2)}, u32[]{:S(2)}) collective-permute-start(f32[16,8,512]{2,1,0:T(8,128)S(1)} %get-tuple-element.13), channel_id=1, source_target_pairs={{0,7},{1,0},{2,1},{3,2},{4,3},{5,4},{6,5},{7,6},{8,15},{9,8},{10,9... | collective-permute-start | bytes 786440 | tf_op jit(solution)/shard_map/ppermute | solution.py:280
  11.7 1.7 %collective-permute-start.7 = (f32[27,8,256]{2,1,0:T(8,128)S(1)}, f32[27,8,256]{2,1,0:T(8,128)S(1)}, u32[]{:S(2)}, u32[]{:S(2)}) collective-permute-start(f32[27,8,256]{2,1,0:T(8,128)S(1)} %constant_dynamic-update-slice_fusion.3.mid_ref), channel_id=1, source_target_pairs={{0,7},{1,0},{2,1},{3,2},{4,3},{5,4},{6,5},{7,6},{8,15},{9,8},{10,9... | collective-permute-start | bytes 663560 | tf_op jit(solution)/shard_map/ppermute | solution.py:280
  13.4 2.3 %collective-permute-done.side_low = f32[16,8,512]{2,1,0:T(8,128)S(1)} collective-permute-done((f32[16,8,512]{2,1,0:T(8,128)S(1)}, f32[16,8,512]{2,1,0:T(8,128)S(1)}, u32[]{:S(2)}, u32[]{:S(2)}) %collective-permute-start) | collective-permute-done | bytes 262176 | tf_op jit(solution)/shard_map/ppermute | solution.py:280
  15.8 2.1 %collective-permute-done.7.high_ref = f32[27,8,256]{2,1,0:T(8,128)S(1)} collective-permute-done((f32[27,8,256]{2,1,0:T(8,128)S(1)}, f32[27,8,256]{2,1,0:T(8,128)S(1)}, u32[]{:S(2)}, u32[]{:S(2)}) %collective-permute-start.7) | collective-permute-done | bytes 221216 | tf_op jit(solution)/shard_map/ppermute | solution.py:280
  17.9 2.0 %collective-permute-done.6.low_ref = f32[27,8,256]{2,1,0:T(8,128)S(1)} collective-permute-done((f32[27,8,256]{2,1,0:T(8,128)S(1)}, f32[27,8,256]{2,1,0:T(8,128)S(1)}, u32[]{:S(2)}, u32[]{:S(2)}) %collective-permute-start.6) | collective-permute-done | bytes 221216 | tf_op jit(solution)/shard_map/ppermute | solution.py:280
  19.9 1.6 %coarse.1 = (f32[8,8,256]{2,1,0:T(8,128)S(1)}, f32[4,4,512]{2,1,0:T(4,128)S(1)}, f32[4,4,512]{2,1,0:T(4,128)S(1)}) custom-call(f32[27,8,256]{2,1,0:T(8,128)S(1)} %constant_dynamic-update-slice_fusion.3.mid_ref, f32[27,8,256]{2,1,0:T(8,128)S(1)} %collective-permute-done.6.low_ref, f32[27,8,256]{2,1,0:T(8,128)S(1)} %collective-permute-done.7.high_ref), custom_call_target="tpu_custom_call" | custom-call | tf_op jit(solution)/shard_map/coarse/pallas_call | solution.py:287
  21.5 0.0 copy-start.1
  21.6 0.0 collective-permute-start.8
  21.6 0.1 fusion
  21.7 5.2 %collective-permute-start.3 = (f32[8,32,512]{2,1,0:T(8,128)S(1)}, f32[8,32,512]{2,1,0:T(8,128)S(1)}, u32[]{:S(2)}, u32[]{:S(2)}) collective-permute-start(f32[8,32,512]{2,1,0:T(8,128)S(1)} %get-tuple-element.22), channel_id=1, source_target_pairs={{0,120},{8,0},{16,8},{24,16},{32,24},{40,32},{48,40},{56,48},{64,5... | collective-permute-start | bytes 1572872 | tf_op jit(solution)/shard_map/ppermute | solution.py:280
  26.8 2.7 %collective-permute-start.9 = (f32[8,8,256]{2,1,0:T(8,128)S(1)}, f32[8,8,256]{2,1,0:T(8,128)S(1)}, u32[]{:S(2)}, u32[]{:S(2)}) collective-permute-start(f32[8,8,256]{2,1,0:T(8,128)S(1)} %get-tuple-element.15.c_ref), channel_id=1, source_target_pairs={{0,7},{1,0},{2,1},{3,2},{4,3},{5,4},{6,5},{7,6},{8,15},{9,8},{10,9... | collective-permute-start | bytes 196616 | tf_op jit(solution)/shard_map/ppermute | solution.py:280
  29.5 1.9 %collective-permute-done.9.c_high = f32[8,8,256]{2,1,0:T(8,128)S(1)} collective-permute-done((f32[8,8,256]{2,1,0:T(8,128)S(1)}, f32[8,8,256]{2,1,0:T(8,128)S(1)}, u32[]{:S(2)}, u32[]{:S(2)}) %collective-permute-start.9) | collective-permute-done | bytes 65568 | tf_op jit(solution)/shard_map/ppermute | solution.py:280
  31.4 5.1 %collective-permute-start.11 = (f32[5,24,256]{2,1,0:T(8,128)S(1)}, f32[5,24,256]{2,1,0:T(8,128)S(1)}, u32[]{:S(2)}, u32[]{:S(2)}) collective-permute-start(f32[5,24,256]{2,1,0:T(8,128)S(1)} %get-tuple-element.24), channel_id=1, source_target_pairs={{0,120},{8,0},{16,8},{24,16},{32,24},{40,32},{48,40},{56,48},{64,5... | collective-permute-start | bytes 368648 | tf_op jit(solution)/shard_map/ppermute | solution.py:280
  36.6 0.0 collective-permute-start.10
  36.6 2.6 %inner.1 = (f32[16,4,48,128]{3,2,1,0:T(8,128)S(1)}, f32[16,4,48,128]{3,2,1,0:T(8,128)S(1)}, f32[16,4,48,128]{3,2,1,0:T(8,128)S(1)}, f32[2,4,48,128]{3,2,1,0:T(8,128)S(1)}) custom-call(f32[16,16,512]{2,1,0:T(8,128)S(1)} %copy-done.1, f32[16,8,512]{2,1,0:T(8,128)S(1)} %collective-permute-done.side_low, f32[16,8,512]{2,1,0:T(8,128)S(1)} %collective-permute-done.1.side_high, ...), custom_call_target="tpu_custom_call" | custom-call | tf_op jit(solution)/shard_map/inner/pallas_call | solution.py:299
  39.2 0.2 collective-permute-done.11.c_high
  39.4 5.5 %collective-permute-done.10.c_low = f32[5,24,256]{2,1,0:T(8,128)S(1)} collective-permute-done((f32[5,24,256]{2,1,0:T(8,128)S(1)}, f32[5,24,256]{2,1,0:T(8,128)S(1)}, u32[]{:S(2)}, u32[]{:S(2)}) %collective-permute-start.10) | collective-permute-done | bytes 122912 | tf_op jit(solution)/shard_map/ppermute | solution.py:280
  44.9 6.1 %outer.1 = (f32[16,16,512]{2,1,0:T(8,128)}, f32[16,16,512]{2,1,0:T(8,128)}) custom-call(f32[16,16,512]{2,1,0:T(8,128)S(1)} %copy-done.1, f32[8,32,512]{2,1,0:T(8,128)S(1)} %collective-permute-done.2.side_low, f32[8,32,512]{2,1,0:T(8,128)S(1)} %collective-permute-done.3.side_high, f32[5,24,256]{2,1,0:T(8,128)S(1)} %collective-permute-done.10.c_low, ...), custom_call_target="tpu_custom_call" | custom-call | tf_op jit(solution)/shard_map/outer/pallas_call | solution.py:303
  (21 shorter events, 0.2 us)
Async XLA Ops:
  0.6 1.0 %copy-start = (f32[16,16,512]{2,1,0:T(8,128)S(1)}, f32[16,16,512]{2,1,0:T(8,128)}, u32[]{:S(2)}) copy-start(f32[16,16,512]{2,1,0:T(8,128)} %side_ref.5) | copy-start | bytes 1572868
  1.7 0.7 %copy-start.2 = (s32[2,2,64]{2,1,0:T(2,128)S(1)}, s32[2,2,64]{2,1,0:T(2,128)}, u32[]{:S(2)}) copy-start(s32[2,2,64]{2,1,0:T(2,128)} %counts_ref.1) | copy-start | bytes 3076
  3.0 8.6 %collective-permute-start.4 = (f32[9,8,256]{2,1,0:T(8,128)S(1)}, f32[9,8,256]{2,1,0:T(8,128)S(1)}, u32[]{:S(2)}, u32[]{:S(2)}) collective-permute-start(f32[9,8,256]{2,1,0:T(8,128)S(1)} %get-tuple-element.14), channel_id=1, source_target_pairs={{0,8},{8,16},{16,24},{24,32},{32,40},{40,48},{48,56},{56,64},{64,7... | collective-permute-start | bytes 221192 | tf_op jit(solution)/shard_map/ppermute | solution.py:280
  4.6 7.0 %collective-permute-start.5 = (f32[9,8,256]{2,1,0:T(8,128)S(1)}, f32[9,8,256]{2,1,0:T(8,128)S(1)}, u32[]{:S(2)}, u32[]{:S(2)}) collective-permute-start(f32[9,8,256]{2,1,0:T(8,128)S(1)} %get-tuple-element.14), channel_id=1, source_target_pairs={{0,120},{8,0},{16,8},{24,16},{32,24},{40,32},{48,40},{56,48},{64,5... | collective-permute-start | bytes 221192 | tf_op jit(solution)/shard_map/ppermute | solution.py:280
  8.4 7.2 %collective-permute-start = (f32[16,8,512]{2,1,0:T(8,128)S(1)}, f32[16,8,512]{2,1,0:T(8,128)S(1)}, u32[]{:S(2)}, u32[]{:S(2)}) collective-permute-start(f32[16,8,512]{2,1,0:T(8,128)S(1)} %get-tuple-element.12), channel_id=1, source_target_pairs={{0,1},{1,2},{2,3},{3,4},{4,5},{5,6},{6,7},{7,0},{8,9},{9,10},{10,1... | collective-permute-start | bytes 786440 | tf_op jit(solution)/shard_map/ppermute | solution.py:280
  8.4 7.3 %collective-permute-start.1 = (f32[16,8,512]{2,1,0:T(8,128)S(1)}, f32[16,8,512]{2,1,0:T(8,128)S(1)}, u32[]{:S(2)}, u32[]{:S(2)}) collective-permute-start(f32[16,8,512]{2,1,0:T(8,128)S(1)} %get-tuple-element.13), channel_id=1, source_target_pairs={{0,7},{1,0},{2,1},{3,2},{4,3},{5,4},{6,5},{7,6},{8,15},{9,8},{10,9... | collective-permute-start | bytes 786440 | tf_op jit(solution)/shard_map/ppermute | solution.py:280
  11.7 6.2 %collective-permute-start.7 = (f32[27,8,256]{2,1,0:T(8,128)S(1)}, f32[27,8,256]{2,1,0:T(8,128)S(1)}, u32[]{:S(2)}, u32[]{:S(2)}) collective-permute-start(f32[27,8,256]{2,1,0:T(8,128)S(1)} %constant_dynamic-update-slice_fusion.3.mid_ref), channel_id=1, source_target_pairs={{0,7},{1,0},{2,1},{3,2},{4,3},{5,4},{6,5},{7,6},{8,15},{9,8},{10,9... | collective-permute-start | bytes 663560 | tf_op jit(solution)/shard_map/ppermute | solution.py:280
  13.3 6.6 %collective-permute-start.6 = (f32[27,8,256]{2,1,0:T(8,128)S(1)}, f32[27,8,256]{2,1,0:T(8,128)S(1)}, u32[]{:S(2)}, u32[]{:S(2)}) collective-permute-start(f32[27,8,256]{2,1,0:T(8,128)S(1)} %constant_dynamic-update-slice_fusion.3.mid_ref), channel_id=1, source_target_pairs={{0,1},{1,2},{2,3},{3,4},{4,5},{5,6},{6,7},{7,0},{8,9},{9,10},{10,1... | collective-permute-start | bytes 663560 | tf_op jit(solution)/shard_map/ppermute | solution.py:280
  21.5 15.0 %copy-start.1 = (f32[16,16,512]{2,1,0:T(8,128)S(1)}, f32[16,16,512]{2,1,0:T(8,128)}, u32[]{:S(2)}) copy-start(f32[16,16,512]{2,1,0:T(8,128)} %side_ref.5) | copy-start | bytes 1572868
  21.6 8.0 %collective-permute-start.8 = (f32[8,8,256]{2,1,0:T(8,128)S(1)}, f32[8,8,256]{2,1,0:T(8,128)S(1)}, u32[]{:S(2)}, u32[]{:S(2)}) collective-permute-start(f32[8,8,256]{2,1,0:T(8,128)S(1)} %get-tuple-element.15.c_ref), channel_id=1, source_target_pairs={{0,1},{1,2},{2,3},{3,4},{4,5},{5,6},{6,7},{7,0},{8,9},{9,10},{10,1... | collective-permute-start | bytes 196616 | tf_op jit(solution)/shard_map/ppermute | solution.py:280
  21.7 23.2 %collective-permute-start.3 = (f32[8,32,512]{2,1,0:T(8,128)S(1)}, f32[8,32,512]{2,1,0:T(8,128)S(1)}, u32[]{:S(2)}, u32[]{:S(2)}) collective-permute-start(f32[8,32,512]{2,1,0:T(8,128)S(1)} %get-tuple-element.22), channel_id=1, source_target_pairs={{0,120},{8,0},{16,8},{24,16},{32,24},{40,32},{48,40},{56,48},{64,5... | collective-permute-start | bytes 1572872 | tf_op jit(solution)/shard_map/ppermute | solution.py:280
  26.8 18.1 %collective-permute-start.2 = (f32[8,32,512]{2,1,0:T(8,128)S(1)}, f32[8,32,512]{2,1,0:T(8,128)S(1)}, u32[]{:S(2)}, u32[]{:S(2)}) collective-permute-start(f32[8,32,512]{2,1,0:T(8,128)S(1)} %get-tuple-element.23), channel_id=1, source_target_pairs={{0,8},{8,16},{16,24},{24,32},{32,40},{40,48},{48,56},{56,64},{64,7... | collective-permute-start | bytes 1572872 | tf_op jit(solution)/shard_map/ppermute | solution.py:280
  26.8 4.6 %collective-permute-start.9 = (f32[8,8,256]{2,1,0:T(8,128)S(1)}, f32[8,8,256]{2,1,0:T(8,128)S(1)}, u32[]{:S(2)}, u32[]{:S(2)}) collective-permute-start(f32[8,8,256]{2,1,0:T(8,128)S(1)} %get-tuple-element.15.c_ref), channel_id=1, source_target_pairs={{0,7},{1,0},{2,1},{3,2},{4,3},{5,4},{6,5},{7,6},{8,15},{9,8},{10,9... | collective-permute-start | bytes 196616 | tf_op jit(solution)/shard_map/ppermute | solution.py:280
  31.4 7.9 %collective-permute-start.11 = (f32[5,24,256]{2,1,0:T(8,128)S(1)}, f32[5,24,256]{2,1,0:T(8,128)S(1)}, u32[]{:S(2)}, u32[]{:S(2)}) collective-permute-start(f32[5,24,256]{2,1,0:T(8,128)S(1)} %get-tuple-element.24), channel_id=1, source_target_pairs={{0,120},{8,0},{16,8},{24,16},{32,24},{40,32},{48,40},{56,48},{64,5... | collective-permute-start | bytes 368648 | tf_op jit(solution)/shard_map/ppermute | solution.py:280
  36.6 8.3 %collective-permute-start.10 = (f32[5,24,256]{2,1,0:T(8,128)S(1)}, f32[5,24,256]{2,1,0:T(8,128)S(1)}, u32[]{:S(2)}, u32[]{:S(2)}) collective-permute-start(f32[5,24,256]{2,1,0:T(8,128)S(1)} %get-tuple-element.25), channel_id=1, source_target_pairs={{0,8},{8,16},{16,24},{24,32},{32,40},{40,48},{48,56},{56,64},{64,7... | collective-permute-start | bytes 368648 | tf_op jit(solution)/shard_map/ppermute | solution.py:280

commit v3 on v2

--- a/solution.py
+++ b/solution.py
@@ -11,6 +11,8 @@
 THIRD = 1.0 - OMEGA
 F32 = jnp.float32
 HIGH = lax.Precision.HIGHEST
+COARSE_US = 20
+INNER_US = 20
 
 
 def iota(shape, dim):
@@ -203,8 +205,9 @@
         )
 
 
-def outer_kernel(side_ref, side_low, side_high, c_low, c_high, inv_ref, center_ref, inner_even, inner_odd,
-                 inner_drive, inner_coupling, solution_ref, residual_ref, even, odd, drive, coupling):
+def outer_kernel(side_ref, side_left, side_right, corner_low, corner_high, c_low, c_high, inv_ref, center_ref,
+                 inner_even, inner_odd, inner_drive, inner_coupling, solution_ref, residual_ref,
+                 even, odd, drive, coupling):
     gx, gy, n_gx, n_gy = place()
     zero = jnp.zeros((8, 128), F32)
     for x in range(36):
@@ -219,13 +222,14 @@
                 rows.append(ref[x, 8 * j : 8 * j + 8, :] * inside)
                 targets.append((even, first + 2 * x, 16 * j))
     inject(rows, targets)
-    weigh(
-        inv_ref, (0, 3), coupling, 0,
-        lambda xb: [
-            (drive, x + (2 if xb == 0 else 26), [(side_low if xb == 0 else side_high, x, 8 * yb) for yb in range(4)])
+    def outer_rows(xb):
+        first, at, ref = (2, 0, side_left) if xb == 0 else (26, 8, side_right)
+        return [
+            (drive, x + first, ((corner_low, at + x, 0), (ref, x, 0), (ref, x, 8), (corner_high, at + x, 0)))
             for x in range(8)
-        ],
-    )
+        ]
+
+    weigh(inv_ref, (0, 3), coupling, 0, outer_rows)
 
     def state(k, x):
         if k <= x < 16 - k:
@@ -264,12 +268,14 @@
     return jax.ShapeDtypeStruct(dims, F32)
 
 
-def call(kernel, outputs, scratch, name):
+def call(kernel, outputs, scratch, name, microseconds):
+    cost = pl.CostEstimate(flops=int(microseconds * 1.0e9), bytes_accessed=int(microseconds * 3.69e6), transcendentals=0)
     return pl.pallas_call(
         kernel,
         out_shape=[shape(*dims) for dims in outputs],
         scratch_shapes=[pltpu.VMEM(dims, F32) for dims in scratch],
         compiler_params=pltpu.CompilerParams(vmem_limit_bytes=20 * 1024 * 1024),
+        cost_estimate=cost,
         name=name,
     )
 
@@ -280,29 +286,36 @@
         return lax.ppermute(value, axis, [(i, (i + step) % count) for i in range(count)])
 
     packed, first, second = call(
-        restrict_kernel, [(9, 8, 256), (16, 8, 512), (16, 8, 512)], [(128, 512)], "restrict"
+        restrict_kernel, [(9, 8, 256), (16, 8, 512), (16, 8, 512)], [(128, 512)], "restrict", 1
     )(right_side, point_counts)
     packed = jnp.concatenate([move(packed, "gx", 1), packed, move(packed, "gx", -1)], axis=0)
     side_low, side_high = move(second, "gy", 1), move(first, "gy", -1)
+    side, side_low, side_high = lax.optimization_barrier((right_side, side_low, side_high))
+    side_left, side_right = move(side[8:16], "gx", 1), move(side[0:8], "gx", -1)
     coarse, inverse, center = call(
         coarse_kernel,
         [(8, 8, 256), (4, 4, 512), (4, 4, 512)],
         [(26, 2, 40, 128)] * 3 + [(6, 2, 40, 128)],
         "coarse",
+        COARSE_US,
     )(packed, move(packed, "gy", 1), move(packed, "gy", -1))
+    coarse, side_left, side_right = lax.optimization_barrier((coarse, side_left, side_right))
     coarse_low, coarse_high = move(coarse, "gy", 1), move(coarse, "gy", -1)
-    side = jnp.concatenate([side_low, right_side, side_high], axis=1)
-    side_left, side_right = move(side[8:16], "gx", 1), move(side[0:8], "gx", -1)
     wide = jnp.concatenate([coarse_low, coarse, coarse_high], axis=1)
+    wide, side_left, side_right = lax.optimization_barrier((wide, side_left, side_right))
     coarse_left, coarse_right = move(wide[3:8], "gx", 1), move(wide[0:5], "gx", -1)
+    corner_low = move(jnp.concatenate([side_left[:, 8:16], side_right[:, 8:16]], axis=0), "gy", 1)
+    corner_high = move(jnp.concatenate([side_left[:, 0:8], side_right[:, 0:8]], axis=0), "gy", -1)
     field = (16, 4, 48, 128)
-    inner = call(inner_kernel, [field, field, field, (2, 4, 48, 128)], [], "inner")(
+    inner = call(inner_kernel, [field, field, field, (2, 4, 48, 128)], [], "inner", INNER_US)(
         right_side, side_low, side_high, coarse, coarse_low, coarse_high, inverse
     )
     field = (36, 4, 48, 128)
     return call(
-        outer_kernel, [(16, 16, 512)] * 2, [field, field, field, (4, 4, 48, 128)], "outer"
-    )(right_side, side_left, side_right, coarse_left, coarse_right, inverse, center, *inner)
+        outer_kernel, [(16, 16, 512)] * 2, [field, field, field, (4, 4, 48, 128)], "outer", 6
+    )(
+        right_side, side_left, side_right, corner_low, corner_high, coarse_left, coarse_right, inverse, center, *inner
+    )
 
 
 def solution(mesh):

time: 51.2 us -> 53.4 us (1.043)
  waiting for transfers between devices: 14.1 us -> 17.8 us
  starting transfers between devices: 23.3 us -> 21.3 us
    ppermute x12 -> x14, waiting for transfers between devices: 14.1 us -> 17.8 us  [move(): lax.ppermute(value, axis, [(i, (i + step) % count) for i in range(count)])]
    ppermute x12 -> x14, starting transfers between devices: 23.3 us -> 21.3 us  [move(): lax.ppermute(value, axis, [(i, (i + step) % count) for i in range(count)])]
    unnamed x12 -> x8, local copies, waits for them, and re-layouts: 1.81 us -> 1.74 us
  transfers between devices with their start and end apart: 12 -> 14, of which waited for: 6 -> 8; matrix products, arithmetic and copies ran while one was open for 0% -> 0% of each run, Pallas kernels for 5% -> 8%
where the time goes in v3:
time: 53.4 us; the launch traced here: 53.2 us
  starting transfers between devices  21.3 us (40%)
  waiting for transfers between devices  17.8 us (33%)
  Pallas kernels  11.4 us (21%)
  local copies, waits for them, and re-layouts  1.84 us (3%)
  between operations  0.76 us (1%)
    ppermute x14, starting transfers between devices, move(): lax.ppermute(value, axis, [(i, (i + step) % count) for i in range(count)])  21.3 us
    ppermute x14, waiting for transfers between devices, move(): lax.ppermute(value, axis, [(i, (i + step) % count) for i in range(count)])  17.8 us
    pallas_call x1, Pallas kernels, shards(): call(outer_kernel, [(16, 16, 512)] * 2, [field, field, field, (4, 4, 48,...  6.32 us
    pallas_call x1, Pallas kernels, shards(): call(inner_kernel, [field, field, field, (2, 4, 48, 128)], [], 'inner', I...  2.85 us
    unnamed x8, local copies, waits for them, and re-layouts  1.74 us
    pallas_call x1, Pallas kernels, shards(): call(coarse_kernel, [(8, 8, 256), (4, 4, 512), (4, 4, 512)], [(26, 2, 40,...  1.62 us
  transfers between devices with their start and end apart: 14, of which 8 were waited for; matrix products, arithmetic and copies ran while one was open for 0% of the time, Pallas kernels for 8%

profile of v3, /device:TPU:0, one launch (start us, length us, event | category | flops | bytes accessed | tf_op | source)
XLA Modules:
  0.0 53.2 jit_solution(11485184647179888579)
XLA Ops:
  0.6 1.0 %copy-done = f32[16,16,512]{2,1,0:T(8,128)S(1)} copy-done((f32[16,16,512]{2,1,0:T(8,128)S(1)}, f32[16,16,512]{2,1,0:T(8,128)}, u32[]{:S(2)}) %copy-start) | copy-done | bytes 524312
  1.7 0.7 %copy-done.2 = s32[2,2,64]{2,1,0:T(2,128)S(1)} copy-done((s32[2,2,64]{2,1,0:T(2,128)S(1)}, s32[2,2,64]{2,1,0:T(2,128)}, u32[]{:S(2)}) %copy-start.2) | copy-done | bytes 1048
  2.4 0.6 %restrict.1 = (f32[9,8,256]{2,1,0:T(8,128)S(1)}, f32[16,8,512]{2,1,0:T(8,128)S(1)}, f32[16,8,512]{2,1,0:T(8,128)S(1)}) custom-call(f32[16,16,512]{2,1,0:T(8,128)S(1)} %copy-done, s32[2,2,64]{2,1,0:T(2,128)S(1)} %copy-done.2), custom_call_target="tpu_custom_call" | custom-call | flops 1000000000 | bytes 3690000 | tf_op jit(solution)/shard_map/restrict/pallas_call | solution.py:288
  3.0 1.6 %collective-permute-start = (f32[9,8,256]{2,1,0:T(8,128)S(1)}, f32[9,8,256]{2,1,0:T(8,128)S(1)}, u32[]{:S(2)}, u32[]{:S(2)}) collective-permute-start(f32[9,8,256]{2,1,0:T(8,128)S(1)} %get-tuple-element.21), channel_id=1, source_target_pairs={{0,8},{8,16},{16,24},{24,32},{32,40},{40,48},{48,56},{56,64},{64,7... | collective-permute-start | bytes 221192 | tf_op jit(solution)/shard_map/ppermute | solution.py:286
  4.6 3.8 %collective-permute-start.1 = (f32[9,8,256]{2,1,0:T(8,128)S(1)}, f32[9,8,256]{2,1,0:T(8,128)S(1)}, u32[]{:S(2)}, u32[]{:S(2)}) collective-permute-start(f32[9,8,256]{2,1,0:T(8,128)S(1)} %get-tuple-element.21), channel_id=1, source_target_pairs={{0,120},{8,0},{16,8},{24,16},{32,24},{40,32},{48,40},{56,48},{64,5... | collective-permute-start | bytes 221192 | tf_op jit(solution)/shard_map/ppermute | solution.py:286
  8.4 3.2 %collective-permute-start.5 = (f32[16,8,512]{2,1,0:T(8,128)S(1)}, f32[16,8,512]{2,1,0:T(8,128)S(1)}, u32[]{:S(2)}, u32[]{:S(2)}) collective-permute-start(f32[16,8,512]{2,1,0:T(8,128)S(1)} %get-tuple-element.24), channel_id=1, source_target_pairs={{0,7},{1,0},{2,1},{3,2},{4,3},{5,4},{6,5},{7,6},{8,15},{9,8},{10,9... | collective-permute-start | bytes 786440 | tf_op jit(solution)/shard_map/ppermute | solution.py:286
  11.7 1.7 %collective-permute-start.3 = (f32[27,8,256]{2,1,0:T(8,128)S(1)}, f32[27,8,256]{2,1,0:T(8,128)S(1)}, u32[]{:S(2)}, u32[]{:S(2)}) collective-permute-start(f32[27,8,256]{2,1,0:T(8,128)S(1)} %constant_dynamic-update-slice_fusion.mid_ref), channel_id=1, source_target_pairs={{0,7},{1,0},{2,1},{3,2},{4,3},{5,4},{6,5},{7,6},{8,15},{9,8},{10,9... | collective-permute-start | bytes 663560 | tf_op jit(solution)/shard_map/ppermute | solution.py:286
  13.4 2.3 %collective-permute-done.4.side_low = f32[16,8,512]{2,1,0:T(8,128)S(1)} collective-permute-done((f32[16,8,512]{2,1,0:T(8,128)S(1)}, f32[16,8,512]{2,1,0:T(8,128)S(1)}, u32[]{:S(2)}, u32[]{:S(2)}) %collective-permute-start.4) | collective-permute-done | bytes 262176 | tf_op jit(solution)/shard_map/ppermute | solution.py:286
  15.7 2.8 %collective-permute-start.7 = (f32[8,16,512]{2,1,0:T(8,128)S(1)}, f32[8,16,512]{2,1,0:T(8,128)S(1)}, u32[]{:S(2)}, u32[]{:S(2)}) collective-permute-start(f32[8,16,512]{2,1,0:T(8,128)S(1)} %get-tuple-element.40), channel_id=1, source_target_pairs={{0,120},{8,0},{16,8},{24,16},{32,24},{40,32},{48,40},{56,48},{64,5... | collective-permute-start | bytes 786440 | tf_op jit(solution)/shard_map/ppermute | solution.py:286
  18.6 1.3 %collective-permute-done.2.low_ref = f32[27,8,256]{2,1,0:T(8,128)S(1)} collective-permute-done((f32[27,8,256]{2,1,0:T(8,128)S(1)}, f32[27,8,256]{2,1,0:T(8,128)S(1)}, u32[]{:S(2)}, u32[]{:S(2)}) %collective-permute-start.2) | collective-permute-done | bytes 221216 | tf_op jit(solution)/shard_map/ppermute | solution.py:286
  19.9 1.6 %coarse.1 = (f32[8,8,256]{2,1,0:T(8,128)S(1)}, f32[4,4,512]{2,1,0:T(4,128)S(1)}, f32[4,4,512]{2,1,0:T(4,128)S(1)}) custom-call(f32[27,8,256]{2,1,0:T(8,128)S(1)} %constant_dynamic-update-slice_fusion.mid_ref, f32[27,8,256]{2,1,0:T(8,128)S(1)} %collective-permute-done.2.low_ref, f32[27,8,256]{2,1,0:T(8,128)S(1)} %collective-permute-done.3.high_ref), custom_call_target="tpu_custom_call" | custom-call | flops 20000000000 | bytes 73800000 | tf_op jit(solution)/shard_map/coarse/pallas_call | solution.py:295
  21.6 3.1 %collective-permute-done.7.side_right = f32[8,16,512]{2,1,0:T(8,128)S(1)} collective-permute-done((f32[8,16,512]{2,1,0:T(8,128)S(1)}, f32[8,16,512]{2,1,0:T(8,128)S(1)}, u32[]{:S(2)}, u32[]{:S(2)}) %collective-permute-start.7) | collective-permute-done | bytes 262176 | tf_op jit(solution)/shard_map/ppermute | solution.py:286
  24.7 5.0 %collective-permute-done.6.side_left = f32[8,16,512]{2,1,0:T(8,128)S(1)} collective-permute-done((f32[8,16,512]{2,1,0:T(8,128)S(1)}, f32[8,16,512]{2,1,0:T(8,128)S(1)}, u32[]{:S(2)}, u32[]{:S(2)}) %collective-permute-start.6) | collective-permute-done | bytes 262176 | tf_op jit(solution)/shard_map/ppermute | solution.py:286
  29.6 3.1 %collective-permute-start.9 = (f32[8,8,256]{2,1,0:T(8,128)S(1)}, f32[8,8,256]{2,1,0:T(8,128)S(1)}, u32[]{:S(2)}, u32[]{:S(2)}) collective-permute-start(f32[8,8,256]{2,1,0:T(8,128)S(1)} %get-tuple-element.26.c_ref), channel_id=1, source_target_pairs={{0,7},{1,0},{2,1},{3,2},{4,3},{5,4},{6,5},{7,6},{8,15},{9,8},{10,9... | collective-permute-start | bytes 196616 | tf_op jit(solution)/shard_map/ppermute | solution.py:286
  32.7 1.9 %collective-permute-done.9.c_high = f32[8,8,256]{2,1,0:T(8,128)S(1)} collective-permute-done((f32[8,8,256]{2,1,0:T(8,128)S(1)}, f32[8,8,256]{2,1,0:T(8,128)S(1)}, u32[]{:S(2)}, u32[]{:S(2)}) %collective-permute-start.9) | collective-permute-done | bytes 65568 | tf_op jit(solution)/shard_map/ppermute | solution.py:286
  34.6 3.0 %collective-permute-done.8.c_low = f32[8,8,256]{2,1,0:T(8,128)S(1)} collective-permute-done((f32[8,8,256]{2,1,0:T(8,128)S(1)}, f32[8,8,256]{2,1,0:T(8,128)S(1)}, u32[]{:S(2)}, u32[]{:S(2)}) %collective-permute-start.8) | collective-permute-done | bytes 65568 | tf_op jit(solution)/shard_map/ppermute | solution.py:286
  37.7 0.3 collective-permute-start.13
  38.0 1.8 %collective-permute-start.12 = (f32[5,24,256]{2,1,0:T(8,128)S(1)}, f32[5,24,256]{2,1,0:T(8,128)S(1)}, u32[]{:S(2)}, u32[]{:S(2)}) collective-permute-start(f32[5,24,256]{2,1,0:T(8,128)S(1)} %get-tuple-element.47), channel_id=1, source_target_pairs={{0,8},{8,16},{16,24},{24,32},{32,40},{40,48},{48,56},{56,64},{64,7... | collective-permute-start | bytes 368648 | tf_op jit(solution)/shard_map/ppermute | solution.py:286
  39.8 0.0 collective-permute-start.10
  39.9 2.9 %collective-permute-start.11 = (f32[16,8,512]{2,1,0:T(8,128)S(1)}, f32[16,8,512]{2,1,0:T(8,128)S(1)}, u32[]{:S(2)}, u32[]{:S(2)}) collective-permute-start(f32[16,8,512]{2,1,0:T(8,128)S(1)} %pad_maximum_fusion.1), channel_id=1, source_target_pairs={{0,7},{1,0},{2,1},{3,2},{4,3},{5,4},{6,5},{7,6},{8,15},{9,8},{10,9... | collective-permute-start | bytes 786440 | tf_op jit(solution)/shard_map/ppermute | solution.py:286
  42.8 2.9 %inner.1 = (f32[16,4,48,128]{3,2,1,0:T(8,128)S(1)}, f32[16,4,48,128]{3,2,1,0:T(8,128)S(1)}, f32[16,4,48,128]{3,2,1,0:T(8,128)S(1)}, f32[2,4,48,128]{3,2,1,0:T(8,128)S(1)}) custom-call(f32[16,16,512]{2,1,0:T(8,128)S(1)} %copy-done.1, f32[16,8,512]{2,1,0:T(8,128)S(1)} %collective-permute-done.4.side_low, f32[16,8,512]{2,1,0:T(8,128)S(1)} %collective-permute-done.5.side_high, ...), custom_call_target="tpu_custom_call" | custom-call | flops 20000000000 | bytes 73800000 | tf_op jit(solution)/shard_map/inner/pallas_call | solution.py:310
  45.7 0.5 collective-permute-done.12.c_low
  46.2 0.7 %collective-permute-done.10.corner_low = f32[16,8,512]{2,1,0:T(8,128)S(1)} collective-permute-done((f32[16,8,512]{2,1,0:T(8,128)S(1)}, f32[16,8,512]{2,1,0:T(8,128)S(1)}, u32[]{:S(2)}, u32[]{:S(2)}) %collective-permute-start.10) | collective-permute-done | bytes 262176 | tf_op jit(solution)/shard_map/ppermute | solution.py:286
  46.8 6.3 %outer.1 = (f32[16,16,512]{2,1,0:T(8,128)}, f32[16,16,512]{2,1,0:T(8,128)}) custom-call(f32[16,16,512]{2,1,0:T(8,128)S(1)} %copy-done.1, f32[8,16,512]{2,1,0:T(8,128)S(1)} %collective-permute-done.6.side_left, f32[8,16,512]{2,1,0:T(8,128)S(1)} %collective-permute-done.7.side_right, f32[16,8,512]{2,1,0:T(8,128)S(1)} %collective-permute-done.10.corner_low, ...), custom_call_target="tpu_custom_call" | custom-call | flops 6000000000 | bytes 22140000 | tf_op jit(solution)/shard_map/outer/pallas_call | solution.py:314
  (23 shorter events, 0.2 us)
Async XLA Ops:
  0.6 1.0 %copy-start = (f32[16,16,512]{2,1,0:T(8,128)S(1)}, f32[16,16,512]{2,1,0:T(8,128)}, u32[]{:S(2)}) copy-start(f32[16,16,512]{2,1,0:T(8,128)} %side_ref.5) | copy-start | bytes 1572868
  1.7 0.7 %copy-start.2 = (s32[2,2,64]{2,1,0:T(2,128)S(1)}, s32[2,2,64]{2,1,0:T(2,128)}, u32[]{:S(2)}) copy-start(s32[2,2,64]{2,1,0:T(2,128)} %counts_ref.1) | copy-start | bytes 3076
  3.0 8.6 %collective-permute-start = (f32[9,8,256]{2,1,0:T(8,128)S(1)}, f32[9,8,256]{2,1,0:T(8,128)S(1)}, u32[]{:S(2)}, u32[]{:S(2)}) collective-permute-start(f32[9,8,256]{2,1,0:T(8,128)S(1)} %get-tuple-element.21), channel_id=1, source_target_pairs={{0,8},{8,16},{16,24},{24,32},{32,40},{40,48},{48,56},{56,64},{64,7... | collective-permute-start | bytes 221192 | tf_op jit(solution)/shard_map/ppermute | solution.py:286
  4.6 7.0 %collective-permute-start.1 = (f32[9,8,256]{2,1,0:T(8,128)S(1)}, f32[9,8,256]{2,1,0:T(8,128)S(1)}, u32[]{:S(2)}, u32[]{:S(2)}) collective-permute-start(f32[9,8,256]{2,1,0:T(8,128)S(1)} %get-tuple-element.21), channel_id=1, source_target_pairs={{0,120},{8,0},{16,8},{24,16},{32,24},{40,32},{48,40},{56,48},{64,5... | collective-permute-start | bytes 221192 | tf_op jit(solution)/shard_map/ppermute | solution.py:286
  8.4 7.2 %collective-permute-start.4 = (f32[16,8,512]{2,1,0:T(8,128)S(1)}, f32[16,8,512]{2,1,0:T(8,128)S(1)}, u32[]{:S(2)}, u32[]{:S(2)}) collective-permute-start(f32[16,8,512]{2,1,0:T(8,128)S(1)} %get-tuple-element.23), channel_id=1, source_target_pairs={{0,1},{1,2},{2,3},{3,4},{4,5},{5,6},{6,7},{7,0},{8,9},{9,10},{10,1... | collective-permute-start | bytes 786440 | tf_op jit(solution)/shard_map/ppermute | solution.py:286
  8.4 7.2 %collective-permute-start.5 = (f32[16,8,512]{2,1,0:T(8,128)S(1)}, f32[16,8,512]{2,1,0:T(8,128)S(1)}, u32[]{:S(2)}, u32[]{:S(2)}) collective-permute-start(f32[16,8,512]{2,1,0:T(8,128)S(1)} %get-tuple-element.24), channel_id=1, source_target_pairs={{0,7},{1,0},{2,1},{3,2},{4,3},{5,4},{6,5},{7,6},{8,15},{9,8},{10,9... | collective-permute-start | bytes 786440 | tf_op jit(solution)/shard_map/ppermute | solution.py:286
  11.7 6.9 %collective-permute-start.3 = (f32[27,8,256]{2,1,0:T(8,128)S(1)}, f32[27,8,256]{2,1,0:T(8,128)S(1)}, u32[]{:S(2)}, u32[]{:S(2)}) collective-permute-start(f32[27,8,256]{2,1,0:T(8,128)S(1)} %constant_dynamic-update-slice_fusion.mid_ref), channel_id=1, source_target_pairs={{0,7},{1,0},{2,1},{3,2},{4,3},{5,4},{6,5},{7,6},{8,15},{9,8},{10,9... | collective-permute-start | bytes 663560 | tf_op jit(solution)/shard_map/ppermute | solution.py:286
  13.3 6.6 %collective-permute-start.2 = (f32[27,8,256]{2,1,0:T(8,128)S(1)}, f32[27,8,256]{2,1,0:T(8,128)S(1)}, u32[]{:S(2)}, u32[]{:S(2)}) collective-permute-start(f32[27,8,256]{2,1,0:T(8,128)S(1)} %constant_dynamic-update-slice_fusion.mid_ref), channel_id=1, source_target_pairs={{0,1},{1,2},{2,3},{3,4},{4,5},{5,6},{6,7},{7,0},{8,9},{9,10},{10,1... | collective-permute-start | bytes 663560 | tf_op jit(solution)/shard_map/ppermute | solution.py:286
  15.7 8.9 %collective-permute-start.7 = (f32[8,16,512]{2,1,0:T(8,128)S(1)}, f32[8,16,512]{2,1,0:T(8,128)S(1)}, u32[]{:S(2)}, u32[]{:S(2)}) collective-permute-start(f32[8,16,512]{2,1,0:T(8,128)S(1)} %get-tuple-element.40), channel_id=1, source_target_pairs={{0,120},{8,0},{16,8},{24,16},{32,24},{40,32},{48,40},{56,48},{64,5... | collective-permute-start | bytes 786440 | tf_op jit(solution)/shard_map/ppermute | solution.py:286
  18.6 11.0 %collective-permute-start.6 = (f32[8,16,512]{2,1,0:T(8,128)S(1)}, f32[8,16,512]{2,1,0:T(8,128)S(1)}, u32[]{:S(2)}, u32[]{:S(2)}) collective-permute-start(f32[8,16,512]{2,1,0:T(8,128)S(1)} %get-tuple-element.41), channel_id=1, source_target_pairs={{0,8},{8,16},{16,24},{24,32},{32,40},{40,48},{48,56},{56,64},{64,7... | collective-permute-start | bytes 786440 | tf_op jit(solution)/shard_map/ppermute | solution.py:286
  21.5 21.3 %copy-start.1 = (f32[16,16,512]{2,1,0:T(8,128)S(1)}, f32[16,16,512]{2,1,0:T(8,128)}, u32[]{:S(2)}) copy-start(f32[16,16,512]{2,1,0:T(8,128)} %side_ref.5) | copy-start | bytes 1572868
  29.6 5.0 %collective-permute-start.9 = (f32[8,8,256]{2,1,0:T(8,128)S(1)}, f32[8,8,256]{2,1,0:T(8,128)S(1)}, u32[]{:S(2)}, u32[]{:S(2)}) collective-permute-start(f32[8,8,256]{2,1,0:T(8,128)S(1)} %get-tuple-element.26.c_ref), channel_id=1, source_target_pairs={{0,7},{1,0},{2,1},{3,2},{4,3},{5,4},{6,5},{7,6},{8,15},{9,8},{10,9... | collective-permute-start | bytes 196616 | tf_op jit(solution)/shard_map/ppermute | solution.py:286
  32.7 4.9 %collective-permute-start.8 = (f32[8,8,256]{2,1,0:T(8,128)S(1)}, f32[8,8,256]{2,1,0:T(8,128)S(1)}, u32[]{:S(2)}, u32[]{:S(2)}) collective-permute-start(f32[8,8,256]{2,1,0:T(8,128)S(1)} %get-tuple-element.26.c_ref), channel_id=1, source_target_pairs={{0,1},{1,2},{2,3},{3,4},{4,5},{5,6},{6,7},{7,0},{8,9},{9,10},{10,1... | collective-permute-start | bytes 196616 | tf_op jit(solution)/shard_map/ppermute | solution.py:286
  37.7 8.0 %collective-permute-start.13 = (f32[5,24,256]{2,1,0:T(8,128)S(1)}, f32[5,24,256]{2,1,0:T(8,128)S(1)}, u32[]{:S(2)}, u32[]{:S(2)}) collective-permute-start(f32[5,24,256]{2,1,0:T(8,128)S(1)} %get-tuple-element.46), channel_id=1, source_target_pairs={{0,120},{8,0},{16,8},{24,16},{32,24},{40,32},{48,40},{56,48},{64,5... | collective-permute-start | bytes 368648 | tf_op jit(solution)/shard_map/ppermute | solution.py:286
  38.0 8.2 %collective-permute-start.12 = (f32[5,24,256]{2,1,0:T(8,128)S(1)}, f32[5,24,256]{2,1,0:T(8,128)S(1)}, u32[]{:S(2)}, u32[]{:S(2)}) collective-permute-start(f32[5,24,256]{2,1,0:T(8,128)S(1)} %get-tuple-element.47), channel_id=1, source_target_pairs={{0,8},{8,16},{16,24},{24,32},{32,40},{40,48},{48,56},{56,64},{64,7... | collective-permute-start | bytes 368648 | tf_op jit(solution)/shard_map/ppermute | solution.py:286
  39.8 7.0 %collective-permute-start.10 = (f32[16,8,512]{2,1,0:T(8,128)S(1)}, f32[16,8,512]{2,1,0:T(8,128)S(1)}, u32[]{:S(2)}, u32[]{:S(2)}) collective-permute-start(f32[16,8,512]{2,1,0:T(8,128)S(1)} %pad_maximum_fusion), channel_id=1, source_target_pairs={{0,1},{1,2},{2,3},{3,4},{4,5},{5,6},{6,7},{7,0},{8,9},{9,10},{10,1... | collective-permute-start | bytes 786440 | tf_op jit(solution)/shard_map/ppermute | solution.py:286
  39.9 7.0 %collective-permute-start.11 = (f32[16,8,512]{2,1,0:T(8,128)S(1)}, f32[16,8,512]{2,1,0:T(8,128)S(1)}, u32[]{:S(2)}, u32[]{:S(2)}) collective-permute-start(f32[16,8,512]{2,1,0:T(8,128)S(1)} %pad_maximum_fusion.1), channel_id=1, source_target_pairs={{0,7},{1,0},{2,1},{3,2},{4,3},{5,4},{6,5},{7,6},{8,15},{9,8},{10,9... | collective-permute-start | bytes 786440 | tf_op jit(solution)/shard_map/ppermute | solution.py:286

commit v4 on v3

--- a/solution.py
+++ b/solution.py
@@ -73,7 +73,7 @@
     return lax.axis_index("gx"), lax.axis_index("gy"), lax.axis_size("gx"), lax.axis_size("gy")
 
 
-def restrict_kernel(side_ref, counts_ref, out_ref, first_ref, second_ref, tmp):
+def restrict_kernel(side_ref, counts_ref, out_ref, first_ref, last_ref, tmp):
     for x in range(8):
         tmp[16 * x : 16 * x + 16, :] = side_ref[2 * x] + side_ref[2 * x + 1]
     halves = pairing(512, 256, 2, 0.5)
@@ -83,8 +83,8 @@
         out_ref[x] = coarse[8 * x : 8 * x + 8, :]
     out_ref[8] = jnp.zeros((8, 256), F32)
     out_ref[8, 0:4, 0:64] = counts_ref[...].reshape(4, 64).astype(F32)
-    first_ref[...] = side_ref[:, 0:8, :]
-    second_ref[...] = side_ref[:, 8:16, :]
+    first_ref[...] = side_ref[0:8]
+    last_ref[...] = side_ref[8:16]
 
 
 def coarse_kernel(mid_ref, low_ref, high_ref, c_ref, inv_ref, center_ref, even, odd, drive, coupling):
@@ -281,31 +281,39 @@
 
 
 def shards(right_side, point_counts):
-    def move(value, axis, step):
-        count = lax.axis_size(axis)
-        return lax.ppermute(value, axis, [(i, (i + step) % count) for i in range(count)])
-
-    packed, first, second = call(
-        restrict_kernel, [(9, 8, 256), (16, 8, 512), (16, 8, 512)], [(128, 512)], "restrict", 1
+    def exchange(axis, to_low, to_high):
+        count, even = lax.axis_size(axis), lax.axis_index(axis) % 2 == 0
+        outer = [(i, (i + (-1 if i % 2 == 0 else 1)) % count) for i in range(count)]
+        inner = [(i, i + (1 if i % 2 == 0 else -1)) for i in range(count)]
+        same = to_low is to_high
+        first = lax.ppermute(to_low if same else jnp.where(even, to_low, to_high), axis, outer)
+        second = lax.ppermute(to_low if same else jnp.where(even, to_high, to_low), axis, inner)
+        return jnp.where(even, first, second), jnp.where(even, second, first)
+
+    packed, first, last = call(
+        restrict_kernel, [(9, 8, 256), (8, 16, 512), (8, 16, 512)], [(128, 512)], "restrict", 1
     )(right_side, point_counts)
-    packed = jnp.concatenate([move(packed, "gx", 1), packed, move(packed, "gx", -1)], axis=0)
-    side_low, side_high = move(second, "gy", 1), move(first, "gy", -1)
-    side, side_low, side_high = lax.optimization_barrier((right_side, side_low, side_high))
-    side_left, side_right = move(side[8:16], "gx", 1), move(side[0:8], "gx", -1)
+    left, right = exchange("gx", packed, packed)
+    packed = jnp.concatenate([left, packed, right], axis=0)
+    side_left, side_right = exchange("gx", first, last)
+    packed, own = lax.optimization_barrier((packed, right_side))
+    side_low, side_high = exchange("gy", own[:, 0:8], own[:, 8:16])
     coarse, inverse, center = call(
         coarse_kernel,
         [(8, 8, 256), (4, 4, 512), (4, 4, 512)],
         [(26, 2, 40, 128)] * 3 + [(6, 2, 40, 128)],
         "coarse",
         COARSE_US,
-    )(packed, move(packed, "gy", 1), move(packed, "gy", -1))
+    )(packed, *exchange("gy", packed, packed))
     coarse, side_left, side_right = lax.optimization_barrier((coarse, side_left, side_right))
-    coarse_low, coarse_high = move(coarse, "gy", 1), move(coarse, "gy", -1)
+    coarse_low, coarse_high = exchange("gy", coarse, coarse)
+    corner_low, corner_high = exchange(
+        "gy",
+        jnp.concatenate([side_left[:, 0:8], side_right[:, 0:8]], axis=0),
+        jnp.concatenate([side_left[:, 8:16], side_right[:, 8:16]], axis=0),
+    )
     wide = jnp.concatenate([coarse_low, coarse, coarse_high], axis=1)
-    wide, side_left, side_right = lax.optimization_barrier((wide, side_left, side_right))
-    coarse_left, coarse_right = move(wide[3:8], "gx", 1), move(wide[0:5], "gx", -1)
-    corner_low = move(jnp.concatenate([side_left[:, 8:16], side_right[:, 8:16]], axis=0), "gy", 1)
-    corner_high = move(jnp.concatenate([side_left[:, 0:8], side_right[:, 0:8]], axis=0), "gy", -1)
+    coarse_left, coarse_right = exchange("gx", wide[0:5], wide[3:8])
     field = (16, 4, 48, 128)
     inner = call(inner_kernel, [field, field, field, (2, 4, 48, 128)], [], "inner", INNER_US)(
         right_side, side_low, side_high, coarse, coarse_low, coarse_high, inverse

time: 53.4 us -> 43.2 us (0.81)
  waiting for transfers between devices: 17.8 us -> 6.04 us
  starting transfers between devices: 21.3 us -> 23 us
    ppermute x14, waiting for transfers between devices: 17.8 us -> 6.04 us  [the longest x7 5.96 us: exchange(): lax.ppermute(to_low if same else jnp.where(even, to_low, to_high), axis,...]
    ppermute x14, starting transfers between devices: 21.3 us -> 23 us  [the longest x7 20.8 us: exchange(): lax.ppermute(to_low if same else jnp.where(even, to_low, to_high), axis,...]
    unnamed x8 -> x6, local copies, waits for them, and re-layouts: 1.74 us -> 1.72 us
  transfers between devices with their start and end apart: 14 -> 14, of which waited for: 8 -> 5; matrix products, arithmetic and copies ran while one was open for 0% -> 1% of each run, Pallas kernels for 8% -> 10%
where the time goes in v4:
time: 43.2 us; the launch traced here: 43 us
  starting transfers between devices  23 us (53%)
  Pallas kernels  10.9 us (25%)
  waiting for transfers between devices  6.04 us (14%)
  local copies, waits for them, and re-layouts  1.76 us (4%)
  between operations  0.87 us (2%)
    ppermute x7, starting transfers between devices, exchange(): lax.ppermute(to_low if same else jnp.where(even, to_low, to_high), axis,...  20.8 us
    pallas_call x1, Pallas kernels, shards(): call(outer_kernel, [(16, 16, 512)] * 2, [field, field, field, (4, 4, 48,...  6.12 us
    ppermute x7, waiting for transfers between devices, exchange(): lax.ppermute(to_low if same else jnp.where(even, to_low, to_high), axis,...  5.96 us
    pallas_call x1, Pallas kernels, shards(): call(inner_kernel, [field, field, field, (2, 4, 48, 128)], [], 'inner', I...  2.58 us
    ppermute x7, starting transfers between devices, exchange(): lax.ppermute(to_low if same else jnp.where(even, to_high, to_low), axis,...  2.17 us
    unnamed x6, local copies, waits for them, and re-layouts  1.72 us
    pallas_call x1, Pallas kernels, shards(): call(coarse_kernel, [(8, 8, 256), (4, 4, 512), (4, 4, 512)], [(26, 2, 40,...  1.61 us
  transfers between devices with their start and end apart: 14, of which 5 were waited for; matrix products, arithmetic and copies ran while one was open for 1% of the time, Pallas kernels for 10%

profile of v4, /device:TPU:0, one launch (start us, length us, event | category | flops | bytes accessed | tf_op | source)
XLA Modules:
  0.0 43.0 jit_solution(11378109147392875021)
XLA Ops:
  0.6 1.0 %copy-done = f32[16,16,512]{2,1,0:T(8,128)S(1)} copy-done((f32[16,16,512]{2,1,0:T(8,128)S(1)}, f32[16,16,512]{2,1,0:T(8,128)}, u32[]{:S(2)}) %copy-start) | copy-done | bytes 524312
  1.7 0.7 %copy-done.2 = s32[2,2,64]{2,1,0:T(2,128)S(1)} copy-done((s32[2,2,64]{2,1,0:T(2,128)S(1)}, s32[2,2,64]{2,1,0:T(2,128)}, u32[]{:S(2)}) %copy-start.2) | copy-done | bytes 1048
  2.4 0.6 %restrict.1 = (f32[9,8,256]{2,1,0:T(8,128)S(1)}, f32[8,16,512]{2,1,0:T(8,128)S(1)}, f32[8,16,512]{2,1,0:T(8,128)S(1)}) custom-call(f32[16,16,512]{2,1,0:T(8,128)S(1)} %copy-done, s32[2,2,64]{2,1,0:T(2,128)S(1)} %copy-done.2), custom_call_target="tpu_custom_call" | custom-call | flops 1000000000 | bytes 3690000 | tf_op jit(solution)/shard_map/restrict/pallas_call | solution.py:293
  3.0 1.7 %collective-permute-start.1 = (f32[9,8,256]{2,1,0:T(8,128)S(1)}, f32[9,8,256]{2,1,0:T(8,128)S(1)}, u32[]{:S(2)}, u32[]{:S(2)}) collective-permute-start(f32[9,8,256]{2,1,0:T(8,128)S(1)} %get-tuple-element.17), channel_id=1, source_target_pairs={{0,8},{8,0},{16,24},{24,16},{32,40},{40,32},{48,56},{56,48},{64,72... | collective-permute-start | bytes 221192 | tf_op jit(solution)/shard_map/ppermute | solution.py:290
  4.7 4.5 %collective-permute-start = (f32[9,8,256]{2,1,0:T(8,128)S(1)}, f32[9,8,256]{2,1,0:T(8,128)S(1)}, u32[]{:S(2)}, u32[]{:S(2)}) collective-permute-start(f32[9,8,256]{2,1,0:T(8,128)S(1)} %get-tuple-element.17), channel_id=1, source_target_pairs={{0,120},{8,16},{16,8},{24,32},{32,24},{40,48},{48,40},{56,64},{64,... | collective-permute-start | bytes 221192 | tf_op jit(solution)/shard_map/ppermute | solution.py:289
  9.3 0.1 collective-permute-start.5
  9.3 1.2 %collective-permute-start.4 = (f32[8,16,512]{2,1,0:T(8,128)S(1)}, f32[8,16,512]{2,1,0:T(8,128)S(1)}, u32[]{:S(2)}, u32[]{:S(2)}) collective-permute-start(f32[8,16,512]{2,1,0:T(8,128)S(1)} %get-tuple-element.43), channel_id=1, source_target_pairs={{0,120},{8,16},{16,8},{24,32},{32,24},{40,48},{48,40},{56,64},{64,... | collective-permute-start | bytes 786440 | tf_op jit(solution)/shard_map/ppermute | solution.py:289
  10.5 1.8 %collective-permute-done = f32[9,8,256]{2,1,0:T(8,128)S(1)} collective-permute-done((f32[9,8,256]{2,1,0:T(8,128)S(1)}, f32[9,8,256]{2,1,0:T(8,128)S(1)}, u32[]{:S(2)}, u32[]{:S(2)}) %collective-permute-start) | collective-permute-done | bytes 73760 | tf_op jit(solution)/shard_map/ppermute | solution.py:289
  12.4 0.1 collective-permute-start.3
  12.5 4.1 %collective-permute-start.2 = (f32[27,8,256]{2,1,0:T(8,128)S(1)}, f32[27,8,256]{2,1,0:T(8,128)S(1)}, u32[]{:S(2)}, u32[]{:S(2)}) collective-permute-start(f32[27,8,256]{2,1,0:T(8,128)S(1)} %pad_maximum_fusion.2.mid_ref), channel_id=1, source_target_pairs={{0,7},{1,2},{2,1},{3,4},{4,3},{5,6},{6,5},{7,0},{8,15},{9,10},{10,... | collective-permute-start | bytes 663560 | tf_op jit(solution)/shard_map/ppermute | solution.py:289
  16.7 0.1 collective-permute-start.13
  16.8 2.0 %collective-permute-start.12 = (f32[16,8,512]{2,1,0:T(8,128)S(1)}, f32[16,8,512]{2,1,0:T(8,128)S(1)}, u32[]{:S(2)}, u32[]{:S(2)}) collective-permute-start(f32[16,8,512]{2,1,0:T(8,128)S(1)} %get-tuple-element.35), channel_id=1, source_target_pairs={{0,7},{1,2},{2,1},{3,4},{4,3},{5,6},{6,5},{7,0},{8,15},{9,10},{10,... | collective-permute-start | bytes 786440 | tf_op jit(solution)/shard_map/ppermute | solution.py:289
  18.8 1.4 %collective-permute-done.4 = f32[8,16,512]{2,1,0:T(8,128)S(1)} collective-permute-done((f32[8,16,512]{2,1,0:T(8,128)S(1)}, f32[8,16,512]{2,1,0:T(8,128)S(1)}, u32[]{:S(2)}, u32[]{:S(2)}) %collective-permute-start.4) | collective-permute-done | bytes 262176 | tf_op jit(solution)/shard_map/ppermute | solution.py:289
  20.3 1.6 %coarse.1 = (f32[8,8,256]{2,1,0:T(8,128)S(1)}, f32[4,4,512]{2,1,0:T(4,128)S(1)}, f32[4,4,512]{2,1,0:T(4,128)S(1)}) custom-call(f32[27,8,256]{2,1,0:T(8,128)S(1)} %pad_maximum_fusion.2.mid_ref, f32[27,8,256]{2,1,0:T(8,128)S(1)} %get-tuple-element.45.low_ref, f32[27,8,256]{2,1,0:T(8,128)S(1)} %get-tuple-element.44.high_ref), custom_call_target="tpu_custom_call" | custom-call | flops 20000000000 | bytes 73800000 | tf_op jit(solution)/shard_map/coarse/pallas_call | solution.py:301
  22.0 0.1 collective-permute-start.9
  22.1 4.1 %collective-permute-start.8 = (f32[8,8,256]{2,1,0:T(8,128)S(1)}, f32[8,8,256]{2,1,0:T(8,128)S(1)}, u32[]{:S(2)}, u32[]{:S(2)}) collective-permute-start(f32[8,8,256]{2,1,0:T(8,128)S(1)} %get-tuple-element.24.c_ref), channel_id=1, source_target_pairs={{0,7},{1,2},{2,1},{3,4},{4,3},{5,6},{6,5},{7,0},{8,15},{9,10},{10,... | collective-permute-start | bytes 196616 | tf_op jit(solution)/shard_map/ppermute | solution.py:289
  26.3 0.1 collective-permute-start.7
  26.4 0.5 %collective-permute-start.6 = (f32[16,8,512]{2,1,0:T(8,128)S(1)}, f32[16,8,512]{2,1,0:T(8,128)S(1)}, u32[]{:S(2)}, u32[]{:S(2)}) collective-permute-start(f32[16,8,512]{2,1,0:T(8,128)S(1)} %get-tuple-element.39), channel_id=1, source_target_pairs={{0,7},{1,2},{2,1},{3,4},{4,3},{5,6},{6,5},{7,0},{8,15},{9,10},{10,... | collective-permute-start | bytes 786440 | tf_op jit(solution)/shard_map/ppermute | solution.py:289
  27.0 1.2 %collective-permute-done.8 = f32[8,8,256]{2,1,0:T(8,128)S(1)} collective-permute-done((f32[8,8,256]{2,1,0:T(8,128)S(1)}, f32[8,8,256]{2,1,0:T(8,128)S(1)}, u32[]{:S(2)}, u32[]{:S(2)}) %collective-permute-start.8) | collective-permute-done | bytes 65568 | tf_op jit(solution)/shard_map/ppermute | solution.py:289
  28.2 0.1 collective-permute-start.11
  28.3 4.3 %collective-permute-start.10 = (f32[5,24,256]{2,1,0:T(8,128)S(1)}, f32[5,24,256]{2,1,0:T(8,128)S(1)}, u32[]{:S(2)}, u32[]{:S(2)}) collective-permute-start(f32[5,24,256]{2,1,0:T(8,128)S(1)} %get-tuple-element.53), channel_id=1, source_target_pairs={{0,120},{8,16},{16,8},{24,32},{32,24},{40,48},{48,40},{56,64},{64,... | collective-permute-start | bytes 368648 | tf_op jit(solution)/shard_map/ppermute | solution.py:289
  32.6 2.6 %inner.1 = (f32[16,4,48,128]{3,2,1,0:T(8,128)S(1)}, f32[16,4,48,128]{3,2,1,0:T(8,128)S(1)}, f32[16,4,48,128]{3,2,1,0:T(8,128)S(1)}, f32[2,4,48,128]{3,2,1,0:T(8,128)S(1)}) custom-call(f32[16,16,512]{2,1,0:T(8,128)S(1)} %copy-done.1, f32[16,8,512]{2,1,0:T(8,128)S(1)} %get-tuple-element.33.side_low, f32[16,8,512]{2,1,0:T(8,128)S(1)} %get-tuple-element.32.side_high, ...), custom_call_target="tpu_custom_call" | custom-call | flops 20000000000 | bytes 73800000 | tf_op jit(solution)/shard_map/inner/pallas_call | solution.py:318
  35.2 1.5 %collective-permute-done.10 = f32[5,24,256]{2,1,0:T(8,128)S(1)} collective-permute-done((f32[5,24,256]{2,1,0:T(8,128)S(1)}, f32[5,24,256]{2,1,0:T(8,128)S(1)}, u32[]{:S(2)}, u32[]{:S(2)}) %collective-permute-start.10) | collective-permute-done | bytes 122912 | tf_op jit(solution)/shard_map/ppermute | solution.py:289
  36.9 6.1 %outer.1 = (f32[16,16,512]{2,1,0:T(8,128)}, f32[16,16,512]{2,1,0:T(8,128)}) custom-call(f32[16,16,512]{2,1,0:T(8,128)S(1)} %copy-done.1, f32[8,16,512]{2,1,0:T(8,128)S(1)} %get-tuple-element.22.side_left, f32[8,16,512]{2,1,0:T(8,128)S(1)} %get-tuple-element.23.side_right, f32[16,8,512]{2,1,0:T(8,128)S(1)} %get-tuple-element.37.corner_low, ...), custom_call_target="tpu_custom_call" | custom-call | flops 6000000000 | bytes 22140000 | tf_op jit(solution)/shard_map/outer/pallas_call | solution.py:322
  (28 shorter events, 0.5 us)
Async XLA Ops:
  0.6 1.0 %copy-start = (f32[16,16,512]{2,1,0:T(8,128)S(1)}, f32[16,16,512]{2,1,0:T(8,128)}, u32[]{:S(2)}) copy-start(f32[16,16,512]{2,1,0:T(8,128)} %side_ref.5) | copy-start | bytes 1572868
  1.7 0.7 %copy-start.2 = (s32[2,2,64]{2,1,0:T(2,128)S(1)}, s32[2,2,64]{2,1,0:T(2,128)}, u32[]{:S(2)}) copy-start(s32[2,2,64]{2,1,0:T(2,128)} %counts_ref.1) | copy-start | bytes 3076
  3.0 13.6 %copy-start.1 = (f32[16,16,512]{2,1,0:T(8,128)S(1)}, f32[16,16,512]{2,1,0:T(8,128)}, u32[]{:S(2)}) copy-start(f32[16,16,512]{2,1,0:T(8,128)} %side_ref.5) | copy-start | bytes 1572868
  3.0 7.5 %collective-permute-start.1 = (f32[9,8,256]{2,1,0:T(8,128)S(1)}, f32[9,8,256]{2,1,0:T(8,128)S(1)}, u32[]{:S(2)}, u32[]{:S(2)}) collective-permute-start(f32[9,8,256]{2,1,0:T(8,128)S(1)} %get-tuple-element.17), channel_id=1, source_target_pairs={{0,8},{8,0},{16,24},{24,16},{32,40},{40,32},{48,56},{56,48},{64,72... | collective-permute-start | bytes 221192 | tf_op jit(solution)/shard_map/ppermute | solution.py:290
  4.7 7.7 %collective-permute-start = (f32[9,8,256]{2,1,0:T(8,128)S(1)}, f32[9,8,256]{2,1,0:T(8,128)S(1)}, u32[]{:S(2)}, u32[]{:S(2)}) collective-permute-start(f32[9,8,256]{2,1,0:T(8,128)S(1)} %get-tuple-element.17), channel_id=1, source_target_pairs={{0,120},{8,16},{16,8},{24,32},{32,24},{40,48},{48,40},{56,64},{64,... | collective-permute-start | bytes 221192 | tf_op jit(solution)/shard_map/ppermute | solution.py:289
  9.3 7.6 %collective-permute-start.5 = (f32[8,16,512]{2,1,0:T(8,128)S(1)}, f32[8,16,512]{2,1,0:T(8,128)S(1)}, u32[]{:S(2)}, u32[]{:S(2)}) collective-permute-start(f32[8,16,512]{2,1,0:T(8,128)S(1)} %get-tuple-element.42), channel_id=1, source_target_pairs={{0,8},{8,0},{16,24},{24,16},{32,40},{40,32},{48,56},{56,48},{64,72... | collective-permute-start | bytes 786440 | tf_op jit(solution)/shard_map/ppermute | solution.py:290
  9.3 10.9 %collective-permute-start.4 = (f32[8,16,512]{2,1,0:T(8,128)S(1)}, f32[8,16,512]{2,1,0:T(8,128)S(1)}, u32[]{:S(2)}, u32[]{:S(2)}) collective-permute-start(f32[8,16,512]{2,1,0:T(8,128)S(1)} %get-tuple-element.43), channel_id=1, source_target_pairs={{0,120},{8,16},{16,8},{24,32},{32,24},{40,48},{48,40},{56,64},{64,... | collective-permute-start | bytes 786440 | tf_op jit(solution)/shard_map/ppermute | solution.py:289
  12.4 7.9 %collective-permute-start.3 = (f32[27,8,256]{2,1,0:T(8,128)S(1)}, f32[27,8,256]{2,1,0:T(8,128)S(1)}, u32[]{:S(2)}, u32[]{:S(2)}) collective-permute-start(f32[27,8,256]{2,1,0:T(8,128)S(1)} %pad_maximum_fusion.2.mid_ref), channel_id=1, source_target_pairs={{0,1},{1,0},{2,3},{3,2},{4,5},{5,4},{6,7},{7,6},{8,9},{9,8},{10,11... | collective-permute-start | bytes 663560 | tf_op jit(solution)/shard_map/ppermute | solution.py:290
  12.5 7.8 %collective-permute-start.2 = (f32[27,8,256]{2,1,0:T(8,128)S(1)}, f32[27,8,256]{2,1,0:T(8,128)S(1)}, u32[]{:S(2)}, u32[]{:S(2)}) collective-permute-start(f32[27,8,256]{2,1,0:T(8,128)S(1)} %pad_maximum_fusion.2.mid_ref), channel_id=1, source_target_pairs={{0,7},{1,2},{2,1},{3,4},{4,3},{5,6},{6,5},{7,0},{8,15},{9,10},{10,... | collective-permute-start | bytes 663560 | tf_op jit(solution)/shard_map/ppermute | solution.py:289
  16.7 9.7 %collective-permute-start.13 = (f32[16,8,512]{2,1,0:T(8,128)S(1)}, f32[16,8,512]{2,1,0:T(8,128)S(1)}, u32[]{:S(2)}, u32[]{:S(2)}) collective-permute-start(f32[16,8,512]{2,1,0:T(8,128)S(1)} %get-tuple-element.34), channel_id=1, source_target_pairs={{0,1},{1,0},{2,3},{3,2},{4,5},{5,4},{6,7},{7,6},{8,9},{9,8},{10,11... | collective-permute-start | bytes 786440 | tf_op jit(solution)/shard_map/ppermute | solution.py:290
  16.8 10.1 %collective-permute-start.12 = (f32[16,8,512]{2,1,0:T(8,128)S(1)}, f32[16,8,512]{2,1,0:T(8,128)S(1)}, u32[]{:S(2)}, u32[]{:S(2)}) collective-permute-start(f32[16,8,512]{2,1,0:T(8,128)S(1)} %get-tuple-element.35), channel_id=1, source_target_pairs={{0,7},{1,2},{2,1},{3,4},{4,3},{5,6},{6,5},{7,0},{8,15},{9,10},{10,... | collective-permute-start | bytes 786440 | tf_op jit(solution)/shard_map/ppermute | solution.py:289
  22.0 5.0 %collective-permute-start.9 = (f32[8,8,256]{2,1,0:T(8,128)S(1)}, f32[8,8,256]{2,1,0:T(8,128)S(1)}, u32[]{:S(2)}, u32[]{:S(2)}) collective-permute-start(f32[8,8,256]{2,1,0:T(8,128)S(1)} %get-tuple-element.24.c_ref), channel_id=1, source_target_pairs={{0,1},{1,0},{2,3},{3,2},{4,5},{5,4},{6,7},{7,6},{8,9},{9,8},{10,11... | collective-permute-start | bytes 196616 | tf_op jit(solution)/shard_map/ppermute | solution.py:290
  22.1 6.1 %collective-permute-start.8 = (f32[8,8,256]{2,1,0:T(8,128)S(1)}, f32[8,8,256]{2,1,0:T(8,128)S(1)}, u32[]{:S(2)}, u32[]{:S(2)}) collective-permute-start(f32[8,8,256]{2,1,0:T(8,128)S(1)} %get-tuple-element.24.c_ref), channel_id=1, source_target_pairs={{0,7},{1,2},{2,1},{3,4},{4,3},{5,6},{6,5},{7,0},{8,15},{9,10},{10,... | collective-permute-start | bytes 196616 | tf_op jit(solution)/shard_map/ppermute | solution.py:289
  26.3 10.5 %collective-permute-start.7 = (f32[16,8,512]{2,1,0:T(8,128)S(1)}, f32[16,8,512]{2,1,0:T(8,128)S(1)}, u32[]{:S(2)}, u32[]{:S(2)}) collective-permute-start(f32[16,8,512]{2,1,0:T(8,128)S(1)} %get-tuple-element.38), channel_id=1, source_target_pairs={{0,1},{1,0},{2,3},{3,2},{4,5},{5,4},{6,7},{7,6},{8,9},{9,8},{10,11... | collective-permute-start | bytes 786440 | tf_op jit(solution)/shard_map/ppermute | solution.py:290
  26.4 10.4 %collective-permute-start.6 = (f32[16,8,512]{2,1,0:T(8,128)S(1)}, f32[16,8,512]{2,1,0:T(8,128)S(1)}, u32[]{:S(2)}, u32[]{:S(2)}) collective-permute-start(f32[16,8,512]{2,1,0:T(8,128)S(1)} %get-tuple-element.39), channel_id=1, source_target_pairs={{0,7},{1,2},{2,1},{3,4},{4,3},{5,6},{6,5},{7,0},{8,15},{9,10},{10,... | collective-permute-start | bytes 786440 | tf_op jit(solution)/shard_map/ppermute | solution.py:289
  28.2 7.0 %collective-permute-start.11 = (f32[5,24,256]{2,1,0:T(8,128)S(1)}, f32[5,24,256]{2,1,0:T(8,128)S(1)}, u32[]{:S(2)}, u32[]{:S(2)}) collective-permute-start(f32[5,24,256]{2,1,0:T(8,128)S(1)} %get-tuple-element.52), channel_id=1, source_target_pairs={{0,8},{8,0},{16,24},{24,16},{32,40},{40,32},{48,56},{56,48},{64,72... | collective-permute-start | bytes 368648 | tf_op jit(solution)/shard_map/ppermute | solution.py:290
  28.3 8.5 %collective-permute-start.10 = (f32[5,24,256]{2,1,0:T(8,128)S(1)}, f32[5,24,256]{2,1,0:T(8,128)S(1)}, u32[]{:S(2)}, u32[]{:S(2)}) collective-permute-start(f32[5,24,256]{2,1,0:T(8,128)S(1)} %get-tuple-element.53), channel_id=1, source_target_pairs={{0,120},{8,16},{16,8},{24,32},{32,24},{40,48},{48,40},{56,64},{64,... | collective-permute-start | bytes 368648 | tf_op jit(solution)/shard_map/ppermute | solution.py:289

commit v5 on v4

v5 whole, which is shorter than its diff:
```python
import jax
import jax.numpy as jnp
from jax import lax
from jax.experimental import pallas as pl
from jax.experimental.pallas import tpu as pltpu
from jax.sharding import PartitionSpec as P

CENTER = 8.0 / 3.0
OMEGA = 2.0 / 3.0
SCREEN = 0.05
THIRD = 1.0 - OMEGA
F32 = jnp.float32
COARSE_US = 20
INNER_US = 20


def iota(shape, dim):
    return lax.broadcasted_iota(jnp.int32, shape, dim)


def pairing(rows, columns, factor, value):
    r, c = iota((rows, columns), 0), iota((rows, columns), 1)
    hit = (r // factor == c) if rows > columns else (c // factor == r)
    return jnp.where(hit, value, 0.0).astype(F32)


def lanes_from(value, index):
    return jnp.take_along_axis(value, index, axis=1, mode="promise_in_bounds")


def stencil_rows(load, rows, blocks):
    v, t = {}, {}
    for x in range(rows[0] - 1, rows[-1] + 2):
        v[x] = load(x, 0)
        t[x] = [a + b for a, b in zip(load(x, -1), load(x, 1))]
    lane = iota(v[rows[0]][0].shape, 1)
    first, last = lane == 0, lane == 127
    zero = jnp.zeros(lane.shape, F32)
    out = {}
    for x in rows:
        m = [t[x - 1][b] + t[x + 1][b] for b in range(blocks)]
        w = [0.5 * m[b] + (t[x][b] + (v[x - 1][b] + v[x + 1][b])) for b in range(blocks)]
        up = [pltpu.roll(w[b], 1, 1) for b in range(blocks)]
        down = [pltpu.roll(w[b], 127, 1) for b in range(blocks)]
        total = []
        for b in range(blocks):
            below = jnp.where(first, up[b - 1] if b else zero, up[b])
            above = jnp.where(last, down[b + 1] if b < blocks - 1 else zero, down[b])
            total.append((below + above) + m[b])
        out[x] = total
    return v, out


def sweep(rows, starts, blocks, source, target, drive, coupling):
    for start in starts:
        def load(x, shift):
            ref, at = source(x)
            return [ref[at, b, pl.ds(start + shift, 8), :] for b in range(blocks)]

        v, out = stencil_rows(load, rows, blocks)
        here = pl.ds(start, 8)
        for x in rows:
            (to, i), (forcing, j), (factor, k) = target(x), drive(x), coupling(x)
            for b in range(blocks):
                to[i, b, here, :] = (
                    THIRD * v[x][b] + factor[k, b, here, :] * out[x][b] + forcing[j, b, here, :]
                )


def in_domain(index, low, count):
    place = low + index - 1
    return jnp.where((place >= 0) & (place < count), 1.0, 0.0).astype(F32)


def place():
    return lax.axis_index("gx"), lax.axis_index("gy"), lax.axis_size("gx"), lax.axis_size("gy")


def restrict_kernel(side_hbm, counts_hbm, out_ref, first_ref, last_ref, tmp, side_ref, counts_ref, arrived):
    copies = [
        pltpu.make_async_copy(counts_hbm, counts_ref, arrived.at[0]),
        pltpu.make_async_copy(side_hbm, side_ref, arrived.at[1]),
    ]
    for copy in copies:
        copy.start()
    for copy in copies:
        copy.wait()
    lane = iota((8, 128), 1)
    pick = (2 * lane) & 127
    for x in range(8):
        for b in range(4):
            lanes = slice(128 * b, 128 * b + 128)
            for start in (0, 8):
                rows = slice(start, start + 8)
                tmp[b, 16 * x + start : 16 * x + start + 8, :] = (
                    side_ref[2 * x, rows, lanes] + side_ref[2 * x + 1, rows, lanes]
                )
    for x in range(8):
        halves = []
        for b in range(4):
            pair = tmp[b, pl.ds(16 * x, 8, stride=2), :] + tmp[b, pl.ds(16 * x + 1, 8, stride=2), :]
            halves.append(lanes_from(pair + pltpu.roll(pair, 127, 1), pick))
        for b in range(2):
            out_ref[x, :, 128 * b : 128 * b + 128] = 0.5 * jnp.where(lane < 64, halves[2 * b], halves[2 * b + 1])
    out_ref[8] = jnp.zeros((8, 256), F32)
    out_ref[8, 0:4, 0:64] = counts_ref[...].reshape(4, 64).astype(F32)
    first_ref[...] = side_ref[0:8]
    last_ref[...] = side_ref[8:16]


def coarse_kernel(mid_ref, low_ref, high_ref, c_ref, counts_ref, even, odd, drive, coupling):
    gx, gy, n_gx, n_gy = place()
    strips = (low_ref, mid_ref, high_ref)
    counts = jnp.concatenate([strips[j][9 * i + 8][:, 0:64] for i in range(3) for j in range(3)], axis=0)
    counts_ref[:, 0:64] = counts
    spread = jnp.dot(counts, pairing(64, 256, 4, 1.0), preferred_element_type=F32)
    weight = OMEGA / (CENTER + (SCREEN * 4.0) * spread)
    sub = iota((8, 128), 0)
    for i in range(3):
        for j in range(3):
            inside = in_domain(i, gx, n_gx) * in_domain(j, gy, n_gy)
            group = weight[8 * (3 * i + j) : 8 * (3 * i + j) + 8, :] * inside
            here = pl.ds(8 * j + 8, 8)
            for k in range(2):
                for b in range(2):
                    lanes = slice(128 * b, 128 * b + 128)
                    tile = jnp.where(
                        sub < 4,
                        jnp.broadcast_to(group[2 * k : 2 * k + 1, lanes], (8, 128)),
                        jnp.broadcast_to(group[2 * k + 1 : 2 * k + 2, lanes], (8, 128)),
                    )
                    coupling[2 * i + k, b, here, :] = tile * (1.0 / 6.0)
                    for x in range(4):
                        at = 8 * i + 4 * k + x
                        value = tile * strips[j][9 * i + 4 * k + x, :, lanes]
                        drive[at + 1, b, here, :] = value
                        even[at + 1, b, here, :] = value
    for k in range(7):
        halo = 6 - k
        source, target = (even, odd) if k % 2 == 0 else (odd, even)
        starts = (8, 16, 24) if halo > 4 else ((12, 20) if halo else (16,))
        sweep(
            range(-halo, 8 + halo), starts, 2,
            lambda x: (source, x + 9),
            lambda x: (target, x + 9),
            lambda x: (drive, x + 9),
            lambda x: (coupling, (x + 8) // 4),
        )
    for x in range(8):
        c_ref[x] = jnp.concatenate([odd[9 + x, b, 16:24, :] for b in range(2)], axis=1)


def fine_starts(k):
    return (8, 16, 24, 32) if k < 5 else (12, 20, 28)


def inject(value, targets):
    half = iota((8, 128), 1) >> 1
    for b in range(4):
        lanes = 128 * (b // 2)
        grown = lanes_from(value[:, lanes : lanes + 128], half + 64 * (b % 2))
        for field, x, start in targets:
            for dx in range(2):
                for dy in range(2):
                    field[x + dx, b, pl.ds(start + dy, 8, stride=2), :] = grown


def inner_kernel(side_ref, side_low, side_high, c_ref, c_low, c_high, counts_ref,
                 even, odd, drive, coupling, center_ref):
    gx, gy, n_gx, n_gy = place()
    for j, ref in enumerate((c_low, c_ref, c_high)):
        inside = in_domain(j, gy, n_gy)
        for x in range(8):
            inject(ref[x] * inside, [(even, 2 * x, 16 * j)])
    spread = jnp.dot(counts_ref[:, 0:64], pairing(64, 512, 8, 1.0), preferred_element_type=F32)
    center = CENTER + SCREEN * spread
    inverse = OMEGA / center
    for xb in range(4):
        i, k = ((xb + 1) // 2, (xb + 1) % 2)
        for yb in range(4):
            j, l = ((yb + 1) // 2, (yb + 1) % 2)
            at = 8 * (3 * i + j) + 2 * k + l
            scale = inverse[at : at + 1, :] * (in_domain(i, gx, n_gx) * in_domain(j, gy, n_gy))
            center_ref[xb, yb : yb + 1, :] = center[at : at + 1, :]
            here = pl.ds(8 * yb + 8, 8)
            for b in range(4):
                lanes = slice(128 * b, 128 * b + 128)
                tile = jnp.broadcast_to(scale[:, lanes], (8, 128))
                coupling[xb, b, here, :] = tile * (1.0 / 6.0)
                if xb in (1, 2):
                    ref, row = (side_low, side_ref, side_ref, side_high)[yb], (0, 0, 8, 0)[yb]
                    for x in range(8 * xb - 8, 8 * xb):
                        drive[x, b, here, :] = tile * ref[x, row : row + 8, lanes]
    for k in range(1, 8):
        source, target = (odd, even) if k % 2 == 0 else (even, odd)
        sweep(
            range(k, 16 - k), fine_starts(k), 4,
            lambda x: (source, x),
            lambda x: (target, x),
            lambda x: (drive, x),
            lambda x: (coupling, x // 8 + 1),
        )


def outer_kernel(side_ref, side_left, side_right, corner_low, corner_high, c_low, c_high, center_ref,
                 inner_even, inner_odd, inner_drive, coupling, solution_hbm, residual_hbm,
                 even, odd, drive, solution_ref, residual_ref, sent):
    gx, gy, n_gx, n_gy = place()
    for i, ref, first in ((0, c_low, 0), (2, c_high, 26)):
        for j in range(3):
            inside = in_domain(i, gx, n_gx) * in_domain(j, gy, n_gy)
            for x in range(5):
                inject(ref[x, 8 * j : 8 * j + 8, :] * inside, [(even, first + 2 * x, 16 * j)])
    for xb, own, first in ((0, side_left, 0), (3, side_right, 8)):
        for yb in range(4):
            ref, at, row = ((corner_low, first, 0), (own, 0, 0), (own, 0, 8), (corner_high, first, 0))[yb]
            here = pl.ds(8 * yb + 8, 8)
            for b in range(4):
                tile = 6.0 * coupling[xb, b, here, :]
                for x in range(8):
                    drive[first + x, b, here, :] = tile * ref[at + x, row : row + 8, 128 * b : 128 * b + 128]

    def forcing(x):
        return (inner_drive, x) if 0 <= x < 16 else (drive, x + 8 if x < 0 else x - 8)

    def state(k, x):
        if k <= x < 16 - k:
            return (inner_odd if k % 2 else inner_even), x
        return (odd if k % 2 else even), x + 10

    for k in range(1, 9):
        for rows in (range(k - 9, k), range(16 - k, 25 - k)):
            sweep(
                rows, fine_starts(k), 4,
                lambda x: state(k - 1, x),
                lambda x: state(k, x),
                forcing,
                lambda x: (coupling, x // 8 + 1),
            )
    copies = []
    for first in (0, 8):
        for start in (16, 24):
            def load(x, shift):
                return [even[x + 10, b, pl.ds(start + shift, 8), :] for b in range(4)]

            v, out = stencil_rows(load, range(first, first + 8), 4)
            for x in range(first, first + 8):
                for b in range(4):
                    lanes, rows = slice(128 * b, 128 * b + 128), slice(start - 16, start - 8)
                    center = center_ref[1 + x // 8, start // 8 - 1 : start // 8, lanes]
                    solution_ref[x, rows, lanes] = v[x][b]
                    residual_ref[x, rows, lanes] = (
                        side_ref[x, rows, lanes] - center * v[x][b] + (1.0 / 6.0) * out[x][b]
                    )
        part = pl.ds(first, 8)
        for n, (source, target) in enumerate(((solution_ref, solution_hbm), (residual_ref, residual_hbm))):
            copies.append(pltpu.make_async_copy(source.at[part], target.at[part], sent.at[first // 4 + n]))
            copies[-1].start()
    for copy in copies:
        copy.wait()


def shape(*dims):
    return jax.ShapeDtypeStruct(dims, F32)


def call(kernel, outputs, scratch, name, microseconds, **specs):
    cost = pl.CostEstimate(flops=int(microseconds * 1.0e9), bytes_accessed=int(microseconds * 3.69e6), transcendentals=0)
    return pl.pallas_call(
        kernel,
        out_shape=[shape(*dims) for dims in outputs],
        scratch_shapes=[pltpu.VMEM(dims, F32) if isinstance(dims, tuple) else dims for dims in scratch],
        compiler_params=pltpu.CompilerParams(vmem_limit_bytes=20 * 1024 * 1024),
        cost_estimate=cost,
        name=name,
        **specs,
    )


def shards(right_side, point_counts):
    def exchange(axis, to_low, to_high):
        count, even = lax.axis_size(axis), lax.axis_index(axis) % 2 == 0
        outer = [(i, (i + (-1 if i % 2 == 0 else 1)) % count) for i in range(count)]
        inner = [(i, i + (1 if i % 2 == 0 else -1)) for i in range(count)]
        same = to_low is to_high
        first = lax.ppermute(to_low if same else jnp.where(even, to_low, to_high), axis, outer)
        second = lax.ppermute(to_low if same else jnp.where(even, to_high, to_low), axis, inner)
        return jnp.where(even, first, second), jnp.where(even, second, first)

    packed, first, last = call(
        restrict_kernel,
        [(9, 8, 256), (8, 16, 512), (8, 16, 512)],
        [(4, 128, 128), (16, 16, 512), pltpu.VMEM((2, 2, 64), jnp.int32), pltpu.SemaphoreType.DMA((2,))],
        "restrict",
        1,
        in_specs=[pl.BlockSpec(memory_space=pltpu.MemorySpace.HBM)] * 2,
    )(
        pltpu.with_memory_space_constraint(right_side, pltpu.MemorySpace.HBM),
        pltpu.with_memory_space_constraint(point_counts, pltpu.MemorySpace.HBM),
    )
    left, right = exchange("gx", packed, packed)
    packed = jnp.concatenate([left, packed, right], axis=0)
    side_left, side_right = exchange("gx", first, last)
    packed, own = lax.optimization_barrier((packed, right_side))
    side_low, side_high = exchange("gy", own[:, 0:8], own[:, 8:16])
    coarse, counts = call(
        coarse_kernel,
        [(8, 8, 256), (72, 128)],
        [(26, 2, 40, 128)] * 3 + [(6, 2, 40, 128)],
        "coarse",
        COARSE_US,
    )(packed, *exchange("gy", packed, packed))
    coarse, side_left, side_right = lax.optimization_barrier((coarse, side_left, side_right))
    coarse_low, coarse_high = exchange("gy", coarse, coarse)
    corner_low, corner_high = exchange(
        "gy",
        jnp.concatenate([side_left[:, 0:8], side_right[:, 0:8]], axis=0),
        jnp.concatenate([side_left[:, 8:16], side_right[:, 8:16]], axis=0),
    )
    wide = jnp.concatenate([coarse_low, coarse, coarse_high], axis=1)
    coarse_left, coarse_right = exchange("gx", wide[0:5], wide[3:8])
    field = (16, 4, 48, 128)
    even, odd, drive, coupling, center = call(
        inner_kernel, [field, field, field, (4, 4, 48, 128), (4, 4, 512)], [], "inner", INNER_US
    )(
        right_side, side_low, side_high, coarse, coarse_low, coarse_high, counts
    )
    field, block = (36, 4, 48, 128), (16, 16, 512)
    return call(
        outer_kernel,
        [block, block],
        [field, field, (16, 4, 48, 128), block, block, pltpu.SemaphoreType.DMA((4,))],
        "outer",
        6,
        out_specs=[pl.BlockSpec(memory_space=pltpu.MemorySpace.HBM)] * 2,
    )(
        right_side, side_left, side_right, corner_low, corner_high, coarse_left, coarse_right, center,
        even, odd, drive, coupling,
    )


def solution(mesh):
    specs = (P("gx", "gy", None), P("gx", "gy", None))
    return jax.shard_map(shards, mesh=mesh, in_specs=specs, out_specs=specs, check_vma=False)
```

time: 43.2 us -> 41.9 us (0.970)
  local copies, waits for them, and re-layouts: 1.76 us -> 0.04 us
    unnamed x6 -> x2, local copies, waits for them, and re-layouts: 1.72 us -> 0.01 us
  transfers between devices with their start and end apart: 14 -> 14, of which waited for: 5 -> 5; matrix products, arithmetic and copies ran while one was open for 1% -> 1% of each run, Pallas kernels for 10% -> 9%
where the time goes in v5:
time: 41.9 us; the launch traced here: 41.7 us
  starting transfers between devices  23 us (55%)
  Pallas kernels  11 us (26%)
  waiting for transfers between devices  6.28 us (15%)
  between operations  1.02 us (2%)
    ppermute x7, starting transfers between devices, exchange(): lax.ppermute(to_low if same else jnp.where(even, to_low, to_high), axis,...  20.8 us
    ppermute x7, waiting for transfers between devices, exchange(): lax.ppermute(to_low if same else jnp.where(even, to_low, to_high), axis,...  6.2 us
    pallas_call x1, Pallas kernels, shards(): call(outer_kernel, [block, block], [field, field, (16, 4, 48, 128), block...  5.9 us
    pallas_call x1, Pallas kernels, shards(): call(inner_kernel, [field, field, field, (4, 4, 48, 128), (4, 4, 512)], [...  2.34 us
    ppermute x7, starting transfers between devices, exchange(): lax.ppermute(to_low if same else jnp.where(even, to_high, to_low), axis,...  2.17 us
    pallas_call x1, Pallas kernels, shards(): call(coarse_kernel, [(8, 8, 256), (72, 128)], [(26, 2, 40, 128)] * 3 + [(...  1.47 us
    pallas_call x1, Pallas kernels, shards(): call(restrict_kernel, [(9, 8, 256), (8, 16, 512), (8, 16, 512)], [(4, 128...  1.31 us
  transfers between devices with their start and end apart: 14, of which 5 were waited for; matrix products, arithmetic and copies ran while one was open for 1% of the time, Pallas kernels for 9%

profile of v5, /device:TPU:0, one launch (start us, length us, event | category | flops | bytes accessed | tf_op | source)
XLA Modules:
  0.0 41.7 jit_solution(13781876650696912979)
XLA Ops:
  0.6 1.3 %restrict.1 = (f32[9,8,256]{2,1,0:T(8,128)S(1)}, f32[8,16,512]{2,1,0:T(8,128)S(1)}, f32[8,16,512]{2,1,0:T(8,128)S(1)}) custom-call(f32[16,16,512]{2,1,0:T(8,128)} %side_ref.3, s32[2,2,64]{2,1,0:T(2,128)} %counts_hbm.1), custom_call_target="tpu_custom_call" | custom-call | flops 1000000000 | bytes 3690000 | tf_op jit(solution)/shard_map/restrict/pallas_call | solution.py:290
  1.9 0.0 copy-start
  2.0 1.7 %collective-permute-start.1 = (f32[9,8,256]{2,1,0:T(8,128)S(1)}, f32[9,8,256]{2,1,0:T(8,128)S(1)}, u32[]{:S(2)}, u32[]{:S(2)}) collective-permute-start(f32[9,8,256]{2,1,0:T(8,128)S(1)} %get-tuple-element.17), channel_id=1, source_target_pairs={{0,8},{8,0},{16,24},{24,16},{32,40},{40,32},{48,56},{56,48},{64,72... | collective-permute-start | bytes 221192 | tf_op jit(solution)/shard_map/ppermute | solution.py:287
  3.6 4.5 %collective-permute-start = (f32[9,8,256]{2,1,0:T(8,128)S(1)}, f32[9,8,256]{2,1,0:T(8,128)S(1)}, u32[]{:S(2)}, u32[]{:S(2)}) collective-permute-start(f32[9,8,256]{2,1,0:T(8,128)S(1)} %get-tuple-element.17), channel_id=1, source_target_pairs={{0,120},{8,16},{16,8},{24,32},{32,24},{40,48},{48,40},{56,64},{64,... | collective-permute-start | bytes 221192 | tf_op jit(solution)/shard_map/ppermute | solution.py:286
  8.2 0.1 collective-permute-start.5
  8.3 1.2 %collective-permute-start.4 = (f32[8,16,512]{2,1,0:T(8,128)S(1)}, f32[8,16,512]{2,1,0:T(8,128)S(1)}, u32[]{:S(2)}, u32[]{:S(2)}) collective-permute-start(f32[8,16,512]{2,1,0:T(8,128)S(1)} %get-tuple-element.43), channel_id=1, source_target_pairs={{0,120},{8,16},{16,8},{24,32},{32,24},{40,48},{48,40},{56,64},{64,... | collective-permute-start | bytes 786440 | tf_op jit(solution)/shard_map/ppermute | solution.py:286
  9.5 1.8 %collective-permute-done = f32[9,8,256]{2,1,0:T(8,128)S(1)} collective-permute-done((f32[9,8,256]{2,1,0:T(8,128)S(1)}, f32[9,8,256]{2,1,0:T(8,128)S(1)}, u32[]{:S(2)}, u32[]{:S(2)}) %collective-permute-start) | collective-permute-done | bytes 73760 | tf_op jit(solution)/shard_map/ppermute | solution.py:286
  11.3 0.1 collective-permute-start.3
  11.4 4.1 %collective-permute-start.2 = (f32[27,8,256]{2,1,0:T(8,128)S(1)}, f32[27,8,256]{2,1,0:T(8,128)S(1)}, u32[]{:S(2)}, u32[]{:S(2)}) collective-permute-start(f32[27,8,256]{2,1,0:T(8,128)S(1)} %pad_maximum_fusion.2.mid_ref), channel_id=1, source_target_pairs={{0,7},{1,2},{2,1},{3,4},{4,3},{5,6},{6,5},{7,0},{8,15},{9,10},{10,... | collective-permute-start | bytes 663560 | tf_op jit(solution)/shard_map/ppermute | solution.py:286
  15.6 0.1 collective-permute-start.13
  15.7 0.1 collective-permute-done.5
  15.8 2.0 %collective-permute-start.12 = (f32[16,8,512]{2,1,0:T(8,128)S(1)}, f32[16,8,512]{2,1,0:T(8,128)S(1)}, u32[]{:S(2)}, u32[]{:S(2)}) collective-permute-start(f32[16,8,512]{2,1,0:T(8,128)S(1)} %get-tuple-element.35), channel_id=1, source_target_pairs={{0,7},{1,2},{2,1},{3,4},{4,3},{5,6},{6,5},{7,0},{8,15},{9,10},{10,... | collective-permute-start | bytes 786440 | tf_op jit(solution)/shard_map/ppermute | solution.py:286
  17.8 1.4 %collective-permute-done.4 = f32[8,16,512]{2,1,0:T(8,128)S(1)} collective-permute-done((f32[8,16,512]{2,1,0:T(8,128)S(1)}, f32[8,16,512]{2,1,0:T(8,128)S(1)}, u32[]{:S(2)}, u32[]{:S(2)}) %collective-permute-start.4) | collective-permute-done | bytes 262176 | tf_op jit(solution)/shard_map/ppermute | solution.py:286
  19.3 1.5 %coarse.1 = (f32[8,8,256]{2,1,0:T(8,128)S(1)}, f32[72,128]{1,0:T(8,128)S(1)}) custom-call(f32[27,8,256]{2,1,0:T(8,128)S(1)} %pad_maximum_fusion.2.mid_ref, f32[27,8,256]{2,1,0:T(8,128)S(1)} %get-tuple-element.45.low_ref, f32[27,8,256]{2,1,0:T(8,128)S(1)} %get-tuple-element.44.high_ref), custom_call_target="tpu_custom_call" | custom-call | flops 20000000000 | bytes 73800000 | tf_op jit(solution)/shard_map/coarse/pallas_call | solution.py:306
  20.8 0.1 collective-permute-start.9
  20.9 4.1 %collective-permute-start.8 = (f32[8,8,256]{2,1,0:T(8,128)S(1)}, f32[8,8,256]{2,1,0:T(8,128)S(1)}, u32[]{:S(2)}, u32[]{:S(2)}) collective-permute-start(f32[8,8,256]{2,1,0:T(8,128)S(1)} %get-tuple-element.24.c_ref), channel_id=1, source_target_pairs={{0,7},{1,2},{2,1},{3,4},{4,3},{5,6},{6,5},{7,0},{8,15},{9,10},{10,... | collective-permute-start | bytes 196616 | tf_op jit(solution)/shard_map/ppermute | solution.py:286
  25.1 0.1 collective-permute-start.7
  25.2 0.5 %collective-permute-start.6 = (f32[16,8,512]{2,1,0:T(8,128)S(1)}, f32[16,8,512]{2,1,0:T(8,128)S(1)}, u32[]{:S(2)}, u32[]{:S(2)}) collective-permute-start(f32[16,8,512]{2,1,0:T(8,128)S(1)} %get-tuple-element.39), channel_id=1, source_target_pairs={{0,7},{1,2},{2,1},{3,4},{4,3},{5,6},{6,5},{7,0},{8,15},{9,10},{10,... | collective-permute-start | bytes 786440 | tf_op jit(solution)/shard_map/ppermute | solution.py:286
  25.8 1.2 %collective-permute-done.8 = f32[8,8,256]{2,1,0:T(8,128)S(1)} collective-permute-done((f32[8,8,256]{2,1,0:T(8,128)S(1)}, f32[8,8,256]{2,1,0:T(8,128)S(1)}, u32[]{:S(2)}, u32[]{:S(2)}) %collective-permute-start.8) | collective-permute-done | bytes 65568 | tf_op jit(solution)/shard_map/ppermute | solution.py:286
  27.0 0.1 collective-permute-start.11
  27.1 4.3 %collective-permute-start.10 = (f32[5,24,256]{2,1,0:T(8,128)S(1)}, f32[5,24,256]{2,1,0:T(8,128)S(1)}, u32[]{:S(2)}, u32[]{:S(2)}) collective-permute-start(f32[5,24,256]{2,1,0:T(8,128)S(1)} %get-tuple-element.53), channel_id=1, source_target_pairs={{0,120},{8,16},{16,8},{24,32},{32,24},{40,48},{48,40},{56,64},{64,... | collective-permute-start | bytes 368648 | tf_op jit(solution)/shard_map/ppermute | solution.py:286
  31.4 2.3 %inner.1 = (f32[16,4,48,128]{3,2,1,0:T(8,128)S(1)}, f32[16,4,48,128]{3,2,1,0:T(8,128)S(1)}, f32[16,4,48,128]{3,2,1,0:T(8,128)S(1)}, f32[4,4,48,128]{3,2,1,0:T(8,128)S(1)}, f32[4,4,512]{2,1,0:T(4,128)S(1)}) custom-call(f32[16,16,512]{2,1,0:T(8,128)S(1)} %copy-done, f32[16,8,512]{2,1,0:T(8,128)S(1)} %get-tuple-element.33.side_low, ...), custom_call_target="tpu_custom_call" | custom-call | flops 20000000000 | bytes 73800000 | tf_op jit(solution)/shard_map/inner/pallas_call | solution.py:323
  33.8 1.8 %collective-permute-done.10 = f32[5,24,256]{2,1,0:T(8,128)S(1)} collective-permute-done((f32[5,24,256]{2,1,0:T(8,128)S(1)}, f32[5,24,256]{2,1,0:T(8,128)S(1)}, u32[]{:S(2)}, u32[]{:S(2)}) %collective-permute-start.10) | collective-permute-done | bytes 122912 | tf_op jit(solution)/shard_map/ppermute | solution.py:286
  35.7 5.9 %outer.1 = (f32[16,16,512]{2,1,0:T(8,128)}, f32[16,16,512]{2,1,0:T(8,128)}) custom-call(f32[16,16,512]{2,1,0:T(8,128)S(1)} %copy-done, f32[8,16,512]{2,1,0:T(8,128)S(1)} %get-tuple-element.22.side_left, f32[8,16,512]{2,1,0:T(8,128)S(1)} %get-tuple-element.23.side_right, f32[16,8,512]{2,1,0:T(8,128)S(1)} %get-tuple-element.37.corner_low, ...), custom_call_target="tpu_custom_call" | custom-call | flops 6000000000 | bytes 22140000 | tf_op jit(solution)/shard_map/outer/pallas_call | solution.py:329
  (24 shorter events, 0.4 us)
Async XLA Ops:
  1.9 13.6 %copy-start = (f32[16,16,512]{2,1,0:T(8,128)S(1)}, f32[16,16,512]{2,1,0:T(8,128)}, u32[]{:S(2)}) copy-start(f32[16,16,512]{2,1,0:T(8,128)} %side_ref.3) | copy-start | bytes 1572868
  2.0 7.5 %collective-permute-start.1 = (f32[9,8,256]{2,1,0:T(8,128)S(1)}, f32[9,8,256]{2,1,0:T(8,128)S(1)}, u32[]{:S(2)}, u32[]{:S(2)}) collective-permute-start(f32[9,8,256]{2,1,0:T(8,128)S(1)} %get-tuple-element.17), channel_id=1, source_target_pairs={{0,8},{8,0},{16,24},{24,16},{32,40},{40,32},{48,56},{56,48},{64,72... | collective-permute-start | bytes 221192 | tf_op jit(solution)/shard_map/ppermute | solution.py:287
  3.6 7.7 %collective-permute-start = (f32[9,8,256]{2,1,0:T(8,128)S(1)}, f32[9,8,256]{2,1,0:T(8,128)S(1)}, u32[]{:S(2)}, u32[]{:S(2)}) collective-permute-start(f32[9,8,256]{2,1,0:T(8,128)S(1)} %get-tuple-element.17), channel_id=1, source_target_pairs={{0,120},{8,16},{16,8},{24,32},{32,24},{40,48},{48,40},{56,64},{64,... | collective-permute-start | bytes 221192 | tf_op jit(solution)/shard_map/ppermute | solution.py:286
  8.2 7.6 %collective-permute-start.5 = (f32[8,16,512]{2,1,0:T(8,128)S(1)}, f32[8,16,512]{2,1,0:T(8,128)S(1)}, u32[]{:S(2)}, u32[]{:S(2)}) collective-permute-start(f32[8,16,512]{2,1,0:T(8,128)S(1)} %get-tuple-element.42), channel_id=1, source_target_pairs={{0,8},{8,0},{16,24},{24,16},{32,40},{40,32},{48,56},{56,48},{64,72... | collective-permute-start | bytes 786440 | tf_op jit(solution)/shard_map/ppermute | solution.py:287
  8.3 10.9 %collective-permute-start.4 = (f32[8,16,512]{2,1,0:T(8,128)S(1)}, f32[8,16,512]{2,1,0:T(8,128)S(1)}, u32[]{:S(2)}, u32[]{:S(2)}) collective-permute-start(f32[8,16,512]{2,1,0:T(8,128)S(1)} %get-tuple-element.43), channel_id=1, source_target_pairs={{0,120},{8,16},{16,8},{24,32},{32,24},{40,48},{48,40},{56,64},{64,... | collective-permute-start | bytes 786440 | tf_op jit(solution)/shard_map/ppermute | solution.py:286
  11.3 7.9 %collective-permute-start.3 = (f32[27,8,256]{2,1,0:T(8,128)S(1)}, f32[27,8,256]{2,1,0:T(8,128)S(1)}, u32[]{:S(2)}, u32[]{:S(2)}) collective-permute-start(f32[27,8,256]{2,1,0:T(8,128)S(1)} %pad_maximum_fusion.2.mid_ref), channel_id=1, source_target_pairs={{0,1},{1,0},{2,3},{3,2},{4,5},{5,4},{6,7},{7,6},{8,9},{9,8},{10,11... | collective-permute-start | bytes 663560 | tf_op jit(solution)/shard_map/ppermute | solution.py:287
  11.4 7.8 %collective-permute-start.2 = (f32[27,8,256]{2,1,0:T(8,128)S(1)}, f32[27,8,256]{2,1,0:T(8,128)S(1)}, u32[]{:S(2)}, u32[]{:S(2)}) collective-permute-start(f32[27,8,256]{2,1,0:T(8,128)S(1)} %pad_maximum_fusion.2.mid_ref), channel_id=1, source_target_pairs={{0,7},{1,2},{2,1},{3,4},{4,3},{5,6},{6,5},{7,0},{8,15},{9,10},{10,... | collective-permute-start | bytes 663560 | tf_op jit(solution)/shard_map/ppermute | solution.py:286
  15.6 9.6 %collective-permute-start.13 = (f32[16,8,512]{2,1,0:T(8,128)S(1)}, f32[16,8,512]{2,1,0:T(8,128)S(1)}, u32[]{:S(2)}, u32[]{:S(2)}) collective-permute-start(f32[16,8,512]{2,1,0:T(8,128)S(1)} %get-tuple-element.34), channel_id=1, source_target_pairs={{0,1},{1,0},{2,3},{3,2},{4,5},{5,4},{6,7},{7,6},{8,9},{9,8},{10,11... | collective-permute-start | bytes 786440 | tf_op jit(solution)/shard_map/ppermute | solution.py:287
  15.8 9.9 %collective-permute-start.12 = (f32[16,8,512]{2,1,0:T(8,128)S(1)}, f32[16,8,512]{2,1,0:T(8,128)S(1)}, u32[]{:S(2)}, u32[]{:S(2)}) collective-permute-start(f32[16,8,512]{2,1,0:T(8,128)S(1)} %get-tuple-element.35), channel_id=1, source_target_pairs={{0,7},{1,2},{2,1},{3,4},{4,3},{5,6},{6,5},{7,0},{8,15},{9,10},{10,... | collective-permute-start | bytes 786440 | tf_op jit(solution)/shard_map/ppermute | solution.py:286
  20.8 5.0 %collective-permute-start.9 = (f32[8,8,256]{2,1,0:T(8,128)S(1)}, f32[8,8,256]{2,1,0:T(8,128)S(1)}, u32[]{:S(2)}, u32[]{:S(2)}) collective-permute-start(f32[8,8,256]{2,1,0:T(8,128)S(1)} %get-tuple-element.24.c_ref), channel_id=1, source_target_pairs={{0,1},{1,0},{2,3},{3,2},{4,5},{5,4},{6,7},{7,6},{8,9},{9,8},{10,11... | collective-permute-start | bytes 196616 | tf_op jit(solution)/shard_map/ppermute | solution.py:287
  20.9 6.1 %collective-permute-start.8 = (f32[8,8,256]{2,1,0:T(8,128)S(1)}, f32[8,8,256]{2,1,0:T(8,128)S(1)}, u32[]{:S(2)}, u32[]{:S(2)}) collective-permute-start(f32[8,8,256]{2,1,0:T(8,128)S(1)} %get-tuple-element.24.c_ref), channel_id=1, source_target_pairs={{0,7},{1,2},{2,1},{3,4},{4,3},{5,6},{6,5},{7,0},{8,15},{9,10},{10,... | collective-permute-start | bytes 196616 | tf_op jit(solution)/shard_map/ppermute | solution.py:286
  25.1 10.5 %collective-permute-start.7 = (f32[16,8,512]{2,1,0:T(8,128)S(1)}, f32[16,8,512]{2,1,0:T(8,128)S(1)}, u32[]{:S(2)}, u32[]{:S(2)}) collective-permute-start(f32[16,8,512]{2,1,0:T(8,128)S(1)} %get-tuple-element.38), channel_id=1, source_target_pairs={{0,1},{1,0},{2,3},{3,2},{4,5},{5,4},{6,7},{7,6},{8,9},{9,8},{10,11... | collective-permute-start | bytes 786440 | tf_op jit(solution)/shard_map/ppermute | solution.py:287
  25.2 10.4 %collective-permute-start.6 = (f32[16,8,512]{2,1,0:T(8,128)S(1)}, f32[16,8,512]{2,1,0:T(8,128)S(1)}, u32[]{:S(2)}, u32[]{:S(2)}) collective-permute-start(f32[16,8,512]{2,1,0:T(8,128)S(1)} %get-tuple-element.39), channel_id=1, source_target_pairs={{0,7},{1,2},{2,1},{3,4},{4,3},{5,6},{6,5},{7,0},{8,15},{9,10},{10,... | collective-permute-start | bytes 786440 | tf_op jit(solution)/shard_map/ppermute | solution.py:286
  27.0 6.8 %collective-permute-start.11 = (f32[5,24,256]{2,1,0:T(8,128)S(1)}, f32[5,24,256]{2,1,0:T(8,128)S(1)}, u32[]{:S(2)}, u32[]{:S(2)}) collective-permute-start(f32[5,24,256]{2,1,0:T(8,128)S(1)} %get-tuple-element.52), channel_id=1, source_target_pairs={{0,8},{8,0},{16,24},{24,16},{32,40},{40,32},{48,56},{56,48},{64,72... | collective-permute-start | bytes 368648 | tf_op jit(solution)/shard_map/ppermute | solution.py:287
  27.1 8.5 %collective-permute-start.10 = (f32[5,24,256]{2,1,0:T(8,128)S(1)}, f32[5,24,256]{2,1,0:T(8,128)S(1)}, u32[]{:S(2)}, u32[]{:S(2)}) collective-permute-start(f32[5,24,256]{2,1,0:T(8,128)S(1)} %get-tuple-element.53), channel_id=1, source_target_pairs={{0,120},{8,16},{16,8},{24,32},{32,24},{40,48},{48,40},{56,64},{64,... | collective-permute-start | bytes 368648 | tf_op jit(solution)/shard_map/ppermute | solution.py:286

commit v6 on v5

--- a/solution.py
+++ b/solution.py
@@ -79,39 +79,42 @@
 def restrict_kernel(side_hbm, counts_hbm, out_ref, first_ref, last_ref, tmp, side_ref, counts_ref, arrived):
     copies = [
         pltpu.make_async_copy(counts_hbm, counts_ref, arrived.at[0]),
-        pltpu.make_async_copy(side_hbm, side_ref, arrived.at[1]),
+        pltpu.make_async_copy(side_hbm.at[0:8], side_ref.at[0:8], arrived.at[1]),
+        pltpu.make_async_copy(side_hbm.at[8:16], side_ref.at[8:16], arrived.at[2]),
     ]
     for copy in copies:
         copy.start()
-    for copy in copies:
-        copy.wait()
     lane = iota((8, 128), 1)
     pick = (2 * lane) & 127
-    for x in range(8):
-        for b in range(4):
-            lanes = slice(128 * b, 128 * b + 128)
-            for start in (0, 8):
-                rows = slice(start, start + 8)
-                tmp[b, 16 * x + start : 16 * x + start + 8, :] = (
-                    side_ref[2 * x, rows, lanes] + side_ref[2 * x + 1, rows, lanes]
+    for part in range(2):
+        copies[1 + part].wait()
+        for x in range(4 * part, 4 * part + 4):
+            for b in range(4):
+                lanes = slice(128 * b, 128 * b + 128)
+                for start in (0, 8):
+                    rows = slice(start, start + 8)
+                    tmp[b, 16 * x + start : 16 * x + start + 8, :] = (
+                        side_ref[2 * x, rows, lanes] + side_ref[2 * x + 1, rows, lanes]
+                    )
+        for x in range(4 * part, 4 * part + 4):
+            halves = []
+            for b in range(4):
+                pair = tmp[b, pl.ds(16 * x, 8, stride=2), :] + tmp[b, pl.ds(16 * x + 1, 8, stride=2), :]
+                halves.append(lanes_from(pair + pltpu.roll(pair, 127, 1), pick))
+            for b in range(2):
+                out_ref[x, :, 128 * b : 128 * b + 128] = 0.5 * jnp.where(
+                    lane < 64, halves[2 * b], halves[2 * b + 1]
                 )
-    for x in range(8):
-        halves = []
-        for b in range(4):
-            pair = tmp[b, pl.ds(16 * x, 8, stride=2), :] + tmp[b, pl.ds(16 * x + 1, 8, stride=2), :]
-            halves.append(lanes_from(pair + pltpu.roll(pair, 127, 1), pick))
-        for b in range(2):
-            out_ref[x, :, 128 * b : 128 * b + 128] = 0.5 * jnp.where(lane < 64, halves[2 * b], halves[2 * b + 1])
+        (first_ref, last_ref)[part][...] = side_ref[8 * part : 8 * part + 8]
+    copies[0].wait()
     out_ref[8] = jnp.zeros((8, 256), F32)
     out_ref[8, 0:4, 0:64] = counts_ref[...].reshape(4, 64).astype(F32)
-    first_ref[...] = side_ref[0:8]
-    last_ref[...] = side_ref[8:16]
 
 
 def coarse_kernel(mid_ref, low_ref, high_ref, c_ref, counts_ref, even, odd, drive, coupling):
     gx, gy, n_gx, n_gy = place()
     strips = (low_ref, mid_ref, high_ref)
-    counts = jnp.concatenate([strips[j][9 * i + 8][:, 0:64] for i in range(3) for j in range(3)], axis=0)
+    counts = jnp.concatenate([strips[j][row][:, 0:64] for row in (7, 16, 24) for j in range(3)], axis=0)
     counts_ref[:, 0:64] = counts
     spread = jnp.dot(counts, pairing(64, 256, 4, 1.0), preferred_element_type=F32)
     weight = OMEGA / (CENTER + (SCREEN * 4.0) * spread)
@@ -132,7 +135,9 @@
                     coupling[2 * i + k, b, here, :] = tile * (1.0 / 6.0)
                     for x in range(4):
                         at = 8 * i + 4 * k + x
-                        value = tile * strips[j][9 * i + 4 * k + x, :, lanes]
+                        if at in (0, 23):
+                            continue
+                        value = tile * strips[j][at + i - 1, :, lanes]
                         drive[at + 1, b, here, :] = value
                         even[at + 1, b, here, :] = value
     for k in range(7):
@@ -229,7 +234,7 @@
         return (odd if k % 2 else even), x + 10
 
     for k in range(1, 9):
-        for rows in (range(k - 9, k), range(16 - k, 25 - k)):
+        for rows in (range(k - 9, k), range(16 - k, 25 - k)) if k < 8 else (range(-1, 17),):
             sweep(
                 rows, fine_starts(k), 4,
                 lambda x: state(k - 1, x),
@@ -238,13 +243,13 @@
                 lambda x: (coupling, x // 8 + 1),
             )
     copies = []
-    for first in (0, 8):
+    for first in (0, 4, 8, 12):
         for start in (16, 24):
             def load(x, shift):
                 return [even[x + 10, b, pl.ds(start + shift, 8), :] for b in range(4)]
 
-            v, out = stencil_rows(load, range(first, first + 8), 4)
-            for x in range(first, first + 8):
+            v, out = stencil_rows(load, range(first, first + 4), 4)
+            for x in range(first, first + 4):
                 for b in range(4):
                     lanes, rows = slice(128 * b, 128 * b + 128), slice(start - 16, start - 8)
                     center = center_ref[1 + x // 8, start // 8 - 1 : start // 8, lanes]
@@ -252,9 +257,9 @@
                     residual_ref[x, rows, lanes] = (
                         side_ref[x, rows, lanes] - center * v[x][b] + (1.0 / 6.0) * out[x][b]
                     )
-        part = pl.ds(first, 8)
+        part = pl.ds(first, 4)
         for n, (source, target) in enumerate(((solution_ref, solution_hbm), (residual_ref, residual_hbm))):
-            copies.append(pltpu.make_async_copy(source.at[part], target.at[part], sent.at[first // 4 + n]))
+            copies.append(pltpu.make_async_copy(source.at[part], target.at[part], sent.at[first // 2 + n]))
             copies[-1].start()
     for copy in copies:
         copy.wait()
@@ -290,7 +295,7 @@
     packed, first, last = call(
         restrict_kernel,
         [(9, 8, 256), (8, 16, 512), (8, 16, 512)],
-        [(4, 128, 128), (16, 16, 512), pltpu.VMEM((2, 2, 64), jnp.int32), pltpu.SemaphoreType.DMA((2,))],
+        [(4, 128, 128), (16, 16, 512), pltpu.VMEM((2, 2, 64), jnp.int32), pltpu.SemaphoreType.DMA((3,))],
         "restrict",
         1,
         in_specs=[pl.BlockSpec(memory_space=pltpu.MemorySpace.HBM)] * 2,
@@ -299,7 +304,7 @@
         pltpu.with_memory_space_constraint(point_counts, pltpu.MemorySpace.HBM),
     )
     left, right = exchange("gx", packed, packed)
-    packed = jnp.concatenate([left, packed, right], axis=0)
+    packed = jnp.concatenate([left[1:9], packed, right[0:7], right[8:9]], axis=0)
     side_left, side_right = exchange("gx", first, last)
     packed, own = lax.optimization_barrier((packed, right_side))
     side_low, side_high = exchange("gy", own[:, 0:8], own[:, 8:16])
@@ -329,7 +334,7 @@
     return call(
         outer_kernel,
         [block, block],
-        [field, field, (16, 4, 48, 128), block, block, pltpu.SemaphoreType.DMA((4,))],
+        [field, field, (16, 4, 48, 128), block, block, pltpu.SemaphoreType.DMA((8,))],
         "outer",
         6,
         out_specs=[pl.BlockSpec(memory_space=pltpu.MemorySpace.HBM)] * 2,

time: 41.9 us -> 41.9 us (level)
  transfers between devices with their start and end apart: 14 -> 14, of which waited for: 5 -> 4; matrix products, arithmetic and copies ran while one was open for 1% -> 1% of each run, Pallas kernels for 9% -> 9%
where the time goes in v6:
time: 41.9 us; the launch traced here: 41.7 us
  starting transfers between devices  22.9 us (55%)
  Pallas kernels  11.1 us (26%)
  waiting for transfers between devices  6.38 us (15%)
  between operations  1.04 us (2%)
    ppermute x7, starting transfers between devices, exchange(): lax.ppermute(to_low if same else jnp.where(even, to_low, to_high), axis,...  20.7 us
    ppermute x7, waiting for transfers between devices, exchange(): lax.ppermute(to_low if same else jnp.where(even, to_low, to_high), axis,...  6.33 us
    pallas_call x1, Pallas kernels, shards(): call(outer_kernel, [block, block], [field, field, (16, 4, 48, 128), block...  5.88 us
    pallas_call x1, Pallas kernels, shards(): call(inner_kernel, [field, field, field, (4, 4, 48, 128), (4, 4, 512)], [...  2.34 us
    ppermute x7, starting transfers between devices, exchange(): lax.ppermute(to_low if same else jnp.where(even, to_high, to_low), axis,...  2.17 us
    pallas_call x1, Pallas kernels, shards(): call(coarse_kernel, [(8, 8, 256), (72, 128)], [(26, 2, 40, 128)] * 3 + [(...  1.47 us
    pallas_call x1, Pallas kernels, shards(): call(restrict_kernel, [(9, 8, 256), (8, 16, 512), (8, 16, 512)], [(4, 128...  1.36 us
  transfers between devices with their start and end apart: 14, of which 4 were waited for; matrix products, arithmetic and copies ran while one was open for 1% of the time, Pallas kernels for 9%

profile of v6, /device:TPU:0, one launch (start us, length us, event | category | flops | bytes accessed | tf_op | source)
XLA Modules:
  0.0 41.7 jit_solution(12146370157512495292)
XLA Ops:
  0.6 1.4 %restrict.1 = (f32[9,8,256]{2,1,0:T(8,128)S(1)}, f32[8,16,512]{2,1,0:T(8,128)S(1)}, f32[8,16,512]{2,1,0:T(8,128)S(1)}) custom-call(f32[16,16,512]{2,1,0:T(8,128)} %side_ref.3, s32[2,2,64]{2,1,0:T(2,128)} %counts_hbm.1), custom_call_target="tpu_custom_call" | custom-call | flops 1000000000 | bytes 3690000 | tf_op jit(solution)/shard_map/restrict/pallas_call | solution.py:295
  2.0 0.0 copy-start
  2.0 1.7 %collective-permute-start.1 = (f32[9,8,256]{2,1,0:T(8,128)S(1)}, f32[9,8,256]{2,1,0:T(8,128)S(1)}, u32[]{:S(2)}, u32[]{:S(2)}) collective-permute-start(f32[9,8,256]{2,1,0:T(8,128)S(1)} %get-tuple-element.17), channel_id=1, source_target_pairs={{0,8},{8,0},{16,24},{24,16},{32,40},{40,32},{48,56},{56,48},{64,72... | collective-permute-start | bytes 221192 | tf_op jit(solution)/shard_map/ppermute | solution.py:292
  3.7 4.5 %collective-permute-start = (f32[9,8,256]{2,1,0:T(8,128)S(1)}, f32[9,8,256]{2,1,0:T(8,128)S(1)}, u32[]{:S(2)}, u32[]{:S(2)}) collective-permute-start(f32[9,8,256]{2,1,0:T(8,128)S(1)} %get-tuple-element.17), channel_id=1, source_target_pairs={{0,120},{8,16},{16,8},{24,32},{32,24},{40,48},{48,40},{56,64},{64,... | collective-permute-start | bytes 221192 | tf_op jit(solution)/shard_map/ppermute | solution.py:291
  8.3 0.1 collective-permute-start.5
  8.3 1.2 %collective-permute-start.4 = (f32[8,16,512]{2,1,0:T(8,128)S(1)}, f32[8,16,512]{2,1,0:T(8,128)S(1)}, u32[]{:S(2)}, u32[]{:S(2)}) collective-permute-start(f32[8,16,512]{2,1,0:T(8,128)S(1)} %get-tuple-element.43), channel_id=1, source_target_pairs={{0,120},{8,16},{16,8},{24,32},{32,24},{40,48},{48,40},{56,64},{64,... | collective-permute-start | bytes 786440 | tf_op jit(solution)/shard_map/ppermute | solution.py:291
  9.5 1.8 %collective-permute-done = f32[9,8,256]{2,1,0:T(8,128)S(1)} collective-permute-done((f32[9,8,256]{2,1,0:T(8,128)S(1)}, f32[9,8,256]{2,1,0:T(8,128)S(1)}, u32[]{:S(2)}, u32[]{:S(2)}) %collective-permute-start) | collective-permute-done | bytes 73760 | tf_op jit(solution)/shard_map/ppermute | solution.py:291
  11.4 0.1 collective-permute-start.3
  11.5 4.1 %collective-permute-start.2 = (f32[25,8,256]{2,1,0:T(8,128)S(1)}, f32[25,8,256]{2,1,0:T(8,128)S(1)}, u32[]{:S(2)}, u32[]{:S(2)}) collective-permute-start(f32[25,8,256]{2,1,0:T(8,128)S(1)} %pad_maximum_fusion.2.mid_ref), channel_id=1, source_target_pairs={{0,7},{1,2},{2,1},{3,4},{4,3},{5,6},{6,5},{7,0},{8,15},{9,10},{10,... | collective-permute-start | bytes 614408 | tf_op jit(solution)/shard_map/ppermute | solution.py:291
  15.7 0.1 collective-permute-start.13
  15.8 0.0 collective-permute-done.5
  15.8 2.0 %collective-permute-start.12 = (f32[16,8,512]{2,1,0:T(8,128)S(1)}, f32[16,8,512]{2,1,0:T(8,128)S(1)}, u32[]{:S(2)}, u32[]{:S(2)}) collective-permute-start(f32[16,8,512]{2,1,0:T(8,128)S(1)} %get-tuple-element.35), channel_id=1, source_target_pairs={{0,7},{1,2},{2,1},{3,4},{4,3},{5,6},{6,5},{7,0},{8,15},{9,10},{10,... | collective-permute-start | bytes 786440 | tf_op jit(solution)/shard_map/ppermute | solution.py:291
  17.8 1.4 %collective-permute-done.4 = f32[8,16,512]{2,1,0:T(8,128)S(1)} collective-permute-done((f32[8,16,512]{2,1,0:T(8,128)S(1)}, f32[8,16,512]{2,1,0:T(8,128)S(1)}, u32[]{:S(2)}, u32[]{:S(2)}) %collective-permute-start.4) | collective-permute-done | bytes 262176 | tf_op jit(solution)/shard_map/ppermute | solution.py:291
  19.3 1.5 %coarse.1 = (f32[8,8,256]{2,1,0:T(8,128)S(1)}, f32[72,128]{1,0:T(8,128)S(1)}) custom-call(f32[25,8,256]{2,1,0:T(8,128)S(1)} %pad_maximum_fusion.2.mid_ref, f32[25,8,256]{2,1,0:T(8,128)S(1)} %get-tuple-element.45.low_ref, f32[25,8,256]{2,1,0:T(8,128)S(1)} %get-tuple-element.44.high_ref), custom_call_target="tpu_custom_call" | custom-call | flops 20000000000 | bytes 73800000 | tf_op jit(solution)/shard_map/coarse/pallas_call | solution.py:311
  20.8 0.1 collective-permute-start.9
  20.9 4.1 %collective-permute-start.8 = (f32[8,8,256]{2,1,0:T(8,128)S(1)}, f32[8,8,256]{2,1,0:T(8,128)S(1)}, u32[]{:S(2)}, u32[]{:S(2)}) collective-permute-start(f32[8,8,256]{2,1,0:T(8,128)S(1)} %get-tuple-element.24.c_ref), channel_id=1, source_target_pairs={{0,7},{1,2},{2,1},{3,4},{4,3},{5,6},{6,5},{7,0},{8,15},{9,10},{10,... | collective-permute-start | bytes 196616 | tf_op jit(solution)/shard_map/ppermute | solution.py:291
  25.1 0.1 collective-permute-start.7
  25.2 0.5 %collective-permute-start.6 = (f32[16,8,512]{2,1,0:T(8,128)S(1)}, f32[16,8,512]{2,1,0:T(8,128)S(1)}, u32[]{:S(2)}, u32[]{:S(2)}) collective-permute-start(f32[16,8,512]{2,1,0:T(8,128)S(1)} %get-tuple-element.39), channel_id=1, source_target_pairs={{0,7},{1,2},{2,1},{3,4},{4,3},{5,6},{6,5},{7,0},{8,15},{9,10},{10,... | collective-permute-start | bytes 786440 | tf_op jit(solution)/shard_map/ppermute | solution.py:291
  25.8 1.2 %collective-permute-done.8 = f32[8,8,256]{2,1,0:T(8,128)S(1)} collective-permute-done((f32[8,8,256]{2,1,0:T(8,128)S(1)}, f32[8,8,256]{2,1,0:T(8,128)S(1)}, u32[]{:S(2)}, u32[]{:S(2)}) %collective-permute-start.8) | collective-permute-done | bytes 65568 | tf_op jit(solution)/shard_map/ppermute | solution.py:291
  27.1 0.1 collective-permute-start.11
  27.2 4.2 %collective-permute-start.10 = (f32[5,24,256]{2,1,0:T(8,128)S(1)}, f32[5,24,256]{2,1,0:T(8,128)S(1)}, u32[]{:S(2)}, u32[]{:S(2)}) collective-permute-start(f32[5,24,256]{2,1,0:T(8,128)S(1)} %get-tuple-element.53), channel_id=1, source_target_pairs={{0,120},{8,16},{16,8},{24,32},{32,24},{40,48},{48,40},{56,64},{64,... | collective-permute-start | bytes 368648 | tf_op jit(solution)/shard_map/ppermute | solution.py:291
  31.3 2.3 %inner.1 = (f32[16,4,48,128]{3,2,1,0:T(8,128)S(1)}, f32[16,4,48,128]{3,2,1,0:T(8,128)S(1)}, f32[16,4,48,128]{3,2,1,0:T(8,128)S(1)}, f32[4,4,48,128]{3,2,1,0:T(8,128)S(1)}, f32[4,4,512]{2,1,0:T(4,128)S(1)}) custom-call(f32[16,16,512]{2,1,0:T(8,128)S(1)} %copy-done, f32[16,8,512]{2,1,0:T(8,128)S(1)} %get-tuple-element.33.side_low, ...), custom_call_target="tpu_custom_call" | custom-call | flops 20000000000 | bytes 73800000 | tf_op jit(solution)/shard_map/inner/pallas_call | solution.py:328
  33.7 1.9 %collective-permute-done.10 = f32[5,24,256]{2,1,0:T(8,128)S(1)} collective-permute-done((f32[5,24,256]{2,1,0:T(8,128)S(1)}, f32[5,24,256]{2,1,0:T(8,128)S(1)}, u32[]{:S(2)}, u32[]{:S(2)}) %collective-permute-start.10) | collective-permute-done | bytes 122912 | tf_op jit(solution)/shard_map/ppermute | solution.py:291
  35.7 5.9 %outer.1 = (f32[16,16,512]{2,1,0:T(8,128)}, f32[16,16,512]{2,1,0:T(8,128)}) custom-call(f32[16,16,512]{2,1,0:T(8,128)S(1)} %copy-done, f32[8,16,512]{2,1,0:T(8,128)S(1)} %get-tuple-element.22.side_left, f32[8,16,512]{2,1,0:T(8,128)S(1)} %get-tuple-element.23.side_right, f32[16,8,512]{2,1,0:T(8,128)S(1)} %get-tuple-element.37.corner_low, ...), custom_call_target="tpu_custom_call" | custom-call | flops 6000000000 | bytes 22140000 | tf_op jit(solution)/shard_map/outer/pallas_call | solution.py:334
  (27 shorter events, 0.4 us)
Async XLA Ops:
  2.0 13.7 %copy-start = (f32[16,16,512]{2,1,0:T(8,128)S(1)}, f32[16,16,512]{2,1,0:T(8,128)}, u32[]{:S(2)}) copy-start(f32[16,16,512]{2,1,0:T(8,128)} %side_ref.3) | copy-start | bytes 1572868
  2.0 7.5 %collective-permute-start.1 = (f32[9,8,256]{2,1,0:T(8,128)S(1)}, f32[9,8,256]{2,1,0:T(8,128)S(1)}, u32[]{:S(2)}, u32[]{:S(2)}) collective-permute-start(f32[9,8,256]{2,1,0:T(8,128)S(1)} %get-tuple-element.17), channel_id=1, source_target_pairs={{0,8},{8,0},{16,24},{24,16},{32,40},{40,32},{48,56},{56,48},{64,72... | collective-permute-start | bytes 221192 | tf_op jit(solution)/shard_map/ppermute | solution.py:292
  3.7 7.7 %collective-permute-start = (f32[9,8,256]{2,1,0:T(8,128)S(1)}, f32[9,8,256]{2,1,0:T(8,128)S(1)}, u32[]{:S(2)}, u32[]{:S(2)}) collective-permute-start(f32[9,8,256]{2,1,0:T(8,128)S(1)} %get-tuple-element.17), channel_id=1, source_target_pairs={{0,120},{8,16},{16,8},{24,32},{32,24},{40,48},{48,40},{56,64},{64,... | collective-permute-start | bytes 221192 | tf_op jit(solution)/shard_map/ppermute | solution.py:291
  8.3 7.6 %collective-permute-start.5 = (f32[8,16,512]{2,1,0:T(8,128)S(1)}, f32[8,16,512]{2,1,0:T(8,128)S(1)}, u32[]{:S(2)}, u32[]{:S(2)}) collective-permute-start(f32[8,16,512]{2,1,0:T(8,128)S(1)} %get-tuple-element.42), channel_id=1, source_target_pairs={{0,8},{8,0},{16,24},{24,16},{32,40},{40,32},{48,56},{56,48},{64,72... | collective-permute-start | bytes 786440 | tf_op jit(solution)/shard_map/ppermute | solution.py:292
  8.3 10.9 %collective-permute-start.4 = (f32[8,16,512]{2,1,0:T(8,128)S(1)}, f32[8,16,512]{2,1,0:T(8,128)S(1)}, u32[]{:S(2)}, u32[]{:S(2)}) collective-permute-start(f32[8,16,512]{2,1,0:T(8,128)S(1)} %get-tuple-element.43), channel_id=1, source_target_pairs={{0,120},{8,16},{16,8},{24,32},{32,24},{40,48},{48,40},{56,64},{64,... | collective-permute-start | bytes 786440 | tf_op jit(solution)/shard_map/ppermute | solution.py:291
  11.4 7.9 %collective-permute-start.3 = (f32[25,8,256]{2,1,0:T(8,128)S(1)}, f32[25,8,256]{2,1,0:T(8,128)S(1)}, u32[]{:S(2)}, u32[]{:S(2)}) collective-permute-start(f32[25,8,256]{2,1,0:T(8,128)S(1)} %pad_maximum_fusion.2.mid_ref), channel_id=1, source_target_pairs={{0,1},{1,0},{2,3},{3,2},{4,5},{5,4},{6,7},{7,6},{8,9},{9,8},{10,11... | collective-permute-start | bytes 614408 | tf_op jit(solution)/shard_map/ppermute | solution.py:292
  11.5 7.8 %collective-permute-start.2 = (f32[25,8,256]{2,1,0:T(8,128)S(1)}, f32[25,8,256]{2,1,0:T(8,128)S(1)}, u32[]{:S(2)}, u32[]{:S(2)}) collective-permute-start(f32[25,8,256]{2,1,0:T(8,128)S(1)} %pad_maximum_fusion.2.mid_ref), channel_id=1, source_target_pairs={{0,7},{1,2},{2,1},{3,4},{4,3},{5,6},{6,5},{7,0},{8,15},{9,10},{10,... | collective-permute-start | bytes 614408 | tf_op jit(solution)/shard_map/ppermute | solution.py:291
  15.7 9.5 %collective-permute-start.13 = (f32[16,8,512]{2,1,0:T(8,128)S(1)}, f32[16,8,512]{2,1,0:T(8,128)S(1)}, u32[]{:S(2)}, u32[]{:S(2)}) collective-permute-start(f32[16,8,512]{2,1,0:T(8,128)S(1)} %get-tuple-element.34), channel_id=1, source_target_pairs={{0,1},{1,0},{2,3},{3,2},{4,5},{5,4},{6,7},{7,6},{8,9},{9,8},{10,11... | collective-permute-start | bytes 786440 | tf_op jit(solution)/shard_map/ppermute | solution.py:292
  15.8 9.9 %collective-permute-start.12 = (f32[16,8,512]{2,1,0:T(8,128)S(1)}, f32[16,8,512]{2,1,0:T(8,128)S(1)}, u32[]{:S(2)}, u32[]{:S(2)}) collective-permute-start(f32[16,8,512]{2,1,0:T(8,128)S(1)} %get-tuple-element.35), channel_id=1, source_target_pairs={{0,7},{1,2},{2,1},{3,4},{4,3},{5,6},{6,5},{7,0},{8,15},{9,10},{10,... | collective-permute-start | bytes 786440 | tf_op jit(solution)/shard_map/ppermute | solution.py:291
  20.8 5.0 %collective-permute-start.9 = (f32[8,8,256]{2,1,0:T(8,128)S(1)}, f32[8,8,256]{2,1,0:T(8,128)S(1)}, u32[]{:S(2)}, u32[]{:S(2)}) collective-permute-start(f32[8,8,256]{2,1,0:T(8,128)S(1)} %get-tuple-element.24.c_ref), channel_id=1, source_target_pairs={{0,1},{1,0},{2,3},{3,2},{4,5},{5,4},{6,7},{7,6},{8,9},{9,8},{10,11... | collective-permute-start | bytes 196616 | tf_op jit(solution)/shard_map/ppermute | solution.py:292
  20.9 6.1 %collective-permute-start.8 = (f32[8,8,256]{2,1,0:T(8,128)S(1)}, f32[8,8,256]{2,1,0:T(8,128)S(1)}, u32[]{:S(2)}, u32[]{:S(2)}) collective-permute-start(f32[8,8,256]{2,1,0:T(8,128)S(1)} %get-tuple-element.24.c_ref), channel_id=1, source_target_pairs={{0,7},{1,2},{2,1},{3,4},{4,3},{5,6},{6,5},{7,0},{8,15},{9,10},{10,... | collective-permute-start | bytes 196616 | tf_op jit(solution)/shard_map/ppermute | solution.py:291
  25.1 10.5 %collective-permute-start.7 = (f32[16,8,512]{2,1,0:T(8,128)S(1)}, f32[16,8,512]{2,1,0:T(8,128)S(1)}, u32[]{:S(2)}, u32[]{:S(2)}) collective-permute-start(f32[16,8,512]{2,1,0:T(8,128)S(1)} %get-tuple-element.38), channel_id=1, source_target_pairs={{0,1},{1,0},{2,3},{3,2},{4,5},{5,4},{6,7},{7,6},{8,9},{9,8},{10,11... | collective-permute-start | bytes 786440 | tf_op jit(solution)/shard_map/ppermute | solution.py:292
  25.2 10.4 %collective-permute-start.6 = (f32[16,8,512]{2,1,0:T(8,128)S(1)}, f32[16,8,512]{2,1,0:T(8,128)S(1)}, u32[]{:S(2)}, u32[]{:S(2)}) collective-permute-start(f32[16,8,512]{2,1,0:T(8,128)S(1)} %get-tuple-element.39), channel_id=1, source_target_pairs={{0,7},{1,2},{2,1},{3,4},{4,3},{5,6},{6,5},{7,0},{8,15},{9,10},{10,... | collective-permute-start | bytes 786440 | tf_op jit(solution)/shard_map/ppermute | solution.py:291
  27.1 6.6 %collective-permute-start.11 = (f32[5,24,256]{2,1,0:T(8,128)S(1)}, f32[5,24,256]{2,1,0:T(8,128)S(1)}, u32[]{:S(2)}, u32[]{:S(2)}) collective-permute-start(f32[5,24,256]{2,1,0:T(8,128)S(1)} %get-tuple-element.52), channel_id=1, source_target_pairs={{0,8},{8,0},{16,24},{24,16},{32,40},{40,32},{48,56},{56,48},{64,72... | collective-permute-start | bytes 368648 | tf_op jit(solution)/shard_map/ppermute | solution.py:292
  27.2 8.5 %collective-permute-start.10 = (f32[5,24,256]{2,1,0:T(8,128)S(1)}, f32[5,24,256]{2,1,0:T(8,128)S(1)}, u32[]{:S(2)}, u32[]{:S(2)}) collective-permute-start(f32[5,24,256]{2,1,0:T(8,128)S(1)} %get-tuple-element.53), channel_id=1, source_target_pairs={{0,120},{8,16},{16,8},{24,32},{32,24},{40,48},{48,40},{56,64},{64,... | collective-permute-start | bytes 368648 | tf_op jit(solution)/shard_map/ppermute | solution.py:291

commit v7 on v5

--- a/solution.py
+++ b/solution.py
@@ -76,7 +76,7 @@
     return lax.axis_index("gx"), lax.axis_index("gy"), lax.axis_size("gx"), lax.axis_size("gy")
 
 
-def restrict_kernel(side_hbm, counts_hbm, out_ref, first_ref, last_ref, tmp, side_ref, counts_ref, arrived):
+def restrict_kernel(side_hbm, counts_hbm, out_ref, tmp, side_ref, counts_ref, arrived):
     copies = [
         pltpu.make_async_copy(counts_hbm, counts_ref, arrived.at[0]),
         pltpu.make_async_copy(side_hbm, side_ref, arrived.at[1]),
@@ -104,6 +104,9 @@
             out_ref[x, :, 128 * b : 128 * b + 128] = 0.5 * jnp.where(lane < 64, halves[2 * b], halves[2 * b + 1])
     out_ref[8] = jnp.zeros((8, 256), F32)
     out_ref[8, 0:4, 0:64] = counts_ref[...].reshape(4, 64).astype(F32)
+
+
+def slices_kernel(packed_ref, side_ref, first_ref, last_ref):
     first_ref[...] = side_ref[0:8]
     last_ref[...] = side_ref[8:16]
 
@@ -229,7 +232,7 @@
         return (odd if k % 2 else even), x + 10
 
     for k in range(1, 9):
-        for rows in (range(k - 9, k), range(16 - k, 25 - k)):
+        for rows in (range(k - 9, k), range(16 - k, 25 - k)) if k < 8 else (range(-1, 17),):
             sweep(
                 rows, fine_starts(k), 4,
                 lambda x: state(k - 1, x),
@@ -287,9 +290,9 @@
         second = lax.ppermute(to_low if same else jnp.where(even, to_high, to_low), axis, inner)
         return jnp.where(even, first, second), jnp.where(even, second, first)
 
-    packed, first, last = call(
+    (packed,) = call(
         restrict_kernel,
-        [(9, 8, 256), (8, 16, 512), (8, 16, 512)],
+        [(9, 8, 256)],
         [(4, 128, 128), (16, 16, 512), pltpu.VMEM((2, 2, 64), jnp.int32), pltpu.SemaphoreType.DMA((2,))],
         "restrict",
         1,
@@ -298,6 +301,7 @@
         pltpu.with_memory_space_constraint(right_side, pltpu.MemorySpace.HBM),
         pltpu.with_memory_space_constraint(point_counts, pltpu.MemorySpace.HBM),
     )
+    first, last = call(slices_kernel, [(8, 16, 512), (8, 16, 512)], [], "slices", 1)(packed, right_side)
     left, right = exchange("gx", packed, packed)
     packed = jnp.concatenate([left, packed, right], axis=0)
     side_left, side_right = exchange("gx", first, last)

time: 41.9 us -> 41.9 us (level)
    pallas_call x1 -> x2, Pallas kernels: 1.31 us -> 1.37 us  [the longest x1 1.33 us: shards(): call(restrict_kernel, [(9, 8, 256)], [(4, 128, 128), (16, 16, 512), pltpu...]
where the time goes in v7:
time: 41.9 us; the launch traced here: 41.8 us
  starting transfers between devices  23 us (55%)
  Pallas kernels  11.1 us (26%)
  waiting for transfers between devices  6.25 us (15%)
  between operations  1.04 us (2%)
    ppermute x7, starting transfers between devices, exchange(): lax.ppermute(to_low if same else jnp.where(even, to_low, to_high), axis,...  20.9 us
    ppermute x7, waiting for transfers between devices, exchange(): lax.ppermute(to_low if same else jnp.where(even, to_low, to_high), axis,...  6.11 us
    pallas_call x1, Pallas kernels, shards(): call(outer_kernel, [block, block], [field, field, (16, 4, 48, 128), block...  5.88 us
    pallas_call x1, Pallas kernels, shards(): call(inner_kernel, [field, field, field, (4, 4, 48, 128), (4, 4, 512)], [...  2.34 us
    ppermute x7, starting transfers between devices, exchange(): lax.ppermute(to_low if same else jnp.where(even, to_high, to_low), axis,...  2.17 us
    pallas_call x1, Pallas kernels, shards(): call(coarse_kernel, [(8, 8, 256), (72, 128)], [(26, 2, 40, 128)] * 3 + [(...  1.47 us
    pallas_call x1, Pallas kernels, shards(): call(restrict_kernel, [(9, 8, 256)], [(4, 128, 128), (16, 16, 512), pltpu...  1.33 us
  transfers between devices with their start and end apart: 14, of which 5 were waited for; matrix products, arithmetic and copies ran while one was open for 1% of the time, Pallas kernels for 9%

profile of v7, /device:TPU:0, one launch (start us, length us, event | category | flops | bytes accessed | tf_op | source)
XLA Modules:
  0.0 41.8 jit_solution(5154607617911149600)
XLA Ops:
  0.6 1.3 %restrict.1.packed_ref = f32[9,8,256]{2,1,0:T(8,128)S(1)} custom-call(f32[16,16,512]{2,1,0:T(8,128)} %side_ref.5, s32[2,2,64]{2,1,0:T(2,128)} %counts_hbm.1), custom_call_target="tpu_custom_call" | custom-call | flops 1000000000 | bytes 3690000 | tf_op jit(solution)/shard_map/restrict/pallas_call | solution.py:293
  2.0 1.7 %collective-permute-start.1 = (f32[9,8,256]{2,1,0:T(8,128)S(1)}, f32[9,8,256]{2,1,0:T(8,128)S(1)}, u32[]{:S(2)}, u32[]{:S(2)}) collective-permute-start(f32[9,8,256]{2,1,0:T(8,128)S(1)} %restrict.1.packed_ref), channel_id=1, source_target_pairs={{0,8},{8,0},{16,24},{24,16},{32,40},{40,32},{48,56},{56,48},{64,72... | collective-permute-start | bytes 221192 | tf_op jit(solution)/shard_map/ppermute | solution.py:290
  3.6 4.5 %collective-permute-start = (f32[9,8,256]{2,1,0:T(8,128)S(1)}, f32[9,8,256]{2,1,0:T(8,128)S(1)}, u32[]{:S(2)}, u32[]{:S(2)}) collective-permute-start(f32[9,8,256]{2,1,0:T(8,128)S(1)} %restrict.1.packed_ref), channel_id=1, source_target_pairs={{0,120},{8,16},{16,8},{24,32},{32,24},{40,48},{48,40},{56,64},{64,... | collective-permute-start | bytes 221192 | tf_op jit(solution)/shard_map/ppermute | solution.py:289
  8.3 0.1 collective-permute-start.5
  8.4 1.2 %collective-permute-start.4 = (f32[8,16,512]{2,1,0:T(8,128)S(1)}, f32[8,16,512]{2,1,0:T(8,128)S(1)}, u32[]{:S(2)}, u32[]{:S(2)}) collective-permute-start(f32[8,16,512]{2,1,0:T(8,128)S(1)} %get-tuple-element.41), channel_id=1, source_target_pairs={{0,120},{8,16},{16,8},{24,32},{32,24},{40,48},{48,40},{56,64},{64,... | collective-permute-start | bytes 786440 | tf_op jit(solution)/shard_map/ppermute | solution.py:289
  9.6 1.7 %collective-permute-done = f32[9,8,256]{2,1,0:T(8,128)S(1)} collective-permute-done((f32[9,8,256]{2,1,0:T(8,128)S(1)}, f32[9,8,256]{2,1,0:T(8,128)S(1)}, u32[]{:S(2)}, u32[]{:S(2)}) %collective-permute-start) | collective-permute-done | bytes 73760 | tf_op jit(solution)/shard_map/ppermute | solution.py:289
  11.3 0.1 collective-permute-start.3
  11.4 4.1 %collective-permute-start.2 = (f32[27,8,256]{2,1,0:T(8,128)S(1)}, f32[27,8,256]{2,1,0:T(8,128)S(1)}, u32[]{:S(2)}, u32[]{:S(2)}) collective-permute-start(f32[27,8,256]{2,1,0:T(8,128)S(1)} %pad_maximum_fusion.2.mid_ref), channel_id=1, source_target_pairs={{0,7},{1,2},{2,1},{3,4},{4,3},{5,6},{6,5},{7,0},{8,15},{9,10},{10,... | collective-permute-start | bytes 663560 | tf_op jit(solution)/shard_map/ppermute | solution.py:289
  15.6 0.1 collective-permute-start.13
  15.7 0.1 collective-permute-done.5
  15.8 2.0 %collective-permute-start.12 = (f32[16,8,512]{2,1,0:T(8,128)S(1)}, f32[16,8,512]{2,1,0:T(8,128)S(1)}, u32[]{:S(2)}, u32[]{:S(2)}) collective-permute-start(f32[16,8,512]{2,1,0:T(8,128)S(1)} %get-tuple-element.33), channel_id=1, source_target_pairs={{0,7},{1,2},{2,1},{3,4},{4,3},{5,6},{6,5},{7,0},{8,15},{9,10},{10,... | collective-permute-start | bytes 786440 | tf_op jit(solution)/shard_map/ppermute | solution.py:289
  17.8 1.4 %collective-permute-done.4 = f32[8,16,512]{2,1,0:T(8,128)S(1)} collective-permute-done((f32[8,16,512]{2,1,0:T(8,128)S(1)}, f32[8,16,512]{2,1,0:T(8,128)S(1)}, u32[]{:S(2)}, u32[]{:S(2)}) %collective-permute-start.4) | collective-permute-done | bytes 262176 | tf_op jit(solution)/shard_map/ppermute | solution.py:289
  19.3 0.0 collective-permute-done.3
  19.4 1.5 %coarse.1 = (f32[8,8,256]{2,1,0:T(8,128)S(1)}, f32[72,128]{1,0:T(8,128)S(1)}) custom-call(f32[27,8,256]{2,1,0:T(8,128)S(1)} %pad_maximum_fusion.2.mid_ref, f32[27,8,256]{2,1,0:T(8,128)S(1)} %get-tuple-element.43.low_ref, f32[27,8,256]{2,1,0:T(8,128)S(1)} %get-tuple-element.42.high_ref), custom_call_target="tpu_custom_call" | custom-call | flops 20000000000 | bytes 73800000 | tf_op jit(solution)/shard_map/coarse/pallas_call | solution.py:310
  20.8 0.1 collective-permute-start.9
  20.9 4.1 %collective-permute-start.8 = (f32[8,8,256]{2,1,0:T(8,128)S(1)}, f32[8,8,256]{2,1,0:T(8,128)S(1)}, u32[]{:S(2)}, u32[]{:S(2)}) collective-permute-start(f32[8,8,256]{2,1,0:T(8,128)S(1)} %get-tuple-element.22.c_ref), channel_id=1, source_target_pairs={{0,7},{1,2},{2,1},{3,4},{4,3},{5,6},{6,5},{7,0},{8,15},{9,10},{10,... | collective-permute-start | bytes 196616 | tf_op jit(solution)/shard_map/ppermute | solution.py:289
  25.2 0.1 collective-permute-start.7
  25.3 0.5 %collective-permute-start.6 = (f32[16,8,512]{2,1,0:T(8,128)S(1)}, f32[16,8,512]{2,1,0:T(8,128)S(1)}, u32[]{:S(2)}, u32[]{:S(2)}) collective-permute-start(f32[16,8,512]{2,1,0:T(8,128)S(1)} %get-tuple-element.37), channel_id=1, source_target_pairs={{0,7},{1,2},{2,1},{3,4},{4,3},{5,6},{6,5},{7,0},{8,15},{9,10},{10,... | collective-permute-start | bytes 786440 | tf_op jit(solution)/shard_map/ppermute | solution.py:289
  25.8 1.2 %collective-permute-done.8 = f32[8,8,256]{2,1,0:T(8,128)S(1)} collective-permute-done((f32[8,8,256]{2,1,0:T(8,128)S(1)}, f32[8,8,256]{2,1,0:T(8,128)S(1)}, u32[]{:S(2)}, u32[]{:S(2)}) %collective-permute-start.8) | collective-permute-done | bytes 65568 | tf_op jit(solution)/shard_map/ppermute | solution.py:289
  27.1 0.1 collective-permute-start.11
  27.2 4.4 %collective-permute-start.10 = (f32[5,24,256]{2,1,0:T(8,128)S(1)}, f32[5,24,256]{2,1,0:T(8,128)S(1)}, u32[]{:S(2)}, u32[]{:S(2)}) collective-permute-start(f32[5,24,256]{2,1,0:T(8,128)S(1)} %get-tuple-element.51), channel_id=1, source_target_pairs={{0,120},{8,16},{16,8},{24,32},{32,24},{40,48},{48,40},{56,64},{64,... | collective-permute-start | bytes 368648 | tf_op jit(solution)/shard_map/ppermute | solution.py:289
  31.5 2.3 %inner.1 = (f32[16,4,48,128]{3,2,1,0:T(8,128)S(1)}, f32[16,4,48,128]{3,2,1,0:T(8,128)S(1)}, f32[16,4,48,128]{3,2,1,0:T(8,128)S(1)}, f32[4,4,48,128]{3,2,1,0:T(8,128)S(1)}, f32[4,4,512]{2,1,0:T(4,128)S(1)}) custom-call(f32[16,16,512]{2,1,0:T(8,128)S(1)} %copy-done, f32[16,8,512]{2,1,0:T(8,128)S(1)} %get-tuple-element.31.side_low, ...), custom_call_target="tpu_custom_call" | custom-call | flops 20000000000 | bytes 73800000 | tf_op jit(solution)/shard_map/inner/pallas_call | solution.py:327
  33.9 1.8 %collective-permute-done.10 = f32[5,24,256]{2,1,0:T(8,128)S(1)} collective-permute-done((f32[5,24,256]{2,1,0:T(8,128)S(1)}, f32[5,24,256]{2,1,0:T(8,128)S(1)}, u32[]{:S(2)}, u32[]{:S(2)}) %collective-permute-start.10) | collective-permute-done | bytes 122912 | tf_op jit(solution)/shard_map/ppermute | solution.py:289
  35.7 5.9 %outer.1 = (f32[16,16,512]{2,1,0:T(8,128)}, f32[16,16,512]{2,1,0:T(8,128)}) custom-call(f32[16,16,512]{2,1,0:T(8,128)S(1)} %copy-done, f32[8,16,512]{2,1,0:T(8,128)S(1)} %get-tuple-element.20.side_left, f32[8,16,512]{2,1,0:T(8,128)S(1)} %get-tuple-element.21.side_right, f32[16,8,512]{2,1,0:T(8,128)S(1)} %get-tuple-element.35.corner_low, ...), custom_call_target="tpu_custom_call" | custom-call | flops 6000000000 | bytes 22140000 | tf_op jit(solution)/shard_map/outer/pallas_call | solution.py:333
  (25 shorter events, 0.5 us)
Async XLA Ops:
  0.6 7.6 %copy-start = (f32[16,16,512]{2,1,0:T(8,128)S(1)}, f32[16,16,512]{2,1,0:T(8,128)}, u32[]{:S(2)}) copy-start(f32[16,16,512]{2,1,0:T(8,128)} %side_ref.5) | copy-start | bytes 1572868
  2.0 7.6 %collective-permute-start.1 = (f32[9,8,256]{2,1,0:T(8,128)S(1)}, f32[9,8,256]{2,1,0:T(8,128)S(1)}, u32[]{:S(2)}, u32[]{:S(2)}) collective-permute-start(f32[9,8,256]{2,1,0:T(8,128)S(1)} %restrict.1.packed_ref), channel_id=1, source_target_pairs={{0,8},{8,0},{16,24},{24,16},{32,40},{40,32},{48,56},{56,48},{64,72... | collective-permute-start | bytes 221192 | tf_op jit(solution)/shard_map/ppermute | solution.py:290
  3.6 7.7 %collective-permute-start = (f32[9,8,256]{2,1,0:T(8,128)S(1)}, f32[9,8,256]{2,1,0:T(8,128)S(1)}, u32[]{:S(2)}, u32[]{:S(2)}) collective-permute-start(f32[9,8,256]{2,1,0:T(8,128)S(1)} %restrict.1.packed_ref), channel_id=1, source_target_pairs={{0,120},{8,16},{16,8},{24,32},{32,24},{40,48},{48,40},{56,64},{64,... | collective-permute-start | bytes 221192 | tf_op jit(solution)/shard_map/ppermute | solution.py:289
  8.3 7.6 %collective-permute-start.5 = (f32[8,16,512]{2,1,0:T(8,128)S(1)}, f32[8,16,512]{2,1,0:T(8,128)S(1)}, u32[]{:S(2)}, u32[]{:S(2)}) collective-permute-start(f32[8,16,512]{2,1,0:T(8,128)S(1)} %get-tuple-element.40), channel_id=1, source_target_pairs={{0,8},{8,0},{16,24},{24,16},{32,40},{40,32},{48,56},{56,48},{64,72... | collective-permute-start | bytes 786440 | tf_op jit(solution)/shard_map/ppermute | solution.py:290
  8.4 10.9 %collective-permute-start.4 = (f32[8,16,512]{2,1,0:T(8,128)S(1)}, f32[8,16,512]{2,1,0:T(8,128)S(1)}, u32[]{:S(2)}, u32[]{:S(2)}) collective-permute-start(f32[8,16,512]{2,1,0:T(8,128)S(1)} %get-tuple-element.41), channel_id=1, source_target_pairs={{0,120},{8,16},{16,8},{24,32},{32,24},{40,48},{48,40},{56,64},{64,... | collective-permute-start | bytes 786440 | tf_op jit(solution)/shard_map/ppermute | solution.py:289
  11.3 8.0 %collective-permute-start.3 = (f32[27,8,256]{2,1,0:T(8,128)S(1)}, f32[27,8,256]{2,1,0:T(8,128)S(1)}, u32[]{:S(2)}, u32[]{:S(2)}) collective-permute-start(f32[27,8,256]{2,1,0:T(8,128)S(1)} %pad_maximum_fusion.2.mid_ref), channel_id=1, source_target_pairs={{0,1},{1,0},{2,3},{3,2},{4,5},{5,4},{6,7},{7,6},{8,9},{9,8},{10,11... | collective-permute-start | bytes 663560 | tf_op jit(solution)/shard_map/ppermute | solution.py:290
  11.4 7.9 %collective-permute-start.2 = (f32[27,8,256]{2,1,0:T(8,128)S(1)}, f32[27,8,256]{2,1,0:T(8,128)S(1)}, u32[]{:S(2)}, u32[]{:S(2)}) collective-permute-start(f32[27,8,256]{2,1,0:T(8,128)S(1)} %pad_maximum_fusion.2.mid_ref), channel_id=1, source_target_pairs={{0,7},{1,2},{2,1},{3,4},{4,3},{5,6},{6,5},{7,0},{8,15},{9,10},{10,... | collective-permute-start | bytes 663560 | tf_op jit(solution)/shard_map/ppermute | solution.py:289
  15.6 9.6 %collective-permute-start.13 = (f32[16,8,512]{2,1,0:T(8,128)S(1)}, f32[16,8,512]{2,1,0:T(8,128)S(1)}, u32[]{:S(2)}, u32[]{:S(2)}) collective-permute-start(f32[16,8,512]{2,1,0:T(8,128)S(1)} %get-tuple-element.32), channel_id=1, source_target_pairs={{0,1},{1,0},{2,3},{3,2},{4,5},{5,4},{6,7},{7,6},{8,9},{9,8},{10,11... | collective-permute-start | bytes 786440 | tf_op jit(solution)/shard_map/ppermute | solution.py:290
  15.8 9.9 %collective-permute-start.12 = (f32[16,8,512]{2,1,0:T(8,128)S(1)}, f32[16,8,512]{2,1,0:T(8,128)S(1)}, u32[]{:S(2)}, u32[]{:S(2)}) collective-permute-start(f32[16,8,512]{2,1,0:T(8,128)S(1)} %get-tuple-element.33), channel_id=1, source_target_pairs={{0,7},{1,2},{2,1},{3,4},{4,3},{5,6},{6,5},{7,0},{8,15},{9,10},{10,... | collective-permute-start | bytes 786440 | tf_op jit(solution)/shard_map/ppermute | solution.py:289
  20.8 5.0 %collective-permute-start.9 = (f32[8,8,256]{2,1,0:T(8,128)S(1)}, f32[8,8,256]{2,1,0:T(8,128)S(1)}, u32[]{:S(2)}, u32[]{:S(2)}) collective-permute-start(f32[8,8,256]{2,1,0:T(8,128)S(1)} %get-tuple-element.22.c_ref), channel_id=1, source_target_pairs={{0,1},{1,0},{2,3},{3,2},{4,5},{5,4},{6,7},{7,6},{8,9},{9,8},{10,11... | collective-permute-start | bytes 196616 | tf_op jit(solution)/shard_map/ppermute | solution.py:290
  20.9 6.1 %collective-permute-start.8 = (f32[8,8,256]{2,1,0:T(8,128)S(1)}, f32[8,8,256]{2,1,0:T(8,128)S(1)}, u32[]{:S(2)}, u32[]{:S(2)}) collective-permute-start(f32[8,8,256]{2,1,0:T(8,128)S(1)} %get-tuple-element.22.c_ref), channel_id=1, source_target_pairs={{0,7},{1,2},{2,1},{3,4},{4,3},{5,6},{6,5},{7,0},{8,15},{9,10},{10,... | collective-permute-start | bytes 196616 | tf_op jit(solution)/shard_map/ppermute | solution.py:289
  25.2 10.5 %collective-permute-start.7 = (f32[16,8,512]{2,1,0:T(8,128)S(1)}, f32[16,8,512]{2,1,0:T(8,128)S(1)}, u32[]{:S(2)}, u32[]{:S(2)}) collective-permute-start(f32[16,8,512]{2,1,0:T(8,128)S(1)} %get-tuple-element.36), channel_id=1, source_target_pairs={{0,1},{1,0},{2,3},{3,2},{4,5},{5,4},{6,7},{7,6},{8,9},{9,8},{10,11... | collective-permute-start | bytes 786440 | tf_op jit(solution)/shard_map/ppermute | solution.py:290
  25.3 10.4 %collective-permute-start.6 = (f32[16,8,512]{2,1,0:T(8,128)S(1)}, f32[16,8,512]{2,1,0:T(8,128)S(1)}, u32[]{:S(2)}, u32[]{:S(2)}) collective-permute-start(f32[16,8,512]{2,1,0:T(8,128)S(1)} %get-tuple-element.37), channel_id=1, source_target_pairs={{0,7},{1,2},{2,1},{3,4},{4,3},{5,6},{6,5},{7,0},{8,15},{9,10},{10,... | collective-permute-start | bytes 786440 | tf_op jit(solution)/shard_map/ppermute | solution.py:289
  27.1 6.8 %collective-permute-start.11 = (f32[5,24,256]{2,1,0:T(8,128)S(1)}, f32[5,24,256]{2,1,0:T(8,128)S(1)}, u32[]{:S(2)}, u32[]{:S(2)}) collective-permute-start(f32[5,24,256]{2,1,0:T(8,128)S(1)} %get-tuple-element.50), channel_id=1, source_target_pairs={{0,8},{8,0},{16,24},{24,16},{32,40},{40,32},{48,56},{56,48},{64,72... | collective-permute-start | bytes 368648 | tf_op jit(solution)/shard_map/ppermute | solution.py:290
  27.2 8.5 %collective-permute-start.10 = (f32[5,24,256]{2,1,0:T(8,128)S(1)}, f32[5,24,256]{2,1,0:T(8,128)S(1)}, u32[]{:S(2)}, u32[]{:S(2)}) collective-permute-start(f32[5,24,256]{2,1,0:T(8,128)S(1)} %get-tuple-element.51), channel_id=1, source_target_pairs={{0,120},{8,16},{16,8},{24,32},{32,24},{40,48},{48,40},{56,64},{64,... | collective-permute-start | bytes 368648 | tf_op jit(solution)/shard_map/ppermute | solution.py:289
